TPU v7x, 128 devices: a whole 4x4x4 slice. The times are simulated.
128 devices in a mesh: dp: 4 (over z_lo, core), expert: 32 (over x, y, z_hi).
Axes of the slice: x: 4, y: 4, z: 4 (z_hi: 2, z_lo: 2; z = z_hi * 2 + z_lo), core: 2. Of those that a mesh axis runs over, the one named last changes fastest.
Arguments:
- tokens: bfloat16 [256, 256, 1280], P(('dp', 'expert')), may hold values from -8 to 8
- router: bfloat16 [128, 1280], P(('dp', 'expert')), may hold values from -28.36068 to 28.36068
- w_in: bfloat16 [128, 1280, 2560], P('expert', None, 'dp'), may hold values from -0.15625 to 0.15625
- w_out: bfloat16 [128, 2560, 1280], P('expert', 'dp'), may hold values from -0.125 to 0.125
- d_out: bfloat16 [256, 256, 1280], P(('dp', 'expert')), may hold values from -6 to 6
Outputs:
- d_tokens: bfloat16 [256, 256, 1280], P(('dp', 'expert'))
- d_router: float32 [128, 1280], P(('dp', 'expert'))
- d_w_out: bfloat16 [128, 2560, 1280], P('expert', 'dp')
All inputs are finite; a program needn't handle non-finite values.
Results may differ from a plain program's by a relative error of at most 0.019.
Values may be sent and summed in bfloat16 or wider, within the bound.
No kernel may reach another device: no remote copies, remote signals or barrier semaphores. Data moves between devices by JAX's collectives and lax.ppermute only.
A program may use at most 128 MiB of HBM per device.

v0:
```python
import math

import jax
import jax.numpy as jnp
from jax import lax
from jax.sharding import PartitionSpec as P


def send_in(payload):
    return (
        lax.all_to_all(payload[0], "expert", split_axis=1, concat_axis=0, tiled=True),
        lax.all_to_all(payload[1], "expert", split_axis=1, concat_axis=0, tiled=True),
    )


def spread_in(payload):
    return (
        lax.all_gather(payload[0], "dp", axis=0, tiled=True),
        lax.all_gather(payload[1], "dp", axis=0, tiled=True),
    )


def share_out(payload):
    groups = lax.axis_size("dp")
    first_blocks = payload[0].reshape(
        (groups, payload[0].shape[0] // groups) + payload[0].shape[1:]
    )
    second_blocks = payload[1].reshape(
        (groups, payload[1].shape[0] // groups) + payload[1].shape[1:]
    )
    received = (
        lax.all_to_all(first_blocks, "dp", split_axis=0, concat_axis=0, tiled=True),
        lax.all_to_all(second_blocks, "dp", split_axis=0, concat_axis=0, tiled=True),
    )
    return (
        jnp.sum(received[0].astype(jnp.float32), axis=0).astype(jnp.bfloat16),
        jnp.sum(received[1].astype(jnp.float32), axis=0).astype(jnp.bfloat16),
    )


def send_out(payload):
    return (
        lax.all_to_all(payload[0], "expert", split_axis=0, concat_axis=1, tiled=True),
        lax.all_to_all(payload[1], "expert", split_axis=0, concat_axis=1, tiled=True),
    )


def body(tokens, router, w_in, w_out, d_out):
    score_scale = 1.0 / math.sqrt(tokens.shape[2])
    router_full = lax.all_gather(router, ("dp", "expert"), axis=0, tiled=True)
    logits = (
        jnp.einsum("imd,nd->imn", tokens, router_full, preferred_element_type=jnp.float32)
        * score_scale
    )
    combine = jax.nn.softmax(logits, axis=2)
    dispatch = jax.nn.softmax(logits, axis=1)
    dispatch_rounded = dispatch.astype(jnp.bfloat16)
    combine_rounded = combine.astype(jnp.bfloat16)
    slot_part = jnp.einsum(
        "imn,imd->ind", dispatch_rounded, tokens, preferred_element_type=jnp.float32
    ).astype(jnp.bfloat16)
    grad_part = jnp.einsum(
        "imn,imd->ind", combine_rounded, d_out, preferred_element_type=jnp.float32
    ).astype(jnp.bfloat16)
    slots, slot_grads = spread_in(send_in((slot_part, grad_part)))
    before = jnp.einsum("red,edf->ref", slots, w_in, preferred_element_type=jnp.float32)
    active, backward = jax.vjp(lambda values: jax.nn.gelu(values, approximate=False), before)
    active_rounded = active.astype(jnp.bfloat16)
    out_part = jnp.einsum(
        "ref,efd->red", active_rounded, w_out, preferred_element_type=jnp.float32
    ).astype(jnp.bfloat16)
    grad_active = jnp.einsum("red,efd->ref", slot_grads, w_out, preferred_element_type=jnp.float32)
    grad_before = backward(grad_active)[0].astype(jnp.bfloat16)
    d_w_out = jnp.einsum(
        "ref,red->efd", active_rounded, slot_grads, preferred_element_type=jnp.float32
    ).astype(jnp.bfloat16)
    back_part = jnp.einsum(
        "ref,edf->red", grad_before, w_in, preferred_element_type=jnp.float32
    ).astype(jnp.bfloat16)
    expert_out, slot_back = send_out(share_out((out_part, back_part)))
    grad_combine = jnp.einsum("imd,ind->imn", d_out, expert_out, preferred_element_type=jnp.float32)
    combine_part = combine * (grad_combine - jnp.sum(combine * grad_combine, axis=2, keepdims=True))
    grad_dispatch = jnp.einsum(
        "imd,ind->imn", tokens, slot_back, preferred_element_type=jnp.float32
    )
    dispatch_part = dispatch * (
        grad_dispatch - jnp.sum(dispatch * grad_dispatch, axis=1, keepdims=True)
    )
    logit_grad = ((combine_part + dispatch_part) * score_scale).astype(jnp.bfloat16)
    d_tokens = (
        jnp.einsum("imn,ind->imd", dispatch_rounded, slot_back, preferred_element_type=jnp.float32)
        + jnp.einsum("imn,nd->imd", logit_grad, router_full, preferred_element_type=jnp.float32)
    ).astype(jnp.bfloat16)
    router_term = jnp.einsum("imn,imd->nd", logit_grad, tokens, preferred_element_type=jnp.float32)
    d_router = lax.psum_scatter(router_term, ("dp", "expert"), scatter_dimension=0, tiled=True)
    return (d_tokens, d_router, d_w_out)


def solution(mesh):
    placed = (
        P(("dp", "expert"), None, None),
        P(("dp", "expert"), None),
        P("expert", None, "dp"),
        P("expert", "dp", None),
        P(("dp", "expert"), None, None),
    )
    return jax.shard_map(
        body,
        mesh=mesh,
        in_specs=placed,
        out_specs=(
            P(("dp", "expert"), None, None),
            P(("dp", "expert"), None),
            P("expert", "dp", None),
        ),
        check_vma=False,
    )
```

profile of v0, /device:TPU:1, one launch (start us, length us, event | category | flops | bytes accessed | tf_op | source)
XLA Modules:
  0.0 727.7 jit_solution(4274580037380280411)
XLA Ops:
  7.2 332.8 %all-gather = bf16[128,1,1280]{2,1,0:T(2,128)(2,1)S(1)} all-gather(bf16[1,1,1280]{2,1,0:T(2,128)(2,1)} %bitcast.155), channel_id=1, replica_groups=mesh['dp'=4,'expert'=32] {'dp','expert'}, dimensions={0}, use_global_device_ids=true | all-gather | bytes 330240 | tf_op jit(solution)/shard_map/all_gather | solution.py:50
  340.0 0.5 convolution_multiply_fusion
  340.5 0.8 fusion.61
  341.3 0.4 convolution_convert_fusion.4
  341.8 0.7 copy.63
  342.5 17.6 %all_to_all.82 = bf16[2,128,1280]{2,0,1:T(2,128)(2,1)S(1)} all-to-all(bf16[2,128,1280]{2,0,1:T(2,128)(2,1)S(1)} %copy.63), channel_id=1, replica_groups=mesh['dp'=4,'expert'=32] {'expert'}, dimensions={1} | all-to-all | bytes 1310720 | tf_op jit(solution)/shard_map/all_to_all | solution.py:11
  360.0 0.5 copy.100
  360.5 1.1 all_to_all.61
  361.6 0.0 all-gather.6.cloned.1.call-start
  361.6 0.9 fusion.62
  362.5 2.5 convolution_convert_fusion.3
  365.0 0.7 copy.66
  365.7 16.4 %all_to_all.83 = bf16[2,128,1280]{2,0,1:T(2,128)(2,1)S(1)} all-to-all(bf16[2,128,1280]{2,0,1:T(2,128)(2,1)S(1)} %copy.66), channel_id=1, replica_groups=mesh['dp'=4,'expert'=32] {'expert'}, dimensions={1} | all-to-all | bytes 1310720 | tf_op jit(solution)/shard_map/all_to_all | solution.py:12
  382.1 0.5 copy.99
  382.6 1.1 all_to_all.65
  383.7 15.0 %all-gather.4.cloned.1.call-done = bf16[256,4,1280]{2,0,1:T(8,128)(2,1)} async-done(((bf16[64,4,1280]{2,0,1:T(8,128)(2,1)}), bf16[256,4,1280]{2,0,1:T(8,128)(2,1)}) %all-gather.4.cloned.1.call-update) | async-done | bytes 2621456 | tf_op jit(solution)/shard_map/all_gather | solution.py:18
  398.7 11.1 %fusion.14 = (bf16[256,4,640]{2,0,1:T(8,128)(2,1)S(1)}, f32[4,256,640]{2,1,0:T(8,128)}) fusion(bf16[256,4,1280]{2,0,1:T(8,128)(2,1)} %all-gather.4.cloned.1.call-done, bf16[4,1280,640]{2,1,0:T(8,128)(2,1)} %param.7), kind=kOutput, calls=%fused_computation.26 | convolution fusion | flops 1720320000 | bytes 13107200 | tf_op jit(solution)/shard_map/red,edf->ref/dot_general | solution.py:66
  409.7 25.0 %all-gather.6.cloned.1.call-done = bf16[256,4,1280]{2,0,1:T(8,128)(2,1)} async-done(((bf16[64,4,1280]{2,0,1:T(8,128)(2,1)}), bf16[256,4,1280]{2,0,1:T(8,128)(2,1)}) %all-gather.6.cloned.1.call-update) | async-done | bytes 2621456 | tf_op jit(solution)/shard_map/all_gather | solution.py:19
  434.8 14.1 %convolution_convert_fusion.2 = bf16[4,256,1280]{2,1,0:T(8,128)(2,1)} fusion(bf16[4,1280,640]{2,1,0:T(8,128)(2,1)} %param.7, f32[4,256,640]{2,1,0:T(8,128)} %get-tuple-element.8, bf16[256,4,1280]{2,0,1:T(8,128)(2,1)} %all-gather.6.cloned.1.call-done, bf16[4,640,1280]{2,1,0:T(8,128)(2,1)} %param.8), kind=kOutput, calls=%fused_computation.7 | convolution fusion | flops 3403939840 | bytes 20971520 | tf_op jit(solution)/shard_map/ref,edf->red/dot_general | solution.py:77
  448.9 3.5 copy.68
  452.4 4.5 all-to-all-start.2
  456.9 5.1 convolution_convert_fusion.1
  462.0 1.8 copy.72
  463.8 23.6 %all-to-all-done.2 = bf16[4,64,4,1280]{3,1,2,0:T(8,128)(2,1)} async-done(((bf16[4,64,4,1280]{3,1,2,0:T(8,128)(2,1)}), bf16[4,64,4,1280]{3,1,2,0:T(8,128)(2,1)}, u32[]{:S(2)}, u32[]{:S(2)}) %all-to-all-start.2) | async-done | bytes 2621472 | tf_op jit(solution)/shard_map/all_to_all | solution.py:33
  487.4 5.4 all-to-all-start.4
  492.8 3.2 reduce_sum.62
  496.0 2.4 copy.70
  498.4 25.0 %all-to-all-done.4 = bf16[4,64,4,1280]{3,1,2,0:T(8,128)(2,1)} async-done(((bf16[4,64,4,1280]{3,1,2,0:T(8,128)(2,1)}), bf16[4,64,4,1280]{3,1,2,0:T(8,128)(2,1)}, u32[]{:S(2)}, u32[]{:S(2)}) %all-to-all-start.4) | async-done | bytes 2621472 | tf_op jit(solution)/shard_map/all_to_all | solution.py:32
  523.4 9.2 %all-to-all-start.3 = ((bf16[64,4,1280]{2,1,0:T(4,128)(2,1)}), bf16[64,4,1280]{2,1,0:T(4,128)(2,1)}, u32[]{:S(2)}, u32[]{:S(2)}) async-start(bf16[64,4,1280]{2,1,0:T(4,128)(2,1)} %copy.70), calls=%async_computation.3 | async-start | bytes 1310720 | tf_op jit(solution)/shard_map/all_to_all | solution.py:44
  532.6 3.2 reduce_sum.63
  535.8 2.4 copy.74
  538.2 8.0 %all-to-all-done.3 = bf16[64,4,1280]{2,1,0:T(4,128)(2,1)} async-done(((bf16[64,4,1280]{2,1,0:T(4,128)(2,1)}), bf16[64,4,1280]{2,1,0:T(4,128)(2,1)}, u32[]{:S(2)}, u32[]{:S(2)}) %all-to-all-start.3) | async-done | bytes 655392 | tf_op jit(solution)/shard_map/all_to_all | solution.py:44
  546.2 4.6 all-to-all-start.5
  550.8 0.0 all-reduce.3.cloned.1.call-start
  550.9 6.4 convolution_convert_fusion
  557.3 1.3 copy.71
  558.6 0.2 all_to_all.70
  558.8 1.2 convolution_bitcast_fusion.1
  560.0 2.0 fusion.50
  562.0 1.4 all-to-all-done.5
  563.4 1.3 copy.75
  564.7 0.2 all_to_all.75
  564.8 1.8 convolution_bitcast_fusion.2
  566.7 1.2 fusion.33
  567.8 4.5 convolution_bitcast_fusion
  572.3 5.2 fusion.4
  577.6 142.2 %all-reduce.3.cloned.1.call-done = f32[128,1280]{1,0:T(8,128)} async-done(((f32[128,1280]{1,0:T(8,128)}), f32[128,1280]{1,0:T(8,128)}) %all-reduce.3.cloned.1.call-update) | async-done | bytes 655376
  719.8 1.4 constant_dynamic-slice_fusion
  (8 shorter events, 0.1 us)
Async XLA Ops:
  7.2 332.9 %copy-start = (bf16[2,256,1280]{2,1,0:T(8,128)(2,1)S(1)}, bf16[2,256,1280]{2,1,0:T(8,128)(2,1)}, u32[]{:S(2)}) copy-start(bf16[2,256,1280]{2,1,0:T(8,128)(2,1)} %param.5) | copy-start | bytes 3932164
  7.2 391.5 %all-gather.4.cloned.1.call-start = ((), (), s32[]{:S(2)}) async-start(), calls=%async_computation.6 | async-start | bytes 3276800 | tf_op jit(solution)/shard_map/all_gather | solution.py:18
  361.6 73.2 %all-gather.6.cloned.1.call-start = ((), (), s32[]{:S(2)}) async-start(), calls=%async_computation.7 | async-start | bytes 3276800 | tf_op jit(solution)/shard_map/all_gather | solution.py:19
  452.4 35.1 %all-to-all-start.2 = ((bf16[4,64,4,1280]{3,1,2,0:T(8,128)(2,1)}), bf16[4,64,4,1280]{3,1,2,0:T(8,128)(2,1)}, u32[]{:S(2)}, u32[]{:S(2)}) async-start(bf16[4,64,4,1280]{3,1,2,0:T(8,128)(2,1)} %copy.68), calls=%async_computation.2 | async-start | bytes 5242880 | tf_op jit(solution)/shard_map/all_to_all | solution.py:33
  487.4 35.9 %all-to-all-start.4 = ((bf16[4,64,4,1280]{3,1,2,0:T(8,128)(2,1)}), bf16[4,64,4,1280]{3,1,2,0:T(8,128)(2,1)}, u32[]{:S(2)}, u32[]{:S(2)}) async-start(bf16[4,64,4,1280]{3,1,2,0:T(8,128)(2,1)} %copy.72), calls=%async_computation.4 | async-start | bytes 5242880 | tf_op jit(solution)/shard_map/all_to_all | solution.py:32
  523.4 22.8 %all-to-all-start.3 = ((bf16[64,4,1280]{2,1,0:T(4,128)(2,1)}), bf16[64,4,1280]{2,1,0:T(4,128)(2,1)}, u32[]{:S(2)}, u32[]{:S(2)}) async-start(bf16[64,4,1280]{2,1,0:T(4,128)(2,1)} %copy.70), calls=%async_computation.3 | async-start | bytes 1310720 | tf_op jit(solution)/shard_map/all_to_all | solution.py:44
  546.2 17.2 %all-to-all-start.5 = ((bf16[64,4,1280]{2,1,0:T(4,128)(2,1)}), bf16[64,4,1280]{2,1,0:T(4,128)(2,1)}, u32[]{:S(2)}, u32[]{:S(2)}) async-start(bf16[64,4,1280]{2,1,0:T(4,128)(2,1)} %copy.74), calls=%async_computation.5 | async-start | bytes 1310720 | tf_op jit(solution)/shard_map/all_to_all | solution.py:43
  550.8 169.0 %all-reduce.3.cloned.1.call-start = ((), (), s32[]{:S(2)}) async-start(), calls=%async_computation.8 | async-start | bytes 1310720
  562.0 4.7 copy-start.1
Sparse Core Ops, SparseCore 0:
  361.7 36.9 all-gather.3
  400.3 34.3 all-gather.5
  572.4 147.3 all-reduce.2
where the time goes:
time: 729 us; the launch traced here: 728 us
  blocking collectives  367 us (50%)
  waiting for transfers between devices  240 us (33%)
  matrix products  54.9 us (8%)
  starting transfers between devices  23.9 us (3%)
  local copies, waits for them, and re-layouts  18.9 us (3%)
  between operations  13.9 us (2%)
  other arithmetic  9.17 us (1%)
    all_gather x1, blocking collectives, body(): router_full = lax.all_gather(router, ('dp', 'expert'), axis=0, tiled=True)  333 us
    unnamed x4, waiting for transfers between devices  142 us
    all_gather x1, waiting for transfers between devices, spread_in(): lax.all_gather(payload[1], 'dp', axis=0, tiled=True)  25 us
    all_to_all x1, waiting for transfers between devices, share_out(): lax.all_to_all(first_blocks, 'dp', split_axis=0, concat_axis=0, tiled=True)  25 us
    all_to_all x1, waiting for transfers between devices, share_out(): lax.all_to_all(second_blocks, 'dp', split_axis=0, concat_axis=0, tiled=True)  23.6 us
    all_to_all x1, blocking collectives, send_in(): lax.all_to_all(payload[0], 'expert', split_axis=1, concat_axis=0, tiled=T...  17.6 us
    all_to_all x1, blocking collectives, send_in(): lax.all_to_all(payload[1], 'expert', split_axis=1, concat_axis=0, tiled=T...  16.4 us
    all_gather x1, waiting for transfers between devices, spread_in(): lax.all_gather(payload[0], 'dp', axis=0, tiled=True)  15 us
  transfers between devices with their start and end apart: 7, of which 7 were waited for; matrix products, arithmetic and copies ran while one was open for 7% of the time, Pallas kernels for 0%

commit v1 on v0

--- a/solution.py
+++ b/solution.py
@@ -4,6 +4,19 @@
 import jax.numpy as jnp
 from jax import lax
 from jax.sharding import PartitionSpec as P
+
+
+def gather_router(router):
+    rows = lax.axis_size(("dp", "expert")) * router.shape[0]
+    spread = jnp.broadcast_to(router, (rows, router.shape[1]))
+    return lax.all_to_all(spread, ("dp", "expert"), split_axis=0, concat_axis=0, tiled=True)
+
+
+def reduce_router(router_term):
+    received = lax.all_to_all(
+        router_term.astype(jnp.bfloat16), ("dp", "expert"), split_axis=0, concat_axis=0, tiled=True
+    )
+    return jnp.sum(received.astype(jnp.float32), axis=0, keepdims=True)
 
 
 def send_in(payload):
@@ -47,7 +60,7 @@
 
 def body(tokens, router, w_in, w_out, d_out):
     score_scale = 1.0 / math.sqrt(tokens.shape[2])
-    router_full = lax.all_gather(router, ("dp", "expert"), axis=0, tiled=True)
+    router_full = gather_router(router)
     logits = (
         jnp.einsum("imd,nd->imn", tokens, router_full, preferred_element_type=jnp.float32)
         * score_scale
@@ -92,7 +105,7 @@
         + jnp.einsum("imn,nd->imd", logit_grad, router_full, preferred_element_type=jnp.float32)
     ).astype(jnp.bfloat16)
     router_term = jnp.einsum("imn,imd->nd", logit_grad, tokens, preferred_element_type=jnp.float32)
-    d_router = lax.psum_scatter(router_term, ("dp", "expert"), scatter_dimension=0, tiled=True)
+    d_router = reduce_router(router_term)
     return (d_tokens, d_router, d_w_out)
 
 

time: 729 us -> 300 us (0.41)
  blocking collectives: 367 us -> 57.8 us
  waiting for transfers between devices: 240 us -> 105 us
  starting transfers between devices: 23.9 us -> 33.6 us
    all_gather x1 -> x0, blocking collectives: 333 us -> none  [body(): router_full = lax.all_gather(router, ('dp', 'expert'), axis=0, tiled=True)]
    unnamed x4 -> x2, waiting for transfers between devices: 142 us -> 0.03 us
    all_to_all x0 -> x1, blocking collectives: none -> 23.2 us  [gather_router(): lax.all_to_all(spread, ('dp', 'expert'), split_axis=0, concat_axis=0, til...]
    all_to_all x0 -> x1, starting transfers between devices: none -> 9.79 us  [reduce_router(): lax.all_to_all(router_term.astype(jnp.bfloat16), ('dp', 'expert'), split_...]
  transfers between devices with their start and end apart: 7 -> 7, of which waited for: 7 -> 7; matrix products, arithmetic and copies ran while one was open for 7% -> 17% of each run, Pallas kernels for 0% -> 0%
where the time goes in v1:
time: 300 us; the launch traced here: 299 us
  waiting for transfers between devices  105 us (35%)
  blocking collectives  57.8 us (19%)
  matrix products  54.1 us (18%)
  starting transfers between devices  33.6 us (11%)
  local copies, waits for them, and re-layouts  20.4 us (7%)
  other arithmetic  14.2 us (5%)
  between operations  14.2 us (5%)
    all_gather x1, waiting for transfers between devices, spread_in(): lax.all_gather(payload[1], 'dp', axis=0, tiled=True)  25.5 us
    all_to_all x1, waiting for transfers between devices, share_out(): lax.all_to_all(first_blocks, 'dp', split_axis=0, concat_axis=0, tiled=True)  25 us
    all_to_all x1, waiting for transfers between devices, share_out(): lax.all_to_all(second_blocks, 'dp', split_axis=0, concat_axis=0, tiled=True)  23.6 us
    all_to_all x1, blocking collectives, gather_router(): lax.all_to_all(spread, ('dp', 'expert'), split_axis=0, concat_axis=0, til...  23.2 us
    all_to_all x1, blocking collectives, send_in(): lax.all_to_all(payload[0], 'expert', split_axis=1, concat_axis=0, tiled=T...  17.6 us
    all_to_all x1, blocking collectives, send_in(): lax.all_to_all(payload[1], 'expert', split_axis=1, concat_axis=0, tiled=T...  17 us
    all_gather x1, waiting for transfers between devices, spread_in(): lax.all_gather(payload[0], 'dp', axis=0, tiled=True)  15 us
    dot_general x1, matrix products, body(): jnp.einsum('ref,edf->red', grad_before, w_in, preferred_element_type=jnp....  14.1 us
  transfers between devices with their start and end apart: 7, of which 7 were waited for; matrix products, arithmetic and copies ran while one was open for 17% of the time, Pallas kernels for 0%

profile of v1, /device:TPU:1, one launch (start us, length us, event | category | flops | bytes accessed | tf_op | source)
XLA Modules:
  0.0 299.3 jit_solution(10485731861317465057)
XLA Ops:
  7.2 0.8 reduce.3
  8.4 0.5 broadcast.71
  8.9 2.6 reduce.4
  11.6 23.2 %all_to_all.100 = bf16[128,2,640]{2,1,0:T(2,128)(2,1)S(1)} all-to-all(bf16[128,2,640]{2,1,0:T(2,128)(2,1)S(1)} %reshape.33), channel_id=1, replica_groups=mesh['dp'=4,'expert'=32] {'dp','expert'}, dimensions={0} | all-to-all | bytes 655360 | tf_op jit(solution)/shard_map/all_to_all | solution.py:12
  35.0 0.5 convolution_multiply_fusion
  35.5 0.8 fusion.63
  36.8 0.7 copy.65
  37.5 17.6 %all_to_all.101 = bf16[2,128,1280]{2,0,1:T(2,128)(2,1)S(1)} all-to-all(bf16[2,128,1280]{2,0,1:T(2,128)(2,1)S(1)} %copy.65), channel_id=1, replica_groups=mesh['dp'=4,'expert'=32] {'expert'}, dimensions={1} | all-to-all | bytes 1310720 | tf_op jit(solution)/shard_map/all_to_all | solution.py:24
  55.5 1.1 all_to_all.75
  56.6 0.9 fusion.64
  57.5 2.5 convolution_convert_fusion.3
  60.0 0.7 copy.68
  60.7 17.0 %all_to_all.102 = bf16[2,128,1280]{2,0,1:T(2,128)(2,1)S(1)} all-to-all(bf16[2,128,1280]{2,0,1:T(2,128)(2,1)S(1)} %copy.68), channel_id=1, replica_groups=mesh['dp'=4,'expert'=32] {'expert'}, dimensions={1} | all-to-all | bytes 1310720 | tf_op jit(solution)/shard_map/all_to_all | solution.py:25
  78.2 1.1 all_to_all.79
  79.3 15.0 %all-gather.3.cloned.1.call-done = bf16[256,4,1280]{2,0,1:T(8,128)(2,1)} async-done(((bf16[64,4,1280]{2,0,1:T(8,128)(2,1)}), bf16[256,4,1280]{2,0,1:T(8,128)(2,1)}) %all-gather.3.cloned.1.call-update) | async-done | bytes 2621456 | tf_op jit(solution)/shard_map/all_gather | solution.py:31
  94.3 11.1 %fusion.14 = (bf16[256,4,640]{2,0,1:T(8,128)(2,1)S(1)}, f32[4,256,640]{2,1,0:T(8,128)}) fusion(bf16[256,4,1280]{2,0,1:T(8,128)(2,1)} %all-gather.3.cloned.1.call-done, bf16[4,1280,640]{2,1,0:T(8,128)(2,1)} %param.7), kind=kOutput, calls=%fused_computation.26 | convolution fusion | flops 1720320000 | bytes 13107200 | tf_op jit(solution)/shard_map/red,edf->ref/dot_general | solution.py:79
  105.4 25.5 %all-gather.5.cloned.1.call-done = bf16[256,4,1280]{2,0,1:T(8,128)(2,1)} async-done(((bf16[64,4,1280]{2,0,1:T(8,128)(2,1)}), bf16[256,4,1280]{2,0,1:T(8,128)(2,1)}) %all-gather.5.cloned.1.call-update) | async-done | bytes 2621456 | tf_op jit(solution)/shard_map/all_gather | solution.py:32
  130.9 14.1 %convolution_convert_fusion.2 = bf16[4,256,1280]{2,1,0:T(8,128)(2,1)} fusion(bf16[4,1280,640]{2,1,0:T(8,128)(2,1)} %param.7, f32[4,256,640]{2,1,0:T(8,128)} %get-tuple-element.8, bf16[256,4,1280]{2,0,1:T(8,128)(2,1)} %all-gather.5.cloned.1.call-done, bf16[4,640,1280]{2,1,0:T(8,128)(2,1)} %param.8), kind=kOutput, calls=%fused_computation.7 | convolution fusion | flops 3403939840 | bytes 20971520 | tf_op jit(solution)/shard_map/ref,edf->red/dot_general | solution.py:90
  145.0 3.5 %copy.70 = bf16[4,64,4,1280]{3,1,2,0:T(8,128)(2,1)} copy(bf16[4,64,4,1280]{3,1,0,2:T(8,128)(2,1)} %bitcast.155) | data formatting | bytes 5242880 | tf_op jit(solution)/shard_map/reshape | solution.py:41
  148.5 4.5 %all-to-all-start.3 = ((bf16[4,64,4,1280]{3,1,2,0:T(8,128)(2,1)}), bf16[4,64,4,1280]{3,1,2,0:T(8,128)(2,1)}, u32[]{:S(2)}, u32[]{:S(2)}) async-start(bf16[4,64,4,1280]{3,1,2,0:T(8,128)(2,1)} %copy.70), calls=%async_computation.3 | async-start | bytes 5242880 | tf_op jit(solution)/shard_map/all_to_all | solution.py:46
  153.1 5.1 %convolution_convert_fusion.1 = bf16[4,256,1280]{2,1,0:T(8,128)(2,1)S(1)} fusion(bf16[256,4,640]{2,0,1:T(8,128)(2,1)S(1)} %get-tuple-element.7, bf16[4,640,1280]{2,1,0:T(8,128)(2,1)} %param.8), kind=kOutput, calls=%fused_computation.6 | convolution fusion | flops 1679032320 | bytes 10485760 | tf_op jit(solution)/shard_map/ref,efd->red/dot_general | solution.py:82
  158.1 1.8 copy.74
  160.0 23.6 %all-to-all-done.3 = bf16[4,64,4,1280]{3,1,2,0:T(8,128)(2,1)} async-done(((bf16[4,64,4,1280]{3,1,2,0:T(8,128)(2,1)}), bf16[4,64,4,1280]{3,1,2,0:T(8,128)(2,1)}, u32[]{:S(2)}, u32[]{:S(2)}) %all-to-all-start.3) | async-done | bytes 2621472 | tf_op jit(solution)/shard_map/all_to_all | solution.py:46
  183.6 5.4 %all-to-all-start.5 = ((bf16[4,64,4,1280]{3,1,2,0:T(8,128)(2,1)}), bf16[4,64,4,1280]{3,1,2,0:T(8,128)(2,1)}, u32[]{:S(2)}, u32[]{:S(2)}) async-start(bf16[4,64,4,1280]{3,1,2,0:T(8,128)(2,1)} %copy.74), calls=%async_computation.5 | async-start | bytes 5242880 | tf_op jit(solution)/shard_map/all_to_all | solution.py:45
  189.0 3.2 %reduce_sum.71 = bf16[64,4,1280]{2,0,1:T(8,128)(2,1)} reduce(bf16[4,64,4,1280]{3,1,2,0:T(8,128)(2,1)} %all-to-all-done.3, bf16[]{:T(256)} %constant.33.clone.1), dimensions={0}, to_apply=%region_4.0 | reduce | flops 983040 | bytes 3276802 | tf_op jit(solution)/shard_map/reduce_sum | solution.py:50
  192.1 2.4 copy.72
  194.5 25.0 %all-to-all-done.5 = bf16[4,64,4,1280]{3,1,2,0:T(8,128)(2,1)} async-done(((bf16[4,64,4,1280]{3,1,2,0:T(8,128)(2,1)}), bf16[4,64,4,1280]{3,1,2,0:T(8,128)(2,1)}, u32[]{:S(2)}, u32[]{:S(2)}) %all-to-all-start.5) | async-done | bytes 2621472 | tf_op jit(solution)/shard_map/all_to_all | solution.py:45
  219.5 9.2 %all-to-all-start.4 = ((bf16[64,4,1280]{2,1,0:T(4,128)(2,1)}), bf16[64,4,1280]{2,1,0:T(4,128)(2,1)}, u32[]{:S(2)}, u32[]{:S(2)}) async-start(bf16[64,4,1280]{2,1,0:T(4,128)(2,1)} %copy.72), calls=%async_computation.4 | async-start | bytes 1310720 | tf_op jit(solution)/shard_map/all_to_all | solution.py:57
  228.7 3.2 %reduce_sum.72 = bf16[64,4,1280]{2,0,1:T(8,128)(2,1)} reduce(bf16[4,64,4,1280]{3,1,2,0:T(8,128)(2,1)} %all-to-all-done.5, bf16[]{:T(256)} %constant.33.clone.1), dimensions={0}, to_apply=%region_5.0 | reduce | flops 983040 | bytes 3276802 | tf_op jit(solution)/shard_map/reduce_sum | solution.py:49
  231.9 2.4 copy.76
  234.3 8.0 %all-to-all-done.4 = bf16[64,4,1280]{2,1,0:T(4,128)(2,1)} async-done(((bf16[64,4,1280]{2,1,0:T(4,128)(2,1)}), bf16[64,4,1280]{2,1,0:T(4,128)(2,1)}, u32[]{:S(2)}, u32[]{:S(2)}) %all-to-all-start.4) | async-done | bytes 655392 | tf_op jit(solution)/shard_map/all_to_all | solution.py:57
  242.3 4.6 %all-to-all-start.6 = ((bf16[64,4,1280]{2,1,0:T(4,128)(2,1)}), bf16[64,4,1280]{2,1,0:T(4,128)(2,1)}, u32[]{:S(2)}, u32[]{:S(2)}) async-start(bf16[64,4,1280]{2,1,0:T(4,128)(2,1)} %copy.76), calls=%async_computation.6 | async-start | bytes 1310720 | tf_op jit(solution)/shard_map/all_to_all | solution.py:56
  246.9 6.4 %convolution_convert_fusion = bf16[4,640,1280]{2,1,0:T(8,128)(2,1)} fusion(bf16[256,4,640]{2,0,1:T(8,128)(2,1)S(1)} %get-tuple-element.7, bf16[256,4,1280]{2,0,1:T(8,128)(2,1)} %all-gather.5.cloned.1.call-done), kind=kOutput, calls=%fused_computation.4 | convolution fusion | flops 1680998400 | bytes 10485760 | tf_op jit(solution)/shard_map/ref,red->efd/dot_general | solution.py:87
  253.4 1.3 copy.73
  254.9 1.2 convolution_bitcast_fusion.1
  256.1 2.0 fusion.52
  258.1 1.4 all-to-all-done.6
  259.5 1.3 copy.77
  261.0 1.8 convolution_bitcast_fusion.2
  262.8 1.3 fusion.35
  264.1 3.7 %fusion.28 = bf16[128,1,1280]{2,0,1:T(8,128)(2,1)S(1)} fusion(bf16[2,256,1280]{2,1,0:T(8,128)(2,1)S(1)} %copy-done, f32[2,256,128]{2,1,0:T(8,128)S(1)} %fusion.35, f32[2,256,128]{2,1,0:T(8,128)S(1)} %convolution_bitcast_fusion.2, f32[2,256,128]{2,1,0:T(8,128)} %get-tuple-element.6, f32[2,256]{1,0:T(2,128)S(1)} %get-tuple-element.5), kind=kOutput, calls=%fused_computation.44 | convolution fusion | flops 168460928 | bytes 2426880 | tf_op jit(solution)/shard_map/imn,imd->nd/dot_general | solution.py:107
  267.8 0.8 reduce.5
  268.7 0.8 reshape.35
  269.4 9.8 %all-to-all-start.7 = ((bf16[128,2,640]{2,1,0:T(2,128)(2,1)}), bf16[128,2,640]{2,1,0:T(2,128)(2,1)S(1)}, u32[]{:S(2)}, u32[]{:S(2)}) async-start(bf16[128,2,640]{2,1,0:T(2,128)(2,1)} %reshape.35), calls=%async_computation.7 | async-start | bytes 655360 | tf_op jit(solution)/shard_map/all_to_all | solution.py:16
  279.2 5.2 %fusion.4 = bf16[2,256,1280]{2,1,0:T(8,128)(2,1)} fusion(f32[2,256,1280]{2,1,0:T(8,128)} %fusion.52, f32[2,256,128]{2,1,0:T(8,128)S(1)} %fusion.35, f32[2,256,128]{2,1,0:T(8,128)S(1)} %convolution_bitcast_fusion.2, bf16[128,1,1280]{2,1,0:T(2,128)(2,1)S(1)} %reshape.34, f32[2,256,128]{2,1,0:T(8,128)} %get-tuple-element.6, f32[2,256]{1,0:T(2,128)S(1)} %get-tuple-element.5), kind=kOutput, calls=%fused_computation.9 | convolution fusion | flops 169607808 | bytes 5048320 | tf_op jit(solution)/shard_map/imn,nd->imd/dot_general | solution.py:105
  284.5 6.6 %all-to-all-done.7 = bf16[128,2,640]{2,1,0:T(2,128)(2,1)S(1)} async-done(((bf16[128,2,640]{2,1,0:T(2,128)(2,1)}), bf16[128,2,640]{2,1,0:T(2,128)(2,1)S(1)}, u32[]{:S(2)}, u32[]{:S(2)}) %all-to-all-start.7) | async-done | bytes 327712 | tf_op jit(solution)/shard_map/all_to_all | solution.py:16
  291.3 0.6 convert_reduce_fusion
  291.9 0.6 broadcast_in_dim.5
  (15 shorter events, 2.7 us)
Async XLA Ops:
  7.2 27.9 %copy-start = (bf16[2,256,1280]{2,1,0:T(8,128)(2,1)S(1)}, bf16[2,256,1280]{2,1,0:T(8,128)(2,1)}, u32[]{:S(2)}) copy-start(bf16[2,256,1280]{2,1,0:T(8,128)(2,1)} %param.5) | copy-start | bytes 3932164
  7.2 87.2 %all-gather.3.cloned.1.call-start = ((), (), s32[]{:S(2)}) async-start(), calls=%async_computation.8 | async-start | bytes 3276800 | tf_op jit(solution)/shard_map/all_gather | solution.py:31
  56.6 74.3 %all-gather.5.cloned.1.call-start = ((), (), s32[]{:S(2)}) async-start(), calls=%async_computation.9 | async-start | bytes 3276800 | tf_op jit(solution)/shard_map/all_gather | solution.py:32
  148.5 35.1 %all-to-all-start.3 = ((bf16[4,64,4,1280]{3,1,2,0:T(8,128)(2,1)}), bf16[4,64,4,1280]{3,1,2,0:T(8,128)(2,1)}, u32[]{:S(2)}, u32[]{:S(2)}) async-start(bf16[4,64,4,1280]{3,1,2,0:T(8,128)(2,1)} %copy.70), calls=%async_computation.3 | async-start | bytes 5242880 | tf_op jit(solution)/shard_map/all_to_all | solution.py:46
  183.6 35.9 %all-to-all-start.5 = ((bf16[4,64,4,1280]{3,1,2,0:T(8,128)(2,1)}), bf16[4,64,4,1280]{3,1,2,0:T(8,128)(2,1)}, u32[]{:S(2)}, u32[]{:S(2)}) async-start(bf16[4,64,4,1280]{3,1,2,0:T(8,128)(2,1)} %copy.74), calls=%async_computation.5 | async-start | bytes 5242880 | tf_op jit(solution)/shard_map/all_to_all | solution.py:45
  219.5 22.8 %all-to-all-start.4 = ((bf16[64,4,1280]{2,1,0:T(4,128)(2,1)}), bf16[64,4,1280]{2,1,0:T(4,128)(2,1)}, u32[]{:S(2)}, u32[]{:S(2)}) async-start(bf16[64,4,1280]{2,1,0:T(4,128)(2,1)} %copy.72), calls=%async_computation.4 | async-start | bytes 1310720 | tf_op jit(solution)/shard_map/all_to_all | solution.py:57
  242.3 17.2 %all-to-all-start.6 = ((bf16[64,4,1280]{2,1,0:T(4,128)(2,1)}), bf16[64,4,1280]{2,1,0:T(4,128)(2,1)}, u32[]{:S(2)}, u32[]{:S(2)}) async-start(bf16[64,4,1280]{2,1,0:T(4,128)(2,1)} %copy.76), calls=%async_computation.6 | async-start | bytes 1310720 | tf_op jit(solution)/shard_map/all_to_all | solution.py:56
  269.4 21.6 %all-to-all-start.7 = ((bf16[128,2,640]{2,1,0:T(2,128)(2,1)}), bf16[128,2,640]{2,1,0:T(2,128)(2,1)S(1)}, u32[]{:S(2)}, u32[]{:S(2)}) async-start(bf16[128,2,640]{2,1,0:T(2,128)(2,1)} %reshape.35), calls=%async_computation.7 | async-start | bytes 655360 | tf_op jit(solution)/shard_map/all_to_all | solution.py:16
Sparse Core Ops, SparseCore 0:
  56.7 37.5 all-gather.2
  96.0 34.8 all-gather.4

commit v2 on v1

v2 whole, which is shorter than its diff:
```python
import math

import jax
import jax.numpy as jnp
from jax import lax
from jax.sharding import PartitionSpec as P

ALL = ("dp", "expert")
CHIP = [(index, index ^ 2) for index in range(4)]
CORE = [(index, index ^ 1) for index in range(4)]


def gather_router(router):
    rows = lax.axis_size(ALL) * router.shape[0]
    spread = jnp.broadcast_to(router, (rows, router.shape[1]))
    return lax.all_to_all(spread, ALL, split_axis=0, concat_axis=0, tiled=True)


def reduce_router(router_term):
    received = lax.all_to_all(
        router_term.astype(jnp.bfloat16), ALL, split_axis=0, concat_axis=0, tiled=True
    )
    return jnp.sum(received.astype(jnp.float32), axis=0, keepdims=True)


def send_in(part):
    groups = lax.axis_size("expert")
    images, slots, width = part.shape
    blocks = part.transpose(1, 0, 2).reshape(groups, slots // groups * images, width)
    blocks = lax.all_to_all(blocks, "expert", split_axis=0, concat_axis=0, tiled=True)
    blocks = blocks.reshape(groups, slots // groups, images, width)
    return blocks.transpose(1, 0, 2, 3).reshape(slots // groups, groups * images, width)


def send_out(rows, images):
    groups = lax.axis_size("expert")
    experts, count, width = rows.shape
    blocks = rows.reshape(experts, groups, images, width).transpose(1, 0, 2, 3)
    blocks = blocks.reshape(groups, experts * images, width)
    blocks = lax.all_to_all(blocks, "expert", split_axis=0, concat_axis=0, tiled=True)
    blocks = blocks.reshape(groups * experts, images, width)
    return blocks.transpose(1, 0, 2)


def spread(rows):
    other = lax.ppermute(rows, "dp", CHIP)
    near = lax.ppermute(rows, "dp", CORE)
    far = lax.ppermute(other, "dp", CORE)
    return jnp.concatenate([rows, other, near, far], axis=1)


def collect(kept, sent):
    count = kept.shape[1] // 2
    near = lax.ppermute(sent, "dp", CORE)
    total = kept + near.astype(jnp.float32)
    other = lax.ppermute(total[:, count:].astype(jnp.bfloat16), "dp", CHIP)
    return (total[:, :count] + other.astype(jnp.float32)).astype(jnp.bfloat16)


def dot(spec, left, right):
    return jnp.einsum(spec, left, right, preferred_element_type=jnp.float32)


def body(tokens, router, w_in, w_out, d_out):
    images = tokens.shape[0]
    score_scale = 1.0 / math.sqrt(tokens.shape[2])
    router_full = gather_router(router)
    logits = dot("imd,nd->imn", tokens, router_full) * score_scale
    combine = jax.nn.softmax(logits, axis=2)
    dispatch = jax.nn.softmax(logits, axis=1)
    dispatch_rounded = dispatch.astype(jnp.bfloat16)
    combine_rounded = combine.astype(jnp.bfloat16)
    slot_part = dot("imn,imd->ind", dispatch_rounded, tokens).astype(jnp.bfloat16)
    grad_part = dot("imn,imd->ind", combine_rounded, d_out).astype(jnp.bfloat16)
    slots = spread(send_in(slot_part))
    slot_grads = spread(send_in(grad_part))
    half = slots.shape[1] // 2

    before = dot("erd,edf->erf", slots, w_in)
    below = 0.5 * (1.0 + lax.erf(before * math.sqrt(0.5)))
    slope = below + before * (jnp.exp(-0.5 * before * before) * (1.0 / math.sqrt(2.0 * math.pi)))
    active = (before * below).astype(jnp.bfloat16)
    out_sent = dot("erf,efd->erd", active[:, half:], w_out).astype(jnp.bfloat16)
    out_kept = dot("erf,efd->erd", active[:, :half], w_out)
    expert_out = send_out(collect(out_kept, out_sent), images)

    grad_before = (dot("erd,efd->erf", slot_grads, w_out) * slope).astype(jnp.bfloat16)
    back_sent = dot("erf,edf->erd", grad_before[:, half:], w_in).astype(jnp.bfloat16)
    back_kept = dot("erf,edf->erd", grad_before[:, :half], w_in)
    slot_back = send_out(collect(back_kept, back_sent), images)
    d_w_out = dot("erf,erd->efd", active, slot_grads).astype(jnp.bfloat16)

    grad_combine = dot("imd,ind->imn", d_out, expert_out)
    combine_part = combine * (grad_combine - jnp.sum(combine * grad_combine, axis=2, keepdims=True))
    grad_dispatch = dot("imd,ind->imn", tokens, slot_back)
    dispatch_part = dispatch * (
        grad_dispatch - jnp.sum(dispatch * grad_dispatch, axis=1, keepdims=True)
    )
    logit_grad = ((combine_part + dispatch_part) * score_scale).astype(jnp.bfloat16)
    router_term = dot("imn,imd->nd", logit_grad, tokens)
    d_router = reduce_router(router_term)
    d_tokens = (
        dot("imn,ind->imd", dispatch_rounded, slot_back) + dot("imn,nd->imd", logit_grad, router_full)
    ).astype(jnp.bfloat16)
    return (d_tokens, d_router, d_w_out)


def solution(mesh):
    placed = (
        P(ALL, None, None),
        P(ALL, None),
        P("expert", None, "dp"),
        P("expert", "dp", None),
        P(ALL, None, None),
    )
    return jax.shard_map(
        body,
        mesh=mesh,
        in_specs=placed,
        out_specs=(P(ALL, None, None), P(ALL, None), P("expert", "dp", None)),
        check_vma=False,
    )
```

time: 300 us -> 202 us (0.67)
  waiting for transfers between devices: 105 us -> 66.9 us
  blocking collectives: 57.8 us -> 23.2 us
  matrix products: 54.1 us -> 38.2 us
  between operations: 14.2 us -> 1.12 us
  starting transfers between devices: 33.6 us -> 41.5 us
  other arithmetic: 14.2 us -> 8.38 us
    all_gather x2 -> x0, waiting for transfers between devices: 40.5 us -> none  [the longest x1 25.5 us: spread_in(): lax.all_gather(payload[1], 'dp', axis=0, tiled=True)]
    all_to_all x3 -> x1, blocking collectives: 57.8 us -> 23.2 us  [gather_router(): return lax.all_to_all(spread, ALL, split_axis=0, concat_axis=0, tiled=True)]
    ppermute x0 -> x10, waiting for transfers between devices: none -> 32 us  [the longest x2 17.3 us: spread(): other = lax.ppermute(rows, 'dp', CHIP)]
    all_to_all x5, waiting for transfers between devices: 64.5 us -> 34.9 us  [the longest x2 22.4 us: send_in(): lax.all_to_all(blocks, 'expert', split_axis=0, concat_axis=0, tiled=True)]
    dot_general x12 -> x15, matrix products: 54.1 us -> 38.2 us  [dot(): return jnp.einsum(spec, left, right, preferred_element_type=jnp.float32)]
    ppermute x0 -> x10, starting transfers between devices: none -> 9.62 us  [the longest x2 3.85 us: spread(): far = lax.ppermute(other, 'dp', CORE)]
    reshape x2 -> x12, local copies, waits for them, and re-layouts: 5.3 us -> 11.8 us  [the longest x4 4.47 us: send_out(): blocks = rows.reshape(experts, groups, images, width).transpose(1, 0, 2, 3)]
    reduce_sum x2 -> x0, other arithmetic: 6.33 us -> none  [the longest x1 3.17 us: share_out(): jnp.sum(received[0].astype(jnp.float32), axis=0).astype(jnp.bfloat16)]
  transfers between devices with their start and end apart: 7 -> 15, of which waited for: 7 -> 11; matrix products, arithmetic and copies ran while one was open for 17% -> 18% of each run, Pallas kernels for 0% -> 0%
where the time goes in v2:
time: 202 us; the launch traced here: 201 us
  waiting for transfers between devices  66.9 us (33%)
  starting transfers between devices  41.5 us (21%)
  matrix products  38.2 us (19%)
  blocking collectives  23.2 us (11%)
  local copies, waits for them, and re-layouts  21.3 us (11%)
  other arithmetic  8.38 us (4%)
    dot_general x15, matrix products, dot(): return jnp.einsum(spec, left, right, preferred_element_type=jnp.float32)  38.2 us
    all_to_all x1, blocking collectives, gather_router(): return lax.all_to_all(spread, ALL, split_axis=0, concat_axis=0, tiled=True)  23.2 us
    all_to_all x2, waiting for transfers between devices, send_in(): lax.all_to_all(blocks, 'expert', split_axis=0, concat_axis=0, tiled=True)  22.4 us
    ppermute x2, waiting for transfers between devices, spread(): other = lax.ppermute(rows, 'dp', CHIP)  17.3 us
    ppermute x2, waiting for transfers between devices, collect(): other = lax.ppermute(total[:, count:].astype(jnp.bfloat16), 'dp', CHIP)  13.1 us
    all_to_all x2, starting transfers between devices, send_out(): lax.all_to_all(blocks, 'expert', split_axis=0, concat_axis=0, tiled=True)  13 us
    all_to_all x1, starting transfers between devices, reduce_router(): lax.all_to_all(router_term.astype(jnp.bfloat16), ALL, split_axis=0, conca...  10.8 us
    all_to_all x2, starting transfers between devices, send_in(): lax.all_to_all(blocks, 'expert', split_axis=0, concat_axis=0, tiled=True)  8.13 us
  transfers between devices with their start and end apart: 15, of which 11 were waited for; matrix products, arithmetic and copies ran while one was open for 18% of the time, Pallas kernels for 0%

profile of v2, /device:TPU:1, one launch (start us, length us, event | category | flops | bytes accessed | tf_op | source)
XLA Modules:
  0.0 200.6 jit_solution(1882111109564871415)
XLA Ops:
  0.6 0.8 reduce.1
  2.3 2.6 %reduce.2 = bf16[128,1280]{1,0:T(8,128)(2,1)S(1)} reduce(bf16[128,1,1280]{2,1,0:T(2,128)(2,1)S(1)} %broadcast_in_dim.4, bf16[]{:T(256)} %broadcast.24), dimensions={1}, to_apply=%broadcast_in_dim.4.reduce_sub_computation | reduce | bytes 655362 | tf_op jit(solution)/shard_map/broadcast_in_dim | solution.py:15
  5.0 23.2 %all_to_all.38 = bf16[128,2,640]{2,1,0:T(2,128)(2,1)S(1)} all-to-all(bf16[128,2,640]{2,1,0:T(2,128)(2,1)S(1)} %reshape.73), channel_id=1, replica_groups=mesh['dp'=4,'expert'=32] {'dp','expert'}, dimensions={0} | all-to-all | bytes 655360 | tf_op jit(solution)/shard_map/all_to_all | solution.py:16
  29.0 0.9 fusion.73
  29.8 2.5 %fusion.19 = bf16[128,2,1280]{2,0,1:T(8,128)(2,1)S(1)} fusion(bf16[2,256,1280]{2,1,0:T(8,128)(2,1)} %param.9, f32[2,256]{1,0:T(2,128)S(1)} %get-tuple-element.5, f32[2,256,128]{2,1,0:T(8,128)S(1)} %convolution_multiply_fusion), kind=kOutput, calls=%fused_computation.30 | convolution fusion | flops 168297088 | bytes 2230272 | tf_op jit(solution)/shard_map/imn,imd->ind/dot_general | solution.py:61
  33.1 1.1 reshape.57
  34.1 4.1 %all-to-all-start.1 = ((bf16[32,8,1280]{2,1,0:T(8,128)(2,1)}), bf16[32,8,1280]{2,1,0:T(8,128)(2,1)S(1)}, u32[]{:S(2)}, u32[]{:S(2)}) async-start(bf16[32,8,1280]{2,1,0:T(8,128)(2,1)} %reshape.57), calls=%async_computation.1 | async-start | bytes 1310720 | tf_op jit(solution)/shard_map/all_to_all | solution.py:30
  40.1 1.1 reshape.60
  41.2 10.7 %all-to-all-done.1 = bf16[32,8,1280]{2,1,0:T(8,128)(2,1)S(1)} async-done(((bf16[32,8,1280]{2,1,0:T(8,128)(2,1)}), bf16[32,8,1280]{2,1,0:T(8,128)(2,1)S(1)}, u32[]{:S(2)}, u32[]{:S(2)}) %all-to-all-start.1) | async-done | bytes 655392 | tf_op jit(solution)/shard_map/all_to_all | solution.py:30
  51.9 4.1 %all-to-all-start.2 = ((bf16[32,8,1280]{2,1,0:T(8,128)(2,1)}), bf16[32,8,1280]{2,1,0:T(8,128)(2,1)S(1)}, u32[]{:S(2)}, u32[]{:S(2)}) async-start(bf16[32,8,1280]{2,1,0:T(8,128)(2,1)} %reshape.60), calls=%async_computation.2 | async-start | bytes 1310720 | tf_op jit(solution)/shard_map/all_to_all | solution.py:30
  57.2 11.7 %all-to-all-done.2 = bf16[32,8,1280]{2,1,0:T(8,128)(2,1)S(1)} async-done(((bf16[32,8,1280]{2,1,0:T(8,128)(2,1)}), bf16[32,8,1280]{2,1,0:T(8,128)(2,1)S(1)}, u32[]{:S(2)}, u32[]{:S(2)}) %all-to-all-start.2) | async-done | bytes 655392 | tf_op jit(solution)/shard_map/all_to_all | solution.py:30
  70.2 3.2 %collective-permute-start.1 = (bf16[4,64,1280]{2,1,0:T(8,128)(2,1)S(1)}, bf16[4,64,1280]{2,1,0:T(8,128)(2,1)S(1)}, u32[]{:S(2)}, u32[]{:S(2)}) collective-permute-start(bf16[4,64,1280]{2,1,0:T(8,128)(2,1)S(1)} %reshape.59), channel_id=1, source_target_pairs={{0,32},{32,0},{64,96},{96,64},{1,33},{33,1},{65,97},{97,65},{2,34}... | collective-permute-start | bytes 1966088 | tf_op jit(solution)/shard_map/ppermute | solution.py:47
  73.4 5.9 %collective-permute-done = bf16[4,64,1280]{2,1,0:T(8,128)(2,1)} collective-permute-done((bf16[4,64,1280]{2,1,0:T(8,128)(2,1)S(1)}, bf16[4,64,1280]{2,1,0:T(8,128)(2,1)}, u32[]{:S(2)}, u32[]{:S(2)}) %collective-permute-start) | collective-permute-done | bytes 655392 | tf_op jit(solution)/shard_map/ppermute | solution.py:46
  79.2 2.4 %collective-permute-start.2 = (bf16[4,64,1280]{2,1,0:T(8,128)(2,1)}, bf16[4,64,1280]{2,1,0:T(8,128)(2,1)S(1)}, u32[]{:S(2)}, u32[]{:S(2)}) collective-permute-start(bf16[4,64,1280]{2,1,0:T(8,128)(2,1)} %collective-permute-done), channel_id=1, source_target_pairs={{0,32},{32,0},{64,96},{96,64},{1,33},{33,1},{65,97},{97,65},{2,34}... | collective-permute-start | bytes 1966088 | tf_op jit(solution)/shard_map/ppermute | solution.py:48
  81.7 11.5 %collective-permute-done.3 = bf16[4,64,1280]{2,1,0:T(8,128)(2,1)S(1)} collective-permute-done((bf16[4,64,1280]{2,1,0:T(8,128)(2,1)S(1)}, bf16[4,64,1280]{2,1,0:T(8,128)(2,1)S(1)}, u32[]{:S(2)}, u32[]{:S(2)}) %collective-permute-start.3) | collective-permute-done | bytes 655392 | tf_op jit(solution)/shard_map/ppermute | solution.py:46
  93.2 1.4 collective-permute-start.5
  94.6 1.1 constant_dynamic-update-slice_fusion.2
  96.3 5.6 %multiply_convert_fusion = (bf16[4,256,640]{2,1,0:T(8,128)(2,1)S(1)}, f32[4,256,640]{2,1,0:T(8,128)S(1)}) fusion(bf16[4,1280,640]{2,1,0:T(8,128)(2,1)} %param.7, bf16[4,64,1280]{2,1,0:T(8,128)(2,1)S(1)} %collective-permute-done.5, bf16[4,64,1280]{2,1,0:T(8,128)(2,1)S(1)} %collective-permute-done.4, bf16[4,64,1280]{2,1,0:T(8,128)(2,1)S(1)} %collective-permute-done.3, ...), kind=kOutput, calls=%fused_computation.25 | convolution fusion | flops 1691484160 | bytes 13107200 | tf_op jit(solution)/shard_map/erd,edf->erf/dot_general | solution.py:61
  102.0 2.6 %fusion.10 = bf16[4,256,640]{2,1,0:T(8,128)(2,1)S(1)} fusion(f32[4,256,640]{2,1,0:T(8,128)S(1)} %get-tuple-element.8, bf16[4,256,1280]{2,1,0:T(8,128)(2,1)S(1)} %constant_dynamic-update-slice_fusion, bf16[4,640,1280]{2,1,0:T(8,128)(2,1)S(1)} %bitcast.64), kind=kOutput, calls=%fused_computation.15 | convolution fusion | flops 1684275200 | bytes 13107200 | tf_op jit(solution)/shard_map/erd,efd->erf/dot_general | solution.py:61
  104.6 2.2 %convolution_convert_fusion.2 = bf16[4,128,1280]{2,1,0:T(8,128)(2,1)S(1)} fusion(bf16[4,1280,640]{2,1,0:T(8,128)(2,1)S(1)} %bitcast.62, bf16[4,256,640]{2,1,0:T(8,128)(2,1)S(1)} %fusion.10), kind=kOutput, calls=%fused_computation.9 | convolution fusion | flops 839516160 | bytes 8519680 | tf_op jit(solution)/shard_map/erf,edf->erd/dot_general | solution.py:61
  107.2 1.3 convolution_convert_fusion.1
  108.7 1.2 collective-permute-done.6
  109.9 2.2 %convert_add_fusion.1 = f32[4,128,1280]{2,1,0:T(8,128)S(1)} fusion(bf16[4,128,1280]{2,1,0:T(8,128)(2,1)S(1)} %collective-permute-done.6, bf16[4,1280,640]{2,1,0:T(8,128)(2,1)S(1)} %bitcast.62, bf16[4,256,640]{2,1,0:T(8,128)(2,1)S(1)} %fusion.10), kind=kOutput, calls=%fused_computation.26 | convolution fusion | flops 840171520 | bytes 11141120 | tf_op jit(solution)/shard_map/erf,edf->erd/dot_general | solution.py:61
  112.8 1.3 convert_add_fusion
  114.1 1.5 copy-done.1
  115.6 0.9 slice.62
  116.5 0.8 collective-permute-start.9
  117.4 10.8 %collective-permute-done.7 = bf16[4,64,1280]{2,1,0:T(8,128)(2,1)S(1)} collective-permute-done((bf16[4,64,1280]{2,1,0:T(8,128)(2,1)S(1)}, bf16[4,64,1280]{2,1,0:T(8,128)(2,1)S(1)}, u32[]{:S(2)}, u32[]{:S(2)}) %collective-permute-start.7) | collective-permute-done | bytes 655392 | tf_op jit(solution)/shard_map/ppermute | solution.py:56
  128.3 1.1 reshape.63
  129.4 1.2 copy.59
  130.5 1.2 copy.60
  131.7 8.3 %all-to-all-start.3 = ((bf16[32,8,1280]{2,1,0:T(8,128)(2,1)}), bf16[32,8,1280]{2,1,0:T(8,128)(2,1)}, u32[]{:S(2)}, u32[]{:S(2)}) async-start(bf16[32,8,1280]{2,1,0:T(8,128)(2,1)} %copy.60), calls=%async_computation.3 | async-start | bytes 1310720 | tf_op jit(solution)/shard_map/all_to_all | solution.py:40
  140.0 2.3 %collective-permute-done.9 = bf16[4,64,1280]{2,1,0:T(8,128)(2,1)} collective-permute-done((bf16[4,64,1280]{2,1,0:T(8,128)(2,1)}, bf16[4,64,1280]{2,1,0:T(8,128)(2,1)}, u32[]{:S(2)}, u32[]{:S(2)}) %collective-permute-start.9) | collective-permute-done | bytes 655392 | tf_op jit(solution)/shard_map/ppermute | solution.py:56
  142.3 1.6 fusion.23
  143.9 1.1 reshape.66
  145.0 1.2 copy.62
  146.2 1.2 copy.63
  147.4 5.2 %all-to-all-done.3 = bf16[32,8,1280]{2,1,0:T(8,128)(2,1)} async-done(((bf16[32,8,1280]{2,1,0:T(8,128)(2,1)}), bf16[32,8,1280]{2,1,0:T(8,128)(2,1)}, u32[]{:S(2)}, u32[]{:S(2)}) %all-to-all-start.3) | async-done | bytes 655392 | tf_op jit(solution)/shard_map/all_to_all | solution.py:40
  152.6 4.7 %all-to-all-start.4 = ((bf16[32,8,1280]{2,1,0:T(8,128)(2,1)}), bf16[32,8,1280]{2,1,0:T(8,128)(2,1)S(1)}, u32[]{:S(2)}, u32[]{:S(2)}) async-start(bf16[32,8,1280]{2,1,0:T(8,128)(2,1)} %copy.63), calls=%async_computation.4 | async-start | bytes 1310720 | tf_op jit(solution)/shard_map/all_to_all | solution.py:40
  157.3 6.4 %convolution_convert_fusion = bf16[4,640,1280]{2,1,0:T(8,128)(2,1)} fusion(bf16[4,256,640]{2,1,0:T(8,128)(2,1)S(1)} %get-tuple-element.7, bf16[4,256,1280]{2,1,0:T(8,128)(2,1)} %copy-done.2), kind=kOutput, calls=%fused_computation.4 | convolution fusion | flops 1680998400 | bytes 10485760 | tf_op jit(solution)/shard_map/erf,erd->efd/dot_general | solution.py:61
  163.7 2.0 reshape.65
  166.2 2.0 %fusion.48 = f32[2,256,1280]{2,1,0:T(8,128)} fusion(bf16[128,2,1280]{2,1,0:T(2,128)(2,1)S(1)} %reshape.65, f32[2,128]{1,0:T(2,128)S(1)} %get-tuple-element.3, f32[2,256,128]{2,1,0:T(8,128)S(1)} %convolution_multiply_fusion), kind=kOutput, calls=%fused_computation.63 | convolution fusion | flops 167969280 | bytes 3539968 | tf_op jit(solution)/shard_map/imn,ind->imd/dot_general | solution.py:61
  169.2 1.8 convolution_bitcast_fusion.2
  171.2 3.7 %fusion.22 = bf16[128,1,1280]{2,0,1:T(8,128)(2,1)S(1)} fusion(bf16[2,256,1280]{2,1,0:T(8,128)(2,1)S(1)} %copy-done, f32[2,256,128]{2,1,0:T(8,128)S(1)} %fusion.31, f32[2,256,128]{2,1,0:T(8,128)S(1)} %convolution_bitcast_fusion.2, f32[2,256,128]{2,1,0:T(8,128)} %get-tuple-element.6, f32[2,256]{1,0:T(2,128)S(1)} %get-tuple-element.5), kind=kOutput, calls=%fused_computation.34 | convolution fusion | flops 168460928 | bytes 2426880 | tf_op jit(solution)/shard_map/imn,imd->nd/dot_general | solution.py:61
  174.9 0.8 reduce.3
  176.5 10.8 %all-to-all-start.5 = ((bf16[128,2,640]{2,1,0:T(2,128)(2,1)}), bf16[128,2,640]{2,1,0:T(2,128)(2,1)S(1)}, u32[]{:S(2)}, u32[]{:S(2)}) async-start(bf16[128,2,640]{2,1,0:T(2,128)(2,1)} %reshape.75), calls=%async_computation.5 | async-start | bytes 655360 | tf_op jit(solution)/shard_map/all_to_all | solution.py:20
  187.4 5.2 %fusion.4 = bf16[2,256,1280]{2,1,0:T(8,128)(2,1)} fusion(f32[2,256,1280]{2,1,0:T(8,128)} %fusion.48, f32[2,256,128]{2,1,0:T(8,128)S(1)} %fusion.31, f32[2,256,128]{2,1,0:T(8,128)S(1)} %convolution_bitcast_fusion.2, bf16[128,1,1280]{2,1,0:T(2,128)(2,1)S(1)} %copy-done.4, f32[2,256,128]{2,1,0:T(8,128)} %get-tuple-element.6, f32[2,256]{1,0:T(2,128)S(1)} %get-tuple-element.5), kind=kOutput, calls=%fused_computation.7 | convolution fusion | flops 169607808 | bytes 5048320 | tf_op jit(solution)/shard_map/imn,nd->imd/dot_general | solution.py:61
  192.6 6.5 %all-to-all-done.5 = bf16[128,2,640]{2,1,0:T(2,128)(2,1)S(1)} async-done(((bf16[128,2,640]{2,1,0:T(2,128)(2,1)}), bf16[128,2,640]{2,1,0:T(2,128)(2,1)S(1)}, u32[]{:S(2)}, u32[]{:S(2)}) %all-to-all-start.5) | async-done | bytes 327712 | tf_op jit(solution)/shard_map/all_to_all | solution.py:20
  (60 shorter events, 12.8 us)
Async XLA Ops:
  0.6 27.8 %copy-start = (bf16[2,256,1280]{2,1,0:T(8,128)(2,1)S(1)}, bf16[2,256,1280]{2,1,0:T(8,128)(2,1)}, u32[]{:S(2)}) copy-start(bf16[2,256,1280]{2,1,0:T(8,128)(2,1)} %param.5) | copy-start | bytes 3932164
  28.5 4.6 %copy-start.3 = (bf16[128,1,1280]{2,1,0:T(2,128)(2,1)}, bf16[128,1,1280]{2,1,0:T(2,128)(2,1)S(1)}, u32[]{:S(2)}) copy-start(bf16[128,1,1280]{2,1,0:T(2,128)(2,1)S(1)} %reshape.74) | copy-start | bytes 983044
  34.1 17.8 %all-to-all-start.1 = ((bf16[32,8,1280]{2,1,0:T(8,128)(2,1)}), bf16[32,8,1280]{2,1,0:T(8,128)(2,1)S(1)}, u32[]{:S(2)}, u32[]{:S(2)}) async-start(bf16[32,8,1280]{2,1,0:T(8,128)(2,1)} %reshape.57), calls=%async_computation.1 | async-start | bytes 1310720 | tf_op jit(solution)/shard_map/all_to_all | solution.py:30
  51.9 17.0 %all-to-all-start.2 = ((bf16[32,8,1280]{2,1,0:T(8,128)(2,1)}), bf16[32,8,1280]{2,1,0:T(8,128)(2,1)S(1)}, u32[]{:S(2)}, u32[]{:S(2)}) async-start(bf16[32,8,1280]{2,1,0:T(8,128)(2,1)} %reshape.60), calls=%async_computation.2 | async-start | bytes 1310720 | tf_op jit(solution)/shard_map/all_to_all | solution.py:30
  57.0 22.2 %collective-permute-start = (bf16[4,64,1280]{2,1,0:T(8,128)(2,1)S(1)}, bf16[4,64,1280]{2,1,0:T(8,128)(2,1)}, u32[]{:S(2)}, u32[]{:S(2)}) collective-permute-start(bf16[4,64,1280]{2,1,0:T(8,128)(2,1)S(1)} %reshape.59), channel_id=1, source_target_pairs={{0,64},{32,96},{64,0},{96,32},{1,65},{33,97},{65,1},{97,33},{2,66}... | collective-permute-start | bytes 1966088 | tf_op jit(solution)/shard_map/ppermute | solution.py:46
  70.0 23.2 %collective-permute-start.3 = (bf16[4,64,1280]{2,1,0:T(8,128)(2,1)S(1)}, bf16[4,64,1280]{2,1,0:T(8,128)(2,1)S(1)}, u32[]{:S(2)}, u32[]{:S(2)}) collective-permute-start(bf16[4,64,1280]{2,1,0:T(8,128)(2,1)S(1)} %reshape.62), channel_id=1, source_target_pairs={{0,64},{32,96},{64,0},{96,32},{1,65},{33,97},{65,1},{97,33},{2,66}... | collective-permute-start | bytes 1966088 | tf_op jit(solution)/shard_map/ppermute | solution.py:46
  70.2 25.6 %collective-permute-start.1 = (bf16[4,64,1280]{2,1,0:T(8,128)(2,1)S(1)}, bf16[4,64,1280]{2,1,0:T(8,128)(2,1)S(1)}, u32[]{:S(2)}, u32[]{:S(2)}) collective-permute-start(bf16[4,64,1280]{2,1,0:T(8,128)(2,1)S(1)} %reshape.59), channel_id=1, source_target_pairs={{0,32},{32,0},{64,96},{96,64},{1,33},{33,1},{65,97},{97,65},{2,34}... | collective-permute-start | bytes 1966088 | tf_op jit(solution)/shard_map/ppermute | solution.py:47
  73.4 22.5 %collective-permute-start.4 = (bf16[4,64,1280]{2,1,0:T(8,128)(2,1)S(1)}, bf16[4,64,1280]{2,1,0:T(8,128)(2,1)S(1)}, u32[]{:S(2)}, u32[]{:S(2)}) collective-permute-start(bf16[4,64,1280]{2,1,0:T(8,128)(2,1)S(1)} %reshape.62), channel_id=1, source_target_pairs={{0,32},{32,0},{64,96},{96,64},{1,33},{33,1},{65,97},{97,65},{2,34}... | collective-permute-start | bytes 1966088 | tf_op jit(solution)/shard_map/ppermute | solution.py:47
  79.2 16.6 %collective-permute-start.2 = (bf16[4,64,1280]{2,1,0:T(8,128)(2,1)}, bf16[4,64,1280]{2,1,0:T(8,128)(2,1)S(1)}, u32[]{:S(2)}, u32[]{:S(2)}) collective-permute-start(bf16[4,64,1280]{2,1,0:T(8,128)(2,1)} %collective-permute-done), channel_id=1, source_target_pairs={{0,32},{32,0},{64,96},{96,64},{1,33},{33,1},{65,97},{97,65},{2,34}... | collective-permute-start | bytes 1966088 | tf_op jit(solution)/shard_map/ppermute | solution.py:48
  93.2 3.1 %collective-permute-start.5 = (bf16[4,64,1280]{2,1,0:T(8,128)(2,1)S(1)}, bf16[4,64,1280]{2,1,0:T(8,128)(2,1)S(1)}, u32[]{:S(2)}, u32[]{:S(2)}) collective-permute-start(bf16[4,64,1280]{2,1,0:T(8,128)(2,1)S(1)} %collective-permute-done.3), channel_id=1, source_target_pairs={{0,32},{32,0},{64,96},{96,64},{1,33},{33,1},{65,97},{97,65},{2,34}... | collective-permute-start | bytes 1966088 | tf_op jit(solution)/shard_map/ppermute | solution.py:48
  95.8 6.1 %slice-start.2 = ((s8[6553600]{0:T(1024)(128)(4,1)}), s8[4194304]{0:T(1024)(128)(4,1)S(1)}, s32[]{:S(2)}) async-start(s8[6553600]{0:T(1024)(128)(4,1)} %bitcast.63), calls=%async_computation.8 | async-start | bytes 8388608
  95.9 6.1 %copy-start.2 = (bf16[4,256,1280]{2,1,0:T(8,128)(2,1)}, bf16[4,256,1280]{2,1,0:T(8,128)(2,1)S(1)}, u32[]{:S(2)}) copy-start(bf16[4,256,1280]{2,1,0:T(8,128)(2,1)S(1)} %constant_dynamic-update-slice_fusion) | copy-start | bytes 7864324
  95.9 6.1 %slice-start.3 = ((s8[6553600]{0:T(1024)(128)(4,1)}), s8[2359296]{0:T(1024)(128)(4,1)S(1)}, s32[]{:S(2)}) async-start(s8[6553600]{0:T(1024)(128)(4,1)} %bitcast.63), calls=%async_computation.9 | async-start | bytes 4718592
  96.3 8.2 %slice-start = ((s8[6553600]{0:T(1024)(128)(4,1)}), s8[4194304]{0:T(1024)(128)(4,1)S(1)}, s32[]{:S(2)}) async-start(s8[6553600]{0:T(1024)(128)(4,1)} %bitcast.61), calls=%async_computation.6 | async-start | bytes 8388608
  102.0 2.6 %slice-start.1 = ((s8[6553600]{0:T(1024)(128)(4,1)}), s8[2359296]{0:T(1024)(128)(4,1)S(1)}, s32[]{:S(2)}) async-start(s8[6553600]{0:T(1024)(128)(4,1)} %bitcast.61), calls=%async_computation.7 | async-start | bytes 4718592
  106.8 3.1 %collective-permute-start.6 = (bf16[4,128,1280]{2,1,0:T(8,128)(2,1)S(1)}, bf16[4,128,1280]{2,1,0:T(8,128)(2,1)S(1)}, u32[]{:S(2)}, u32[]{:S(2)}) collective-permute-start(bf16[4,128,1280]{2,1,0:T(8,128)(2,1)S(1)} %convolution_convert_fusion.2), channel_id=1, source_target_pairs={{0,32},{32,0},{64,96},{96,64},{1,33},{33,1},{65,97},{97,65},{2,34}... | collective-permute-start | bytes 3932168 | tf_op jit(solution)/shard_map/ppermute | solution.py:54
  108.4 4.4 %collective-permute-start.8 = (bf16[4,128,1280]{2,1,0:T(8,128)(2,1)S(1)}, bf16[4,128,1280]{2,1,0:T(8,128)(2,1)S(1)}, u32[]{:S(2)}, u32[]{:S(2)}) collective-permute-start(bf16[4,128,1280]{2,1,0:T(8,128)(2,1)S(1)} %convolution_convert_fusion.1), channel_id=1, source_target_pairs={{0,32},{32,0},{64,96},{96,64},{1,33},{33,1},{65,97},{97,65},{2,34}... | collective-permute-start | bytes 3932168 | tf_op jit(solution)/shard_map/ppermute | solution.py:54
  112.1 16.0 %collective-permute-start.7 = (bf16[4,64,1280]{2,1,0:T(8,128)(2,1)S(1)}, bf16[4,64,1280]{2,1,0:T(8,128)(2,1)S(1)}, u32[]{:S(2)}, u32[]{:S(2)}) collective-permute-start(bf16[4,64,1280]{2,1,0:T(8,128)(2,1)S(1)} %slice.63), channel_id=1, source_target_pairs={{0,64},{32,96},{64,0},{96,32},{1,65},{33,97},{65,1},{97,33},{2,66}... | collective-permute-start | bytes 1966088 | tf_op jit(solution)/shard_map/ppermute | solution.py:56
  114.1 1.5 copy-start.1
  116.5 25.8 %collective-permute-start.9 = (bf16[4,64,1280]{2,1,0:T(8,128)(2,1)}, bf16[4,64,1280]{2,1,0:T(8,128)(2,1)}, u32[]{:S(2)}, u32[]{:S(2)}) collective-permute-start(bf16[4,64,1280]{2,1,0:T(8,128)(2,1)} %slice.62), channel_id=1, source_target_pairs={{0,64},{32,96},{64,0},{96,32},{1,65},{33,97},{65,1},{97,33},{2,66}... | collective-permute-start | bytes 1966088 | tf_op jit(solution)/shard_map/ppermute | solution.py:56
  131.7 20.8 %all-to-all-start.3 = ((bf16[32,8,1280]{2,1,0:T(8,128)(2,1)}), bf16[32,8,1280]{2,1,0:T(8,128)(2,1)}, u32[]{:S(2)}, u32[]{:S(2)}) async-start(bf16[32,8,1280]{2,1,0:T(8,128)(2,1)} %copy.60), calls=%async_computation.3 | async-start | bytes 1310720 | tf_op jit(solution)/shard_map/all_to_all | solution.py:40
  152.6 16.4 %all-to-all-start.4 = ((bf16[32,8,1280]{2,1,0:T(8,128)(2,1)}), bf16[32,8,1280]{2,1,0:T(8,128)(2,1)S(1)}, u32[]{:S(2)}, u32[]{:S(2)}) async-start(bf16[32,8,1280]{2,1,0:T(8,128)(2,1)} %copy.63), calls=%async_computation.4 | async-start | bytes 1310720 | tf_op jit(solution)/shard_map/all_to_all | solution.py:40
  166.2 4.8 %copy-start.5 = (f32[2,256,128]{2,1,0:T(8,128)S(1)}, f32[2,256,128]{2,1,0:T(8,128)}, u32[]{:S(2)}) copy-start(f32[2,256,128]{2,1,0:T(8,128)} %get-tuple-element.4) | copy-start | bytes 786436
  171.0 16.3 %copy-start.4 = (bf16[128,1,1280]{2,1,0:T(2,128)(2,1)S(1)}, bf16[128,1,1280]{2,1,0:T(2,128)(2,1)}, u32[]{:S(2)}) copy-start(bf16[128,1,1280]{2,1,0:T(2,128)(2,1)} %copy-done.3) | copy-start | bytes 983044
  176.5 22.6 %all-to-all-start.5 = ((bf16[128,2,640]{2,1,0:T(2,128)(2,1)}), bf16[128,2,640]{2,1,0:T(2,128)(2,1)S(1)}, u32[]{:S(2)}, u32[]{:S(2)}) async-start(bf16[128,2,640]{2,1,0:T(2,128)(2,1)} %reshape.75), calls=%async_computation.5 | async-start | bytes 655360 | tf_op jit(solution)/shard_map/all_to_all | solution.py:20

commit v3 on v2

v3 whole, which is shorter than its diff:
```python
import functools
import math

import jax
import jax.numpy as jnp
from jax import lax
from jax.experimental import pallas as pl
from jax.experimental.pallas import tpu as pltpu
from jax.sharding import PartitionSpec as P

ALL = ("zl", "core", "xy", "zh")
PLANE = ("core", "xy")
SWAP = [(0, 1), (1, 0)]
CROSS = [(index, index ^ 3) for index in range(4)]
MIB = 2**20
FREE = pl.CostEstimate(flops=0, bytes_accessed=0, transcendentals=0)


def gather_router(router):
    rows = lax.axis_size(ALL) * router.shape[0]
    spread = jnp.broadcast_to(router.reshape(1, 10, 128), (rows, 10, 128))
    return lax.all_to_all(spread, ALL, split_axis=0, concat_axis=0, tiled=True).reshape(rows, -1)


def reduce_router(router_term):
    received = lax.all_to_all(router_term, ALL, split_axis=0, concat_axis=0, tiled=True)
    return jnp.sum(received.astype(jnp.float32), axis=0).reshape(1, -1)


def exchange(blocks):
    return lax.all_to_all(blocks, PLANE, split_axis=0, concat_axis=0, tiled=True)


def after(first, *later):
    return lax.optimization_barrier((first,) + later)[1:]


def product(left, right, left_dim=1, right_dim=0):
    dims = (((left_dim,), (right_dim,)), ((), ()))
    return lax.dot_general(left, right, dims, preferred_element_type=jnp.float32)


def moved(source_of, rows):
    count = rows.shape[0]
    source = source_of(lax.broadcasted_iota(jnp.int32, (count, count), 0))
    column = lax.broadcasted_iota(jnp.int32, (count, count), 1)
    pick = jnp.where(source == column, 1.0, 0.0).astype(rows.dtype)
    return product(pick, rows).astype(rows.dtype)


def bits(number, *widths):
    fields = []
    for width in reversed(widths):
        fields.append(number & ((1 << width) - 1))
        number = number >> width
    return fields[::-1]


def wire_from_slots(high, row):
    core, place, tensor, half, image, expert = bits(row, 1, 4, 1, 1, 1, 1)
    return (tensor << 8) | (image << 7) | (place << 3) | ((half ^ high) << 2) | (core << 1) | expert


def sorted_from_wire(row):
    expert, half, tensor, core, place, image = bits(row, 1, 1, 1, 1, 4, 1)
    return (core << 8) | (place << 4) | (tensor << 3) | (half << 2) | (image << 1) | expert


def wire_from_sorted(row):
    core, place, tensor, half, image, expert = bits(row, 1, 4, 1, 1, 1, 1)
    return (expert << 8) | (half << 7) | (tensor << 6) | (core << 5) | (place << 1) | image


def slots_from_wire(high, row):
    tensor, image, place, here, core, expert = bits(row, 1, 1, 4, 1, 1, 1)
    return (core << 8) | (place << 4) | (tensor << 3) | ((here ^ high) << 2) | (image << 1) | expert


def call(kernel, outs, arrays, scalars=(), limit=20, specs=None, out_specs=None, **more):
    whole = [pl.BlockSpec(memory_space=pltpu.VMEM)] * len(arrays)
    return pl.pallas_call(
        kernel,
        in_specs=[pl.BlockSpec(memory_space=pltpu.SMEM)] * len(scalars) + (specs or whole),
        out_specs=out_specs or [pl.BlockSpec(memory_space=pltpu.VMEM)] * len(outs),
        out_shape=[jax.ShapeDtypeStruct(*out) for out in outs],
        compiler_params=pltpu.CompilerParams(vmem_limit_bytes=limit * MIB),
        cost_estimate=FREE,
        **more,
    )(*scalars, *arrays)


def front_kernel(score_scale, high, tokens, router, d_out, wire, dispatch, combine):
    slots, grads = [], []
    for image in range(2):
        logits = product(tokens[image], router[...], 1, 1) * score_scale
        raised = jnp.exp(logits - jnp.max(logits, axis=0, keepdims=True))
        spread = raised / jnp.sum(raised, axis=0, keepdims=True)
        dispatch[image] = spread
        slots.append(product(spread.astype(wire.dtype), tokens[image], 0, 0).astype(wire.dtype))
        raised = jnp.exp(logits - jnp.max(logits, axis=1, keepdims=True))
        spread = raised / jnp.sum(raised, axis=1, keepdims=True)
        combine[image] = spread
        grads.append(product(spread.astype(wire.dtype), d_out[image], 0, 0).astype(wire.dtype))
    rows = jnp.concatenate(slots + grads, axis=0)
    wire[...] = moved(functools.partial(wire_from_slots, high[0]), rows).reshape(wire.shape)


def sort_kernel(wire, *parts):
    rows = moved(sorted_from_wire, wire[...].reshape(512, -1))
    for index, part in enumerate(parts):
        part[...] = rows[128 * index : 128 * index + 128].reshape(part.shape)


def spread(own, other):
    cross = lax.ppermute(other, ("zl", "zh"), CROSS)
    pair = lax.ppermute(own, "zl", SWAP)
    return [own, pair, cross, lax.ppermute(cross, "zl", SWAP)]


def expert_kernel(chunk, core, *refs):
    blocks, weights, refs = refs[:4], refs[4:8], refs[8:]
    parts, (active, grads), (held_in, held_out, sems) = refs[:4], refs[4:6], refs[6:]
    expert = 2 * core[0] + chunk
    copies = []
    for index, weight in enumerate(weights):
        held = (held_in if index % 2 == 0 else held_out).at[index // 2]
        copies.append(pltpu.make_async_copy(weight.at[expert], held, sems.at[index]))
    for copy in copies:
        copy.start()
    rows = jnp.concatenate([block[0] for block in blocks], axis=0)
    grad = jnp.concatenate([block[1] for block in blocks], axis=0)
    grads[...] = grad
    out = back = None
    for quarter in range(2):
        copies[2 * quarter].wait()
        before = product(rows, held_in[quarter])
        below = 0.5 + 0.5 * lax.erf(before * math.sqrt(0.5))
        bell = jnp.exp(-0.5 * before * before) * (1.0 / math.sqrt(2.0 * math.pi))
        slope = below + before * bell
        rounded = (before * below).astype(active.dtype)
        active[quarter] = rounded
        copies[2 * quarter + 1].wait()
        part = product(rounded, held_out[quarter])
        out = part if out is None else out + part
        rounded = (product(grad, held_out[quarter], 1, 1) * slope).astype(grad.dtype)
        part = product(rounded, held_in[quarter], 1, 1)
        back = part if back is None else back + part
    for index, part in enumerate(parts):
        mine = slice(64 * index, 64 * index + 64)
        part[0] = out[mine].astype(part.dtype)
        part[1] = back[mine].astype(part.dtype)


def expert_call(chunk, core, blocks, weights):
    half = jnp.bfloat16
    _, width, hidden = weights[0].shape
    vmem = pl.BlockSpec(memory_space=pltpu.VMEM)
    outs = [((2, 64, width), half)] * 4 + [((2, 256, hidden), half), ((256, width), half)]
    return call(
        functools.partial(expert_kernel, chunk),
        outs,
        list(blocks) + list(weights),
        [core],
        limit=56,
        specs=[vmem] * 4 + [pl.BlockSpec(memory_space=pltpu.HBM)] * 4,
        scratch_shapes=[
            pltpu.VMEM((2, width, hidden), half),
            pltpu.VMEM((2, hidden, width), half),
            pltpu.SemaphoreType.DMA((4,)),
        ],
    )


def sum_kernel(left, right, total):
    total[...] = (left[...].astype(jnp.float32) + right[...].astype(jnp.float32)).astype(total.dtype)


def sum_of(left, right):
    return call(sum_kernel, [(left.shape, left.dtype)], [left, right])[0]


def unsort_kernel(*refs):
    wire = refs[6]
    rows = []
    for index in range(2):
        own, pair, other = refs[3 * index : 3 * index + 3]
        total = own[...].astype(jnp.float32) + pair[...].astype(jnp.float32)
        rows += [total.astype(wire.dtype).reshape(128, -1), other[...].reshape(128, -1)]
    wire[...] = moved(wire_from_sorted, jnp.concatenate(rows, axis=0)).reshape(wire.shape)


def score_kernel(score_scale, high, wire, tokens, d_out, dispatch, combine, logit_grad, slot_back, term):
    rows = moved(functools.partial(slots_from_wire, high[0]), wire[...].reshape(512, -1))
    expert_out, back = rows[:256], rows[256:]
    slot_back[...] = back
    total = None
    for image in range(2):
        mine = slice(128 * image, 128 * image + 128)
        grad = product(d_out[image], expert_out[mine], 1, 1)
        share = combine[image]
        score = share * (grad - jnp.sum(share * grad, axis=1, keepdims=True))
        grad = product(tokens[image], back[mine], 1, 1)
        share = dispatch[image]
        score = score + share * (grad - jnp.sum(share * grad, axis=0, keepdims=True))
        score = (score * score_scale).astype(logit_grad.dtype)
        logit_grad[image] = score
        part = product(score, tokens[image], 0, 0)
        total = part if total is None else total + part
    for index in range(term.shape[1]):
        term[:, index] = total[:, 128 * index : 128 * index + 128].astype(term.dtype)


def token_kernel(dispatch, logit_grad, slot_back, router, d_tokens):
    for image in range(2):
        mine = slice(128 * image, 128 * image + 128)
        total = product(dispatch[image].astype(slot_back.dtype), slot_back[mine])
        d_tokens[image] = (total + product(logit_grad[image], router[...])).astype(d_tokens.dtype)


def weight_kernel(active, grads, mine, away):
    mine[...] = product(active[0], grads[...], 0, 0).astype(mine.dtype)
    away[...] = product(active[1], grads[...], 0, 0).astype(away.dtype)


def gather_kernel(core, *refs):
    blocks, whole = refs[:4], refs[4]
    step = pl.program_id(0)
    source = step ^ (2 * core[0])
    for index, block in enumerate(blocks):

        @pl.when(source == index)
        def _():
            whole[0] = block[...]


def body(tokens, router, w_in, w_out, d_out):
    images, count, width = tokens.shape
    slots = 128
    _, _, hidden = w_in.shape
    score_scale = 1.0 / math.sqrt(width)
    half = jnp.bfloat16
    high = lax.axis_index("zh").reshape(1).astype(jnp.int32)
    core = lax.axis_index("core").reshape(1).astype(jnp.int32)
    far_in = lax.ppermute(w_in, "core", SWAP)
    far_out = lax.ppermute(w_out, "core", SWAP)
    router_full = gather_router(router)
    weights = ((images, count, slots), jnp.float32)
    wire, dispatch, combine = call(
        functools.partial(front_kernel, score_scale),
        [((32, 16, width), half), weights, weights],
        [tokens, router_full, d_out],
        [high],
    )
    (wire,) = after(far_out, *after(far_in, exchange(wire)))
    own_0, other_0, own_1, other_1 = call(sort_kernel, [((2, 64, width), half)] * 4, [wire])
    rows_0 = spread(own_0, other_0)
    rows_1 = spread(own_1, other_1)
    shards = [w_in, w_out, far_in, far_out]

    rows_0 = after(rows_1[2], *rows_0)
    *parts_0, active_0, grads_0 = expert_call(0, core, rows_0, shards)
    rows_1[1:] = after(parts_0[0], *rows_1[1:])
    *parts_1, active_1, grads_1 = expert_call(1, core, rows_1, shards)
    far_0 = lax.ppermute(parts_0[3], "zl", SWAP)
    pair_0 = lax.ppermute(parts_0[1], "zl", SWAP)
    far_1 = lax.ppermute(parts_1[3], "zl", SWAP)
    pair_1 = lax.ppermute(parts_1[1], "zl", SWAP)
    far_0, pair_0 = after(parts_1[0], far_0, pair_0)
    cross_0 = sum_of(parts_0[2], far_0)
    other_0 = lax.ppermute(cross_0, ("zl", "zh"), CROSS)
    (far_1,) = after(cross_0, far_1)
    cross_1 = sum_of(parts_1[2], far_1)
    other_1 = lax.ppermute(cross_1, ("zl", "zh"), CROSS)
    shape = [((hidden, width), half)] * 2
    mine_0, away_0 = call(weight_kernel, shape, [active_0, grads_0])
    mine_1, away_1 = call(weight_kernel, shape, [active_1, grads_1])
    wire = call(
        unsort_kernel,
        [((32, 16, width), half)],
        [parts_0[0], pair_0, other_0, parts_1[0], pair_1, other_1],
    )[0]
    wire = exchange(wire)
    came_0 = lax.ppermute(away_0, "core", SWAP)
    came_1 = lax.ppermute(away_1, "core", SWAP)

    logit_grad, slot_back, term = call(
        functools.partial(score_kernel, score_scale),
        [((images, count, slots), half), ((images * slots, width), half), ((slots, width // 128, 128), half)],
        [wire, tokens, d_out, dispatch, combine],
        [high],
    )
    d_router = reduce_router(term)
    d_tokens = call(
        token_kernel,
        [((images, count, width), half)],
        [dispatch, logit_grad, slot_back, router_full],
    )[0]
    came_0, came_1 = after(logit_grad, came_0, came_1)
    d_w_out = call(
        gather_kernel,
        [(w_out.shape, half)],
        [mine_0, mine_1, came_0, came_1],
        [core],
        out_specs=[pl.BlockSpec((1, hidden, width), lambda step: (step, 0, 0))],
        grid=(4,),
    )[0]
    return (d_tokens, d_router, d_w_out)


def solution(mesh):
    split = jax.sharding.Mesh(mesh.devices.reshape(2, 2, 16, 2), ALL)
    dp, expert = ("zl", "core"), ("xy", "zh")
    placed = (
        P(ALL, None, None),
        P(ALL, None),
        P(expert, None, dp),
        P(expert, dp, None),
        P(ALL, None, None),
    )
    return jax.shard_map(
        body,
        mesh=split,
        in_specs=placed,
        out_specs=(P(ALL, None, None), P(ALL, None), P(expert, dp, None)),
        check_vma=False,
    )
```

time: 202 us -> 180 us (0.89)
  Pallas kernels: 0 us -> 38.8 us
  matrix products: 38.2 us -> 0 us
  blocking collectives: 23.2 us -> 49.3 us
  waiting for transfers between devices: 66.9 us -> 43.6 us
  local copies, waits for them, and re-layouts: 21.3 us -> 9 us
  other arithmetic: 8.38 us -> 1.9 us
  starting transfers between devices: 41.5 us -> 36 us
    pallas_call x0 -> x12, Pallas kernels: none -> 38.8 us  [call(): pl.pallas_call(kernel, in_specs=[pl.BlockSpec(memory_space=pltpu.SMEM)] *...]
    dot_general x15 -> x0, matrix products: 38.2 us -> none  [dot(): return jnp.einsum(spec, left, right, preferred_element_type=jnp.float32)]
    all_to_all x1 -> x2, blocking collectives: 23.2 us -> 49.3 us  [exchange(): lax.all_to_all(blocks, PLANE, split_axis=0, concat_axis=0, tiled=True)]
    all_to_all x5 -> x2, starting transfers between devices: 31.9 us -> 16.1 us  [the longest x1 10.7 us: gather_router(): lax.all_to_all(spread, ALL, split_axis=0, concat_axis=0, tiled=True)]
    all_to_all x5 -> x2, waiting for transfers between devices: 34.9 us -> 19.4 us  [the longest x1 13.9 us: gather_router(): lax.all_to_all(spread, ALL, split_axis=0, concat_axis=0, tiled=True)]
    reshape x12 -> x1, local copies, waits for them, and re-layouts: 11.8 us -> 0.18 us  [gather_router(): lax.all_to_all(spread, ALL, split_axis=0, concat_axis=0, tiled=True)]
    ppermute x10 -> x16, starting transfers between devices: 9.62 us -> 19.9 us  [the longest x1 8.08 us: body(): came_1 = lax.ppermute(away_1, 'core', SWAP)]
    ppermute x10 -> x16, waiting for transfers between devices: 32 us -> 24.2 us  [the longest x2 12.6 us: spread(): cross = lax.ppermute(other, ('zl', 'zh'), CROSS)]
  transfers between devices with their start and end apart: 15 -> 18, of which waited for: 11 -> 7; matrix products, arithmetic and copies ran while one was open for 18% -> 1% of each run, Pallas kernels for 0% -> 21%
where the time goes in v3:
time: 180 us; the launch traced here: 179 us
  blocking collectives  49.3 us (27%)
  waiting for transfers between devices  43.6 us (24%)
  Pallas kernels  38.8 us (22%)
  starting transfers between devices  36 us (20%)
  local copies, waits for them, and re-layouts  9 us (5%)
  other arithmetic  1.9 us (1%)
    all_to_all x2, blocking collectives, exchange(): lax.all_to_all(blocks, PLANE, split_axis=0, concat_axis=0, tiled=True)  49.3 us
    pallas_call x12, Pallas kernels, call(): pl.pallas_call(kernel, in_specs=[pl.BlockSpec(memory_space=pltpu.SMEM)] *...  38.8 us
    all_to_all x1, waiting for transfers between devices, gather_router(): lax.all_to_all(spread, ALL, split_axis=0, concat_axis=0, tiled=True)  13.9 us
    ppermute x2, waiting for transfers between devices, spread(): cross = lax.ppermute(other, ('zl', 'zh'), CROSS)  12.6 us
    all_to_all x1, starting transfers between devices, gather_router(): lax.all_to_all(spread, ALL, split_axis=0, concat_axis=0, tiled=True)  10.7 us
    ppermute x1, starting transfers between devices, body(): came_1 = lax.ppermute(away_1, 'core', SWAP)  8.08 us
    unnamed x41, local copies, waits for them, and re-layouts  7.59 us
    ppermute x1, waiting for transfers between devices, body(): far_1 = lax.ppermute(parts_1[3], 'zl', SWAP)  6.93 us
  transfers between devices with their start and end apart: 18, of which 7 were waited for; matrix products, arithmetic and copies ran while one was open for 1% of the time, Pallas kernels for 21%

profile of v3, /device:TPU:1, one launch (start us, length us, event | category | flops | bytes accessed | tf_op | source)
XLA Modules:
  0.0 179.4 jit_solution(9160611589937205399)
XLA Ops:
  0.7 1.5 collective-permute-start.1
  2.2 0.1 collective-permute-start
  2.2 0.7 reduce
  3.0 0.9 broadcast_in_dim.8
  3.8 10.7 %all-to-all-start = ((bf16[128,10,128]{2,1,0:T(8,128)(2,1)}), bf16[128,10,128]{2,1,0:T(8,128)(2,1)S(1)}, u32[]{:S(2)}, u32[]{:S(2)}) async-start(bf16[128,10,128]{2,1,0:T(8,128)(2,1)} %broadcast_in_dim.8), calls=%async_computation | async-start | bytes 1048576 | tf_op jit(solution)/shard_map/all_to_all | solution.py:22
  14.5 13.9 %all-to-all-done = bf16[128,10,128]{2,1,0:T(8,128)(2,1)S(1)} async-done(((bf16[128,10,128]{2,1,0:T(8,128)(2,1)}), bf16[128,10,128]{2,1,0:T(8,128)(2,1)S(1)}, u32[]{:S(2)}, u32[]{:S(2)}) %all-to-all-start) | async-done | bytes 327712 | tf_op jit(solution)/shard_map/all_to_all | solution.py:22
  28.4 0.4 copy.10
  28.8 0.2 copy.11.router
  29.0 2.2 %shard_map.76 = (bf16[32,16,1280]{2,1,0:T(8,128)(2,1)S(1)}, f32[2,256,128]{2,1,0:T(8,128)S(1)}, f32[2,256,128]{2,1,0:T(8,128)S(1)}) custom-call(s32[1]{0:T(128)} %bitcast.high, bf16[2,256,1280]{2,1,0:T(8,128)(2,1)S(1)} %copy-done, bf16[128,1280]{1,0:T(8,128)(2,1)S(1)} %copy.11.router, bf16[2,256,1280]{2,1,0:T(8,128)(2,1)S(1)} %copy-done.1), custom_call_target="tpu_custom_call" | custom-call | tf_op jit(solution)/shard_map/pallas_call | solution.py:81
  31.2 0.7 copy-done.18
  31.9 23.6 %all_to_all.20.wire = bf16[32,16,1280]{2,1,0:T(8,128)(2,1)S(1)} all-to-all(bf16[32,16,1280]{2,1,0:T(8,128)(2,1)S(1)} %get-tuple-element.44), channel_id=1, replica_groups=mesh['zl'=2,'core'=2,'xy'=16,'zh'=2] {'core','xy'}, dimensions={0} | all-to-all | bytes 2621440 | tf_op jit(solution)/shard_map/all_to_all | solution.py:31
  55.5 1.6 shard_map.77
  57.1 0.9 collective-permute-start.4
  58.0 1.8 collective-permute-start.2
  59.8 7.0 %collective-permute-done.4.refs_2_ = bf16[2,64,1280]{2,1,0:T(8,128)(2,1)} collective-permute-done((bf16[2,64,1280]{2,1,0:T(8,128)(2,1)S(1)}, bf16[2,64,1280]{2,1,0:T(8,128)(2,1)}, u32[]{:S(2)}, u32[]{:S(2)}) %collective-permute-start.4) | collective-permute-done | bytes 327712 | tf_op jit(solution)/shard_map/ppermute | solution.py:115
  66.8 1.5 collective-permute-start.6
  68.3 5.6 %collective-permute-done.2.refs_2_ = bf16[2,64,1280]{2,1,0:T(8,128)(2,1)} collective-permute-done((bf16[2,64,1280]{2,1,0:T(8,128)(2,1)S(1)}, bf16[2,64,1280]{2,1,0:T(8,128)(2,1)}, u32[]{:S(2)}, u32[]{:S(2)}) %collective-permute-start.2) | collective-permute-done | bytes 327712 | tf_op jit(solution)/shard_map/ppermute | solution.py:115
  73.8 9.6 %shard_map.78 = (bf16[2,64,1280]{2,1,0:T(8,128)(2,1)}, bf16[2,64,1280]{2,1,0:T(8,128)(2,1)}, bf16[2,64,1280]{2,1,0:T(8,128)(2,1)}, bf16[2,64,1280]{2,1,0:T(8,128...) custom-call(s32[1]{0:T(128)} %bitcast.2.core, bf16[2,64,1280]{2,1,0:T(8,128)(2,1)} %get-tuple-element.50.refs_0_, ...), custom_call_target="tpu_custom_call" | custom-call | tf_op jit(solution)/shard_map/pallas_call | solution.py:81
  83.5 1.5 collective-permute-start.8
  85.0 0.3 collective-permute-start.9
  85.3 2.0 %collective-permute-done.7.refs_3_ = bf16[2,64,1280]{2,1,0:T(8,128)(2,1)} collective-permute-done((bf16[2,64,1280]{2,1,0:T(8,128)(2,1)}, bf16[2,64,1280]{2,1,0:T(8,128)(2,1)}, u32[]{:S(2)}, u32[]{:S(2)}) %collective-permute-start.7) | collective-permute-done | bytes 327712 | tf_op jit(solution)/shard_map/ppermute | solution.py:117
  87.3 9.7 %shard_map.79 = (bf16[2,64,1280]{2,1,0:T(8,128)(2,1)}, bf16[2,64,1280]{2,1,0:T(8,128)(2,1)}, bf16[2,64,1280]{2,1,0:T(8,128)(2,1)}, bf16[2,64,1280]{2,1,0:T(8,128...) custom-call(s32[1]{0:T(128)} %bitcast.2.core, bf16[2,64,1280]{2,1,0:T(8,128)(2,1)} %copy-done.17, ...), custom_call_target="tpu_custom_call" | custom-call | tf_op jit(solution)/shard_map/pallas_call | solution.py:81
  97.0 0.4 collective-permute-start.12
  97.4 1.2 collective-permute-start.11
  98.6 2.6 %collective-permute-done.9.refs_1_ = bf16[2,64,1280]{2,1,0:T(8,128)(2,1)S(1)} collective-permute-done((bf16[2,64,1280]{2,1,0:T(8,128)(2,1)}, bf16[2,64,1280]{2,1,0:T(8,128)(2,1)S(1)}, u32[]{:S(2)}, u32[]{:S(2)}) %collective-permute-start.9) | collective-permute-done | bytes 327712 | tf_op jit(solution)/shard_map/ppermute | solution.py:265
  101.2 0.1 shard_map.80
  101.3 6.9 %collective-permute-done.12.right = bf16[2,64,1280]{2,1,0:T(8,128)(2,1)S(1)} collective-permute-done((bf16[2,64,1280]{2,1,0:T(8,128)(2,1)}, bf16[2,64,1280]{2,1,0:T(8,128)(2,1)S(1)}, u32[]{:S(2)}, u32[]{:S(2)}) %collective-permute-start.12) | collective-permute-done | bytes 327712 | tf_op jit(solution)/shard_map/ppermute | solution.py:266
  108.3 1.0 copy-done.16
  109.2 0.1 shard_map.81
  109.3 1.0 collective-permute-start.13
  110.3 1.8 collective-permute-start.10
  112.1 2.2 %shard_map.86 = (bf16[640,1280]{1,0:T(8,128)(2,1)S(1)}, bf16[640,1280]{1,0:T(8,128)(2,1)}) custom-call(bf16[2,256,640]{2,1,0:T(8,128)(2,1)S(1)} %copy-done.8, bf16[256,1280]{1,0:T(8,128)(2,1)S(1)} %copy-done.9), custom_call_target="tpu_custom_call" | custom-call | tf_op jit(solution)/shard_map/pallas_call | solution.py:81
  114.3 1.2 copy-done.2
  115.5 8.1 %collective-permute-start.15 = (bf16[640,1280]{1,0:T(8,128)(2,1)}, bf16[640,1280]{1,0:T(8,128)(2,1)}, u32[]{:S(2)}, u32[]{:S(2)}) collective-permute-start(bf16[640,1280]{1,0:T(8,128)(2,1)} %get-tuple-element.80), channel_id=1, source_target_pairs={{0,32},{32,0},{1,33},{33,1},{2,34},{34,2},{3,35},{35,3},{4,36},{36... | collective-permute-start | bytes 4915208 | tf_op jit(solution)/shard_map/ppermute | solution.py:284
  123.6 2.2 %shard_map.85 = (bf16[640,1280]{1,0:T(8,128)(2,1)S(1)}, bf16[640,1280]{1,0:T(8,128)(2,1)}) custom-call(bf16[2,256,640]{2,1,0:T(8,128)(2,1)S(1)} %copy-done.6, bf16[256,1280]{1,0:T(8,128)(2,1)S(1)} %copy-done.7), custom_call_target="tpu_custom_call" | custom-call | tf_op jit(solution)/shard_map/pallas_call | solution.py:81
  125.8 1.3 copy-done.4
  127.1 1.1 shard_map.82
  128.2 25.7 %all_to_all.21.wire = bf16[32,16,1280]{2,1,0:T(8,128)(2,1)S(1)} all-to-all(bf16[32,16,1280]{2,1,0:T(8,128)(2,1)S(1)} %shard_map.82), channel_id=1, replica_groups=mesh['zl'=2,'core'=2,'xy'=16,'zh'=2] {'core','xy'}, dimensions={0} | all-to-all | bytes 2621440 | tf_op jit(solution)/shard_map/all_to_all | solution.py:31
  153.8 3.1 %shard_map.83 = (bf16[2,256,128]{2,1,0:T(8,128)(2,1)S(1)}, bf16[256,1280]{1,0:T(8,128)(2,1)S(1)}, bf16[128,10,128]{2,1,0:T(8,128)(2,1)S(1)}) custom-call(s32[1]{0:T(128)} %bitcast.high, bf16[32,16,1280]{2,1,0:T(8,128)(2,1)S(1)} %all_to_all.21.wire, bf16[2,256,1280]{2,1,0:T(8,128)(2,1)S(1)} %copy-done, bf16[2,256,1280]{2,1,0:T(8,128)(2,1)S(1)} %copy-done.1, ...), custom_call_target="tpu_custom_call" | custom-call | tf_op jit(solution)/shard_map/pallas_call | solution.py:81
  156.9 0.8 copy-done.10
  157.7 0.8 copy-done.12
  158.5 5.4 %all-to-all-start.3 = ((bf16[128,10,128]{2,1,0:T(8,128)(2,1)}), bf16[128,10,128]{2,1,0:T(8,128)(2,1)}, u32[]{:S(2)}, u32[]{:S(2)}) async-start(bf16[128,10,128]{2,1,0:T(8,128)(2,1)} %copy-done.12), calls=%async_computation.3 | async-start | bytes 1048576 | tf_op jit(solution)/shard_map/all_to_all | solution.py:26
  164.0 1.2 copy-done.11
  165.2 1.9 %shard_map.84 = bf16[2,256,1280]{2,1,0:T(8,128)(2,1)} custom-call(f32[2,256,128]{2,1,0:T(8,128)S(1)} %get-tuple-element.43.dispatch, bf16[2,256,128]{2,1,0:T(8,128)(2,1)S(1)} %get-tuple-element.70.logit_grad, bf16[256,1280]{1,0:T(8,128)(2,1)S(1)} %copy-done.11, bf16[128,1280]{1,0:T(8,128)(2,1)S(1)} %copy.11.router), custom_call_target="tpu_custom_call" | custom-call | tf_op jit(solution)/shard_map/pallas_call | solution.py:81
  167.1 5.0 %shard_map.87 = bf16[4,640,1280]{2,1,0:T(8,128)(2,1)} custom-call(s32[1]{0:T(128)} %bitcast.2.core, bf16[640,1280]{1,0:T(8,128)(2,1)S(1)} %copy-done.5, bf16[640,1280]{1,0:T(8,128)(2,1)S(1)} %copy-done.3, bf16[640,1280]{1,0:T(8,128)(2,1)} %collective-permute-done.14.refs_2_, bf16[640,1280]{1,0:T(8,128)(2,1)} %collective-permute-done.15.refs_3_), custom_call_target="tpu_custom_call" | custom-call | tf_op jit(solution)/shard_map/pallas_call | solution.py:81
  172.1 5.5 %all-to-all-done.3 = bf16[128,10,128]{2,1,0:T(8,128)(2,1)} async-done(((bf16[128,10,128]{2,1,0:T(8,128)(2,1)}), bf16[128,10,128]{2,1,0:T(8,128)(2,1)}, u32[]{:S(2)}, u32[]{:S(2)}) %all-to-all-start.3) | async-done | bytes 327712 | tf_op jit(solution)/shard_map/all_to_all | solution.py:26
  177.6 1.2 convert_reduce_fusion
  178.8 0.6 copy.15
  (48 shorter events, 0.1 us)
Async XLA Ops:
  0.6 28.3 %copy-start.1 = (bf16[2,256,1280]{2,1,0:T(8,128)(2,1)S(1)}, bf16[2,256,1280]{2,1,0:T(8,128)(2,1)}, u32[]{:S(2)}) copy-start(bf16[2,256,1280]{2,1,0:T(8,128)(2,1)} %d_out.3) | copy-start | bytes 3932164
  0.6 28.3 %copy-start = (bf16[2,256,1280]{2,1,0:T(8,128)(2,1)S(1)}, bf16[2,256,1280]{2,1,0:T(8,128)(2,1)}, u32[]{:S(2)}) copy-start(bf16[2,256,1280]{2,1,0:T(8,128)(2,1)} %tokens.3) | copy-start | bytes 3932164
  0.7 54.9 %collective-permute-start.1 = (bf16[4,1280,640]{2,1,0:T(8,128)(2,1)}, bf16[4,1280,640]{2,1,0:T(8,128)(2,1)}, u32[]{:S(2)}, u32[]{:S(2)}) collective-permute-start(bf16[4,1280,640]{2,1,0:T(8,128)(2,1)} %refs_4_.3), channel_id=1, source_target_pairs={{0,32},{32,0},{1,33},{33,1},{2,34},{34,2},{3,35},{35,3},{4,36},{36... | collective-permute-start | bytes 19660808 | tf_op jit(solution)/shard_map/ppermute | solution.py:244
  2.2 53.4 %collective-permute-start = (bf16[4,640,1280]{2,1,0:T(8,128)(2,1)}, bf16[4,640,1280]{2,1,0:T(8,128)(2,1)}, u32[]{:S(2)}, u32[]{:S(2)}) collective-permute-start(bf16[4,640,1280]{2,1,0:T(8,128)(2,1)} %refs_5_.3), channel_id=1, source_target_pairs={{0,32},{32,0},{1,33},{33,1},{2,34},{34,2},{3,35},{35,3},{4,36},{36... | collective-permute-start | bytes 19660808 | tf_op jit(solution)/shard_map/ppermute | solution.py:245
  3.8 24.6 %all-to-all-start = ((bf16[128,10,128]{2,1,0:T(8,128)(2,1)}), bf16[128,10,128]{2,1,0:T(8,128)(2,1)S(1)}, u32[]{:S(2)}, u32[]{:S(2)}) async-start(bf16[128,10,128]{2,1,0:T(8,128)(2,1)} %broadcast_in_dim.8), calls=%async_computation | async-start | bytes 1048576 | tf_op jit(solution)/shard_map/all_to_all | solution.py:22
  31.2 0.7 copy-start.18
  57.1 26.3 %copy-start.17 = (bf16[2,64,1280]{2,1,0:T(8,128)(2,1)}, bf16[2,64,1280]{2,1,0:T(8,128)(2,1)S(1)}, u32[]{:S(2)}) copy-start(bf16[2,64,1280]{2,1,0:T(8,128)(2,1)S(1)} %get-tuple-element.55.refs_0_) | copy-start | bytes 983044
  57.1 9.7 %collective-permute-start.4 = (bf16[2,64,1280]{2,1,0:T(8,128)(2,1)S(1)}, bf16[2,64,1280]{2,1,0:T(8,128)(2,1)}, u32[]{:S(2)}, u32[]{:S(2)}) collective-permute-start(bf16[2,64,1280]{2,1,0:T(8,128)(2,1)S(1)} %get-tuple-element.49), channel_id=1, source_target_pairs={{0,65},{1,64},{64,1},{65,0},{2,67},{3,66},{66,3},{67,2},{4,69},{5,... | collective-permute-start | bytes 983048 | tf_op jit(solution)/shard_map/ppermute | solution.py:115
  58.0 15.8 %collective-permute-start.2 = (bf16[2,64,1280]{2,1,0:T(8,128)(2,1)S(1)}, bf16[2,64,1280]{2,1,0:T(8,128)(2,1)}, u32[]{:S(2)}, u32[]{:S(2)}) collective-permute-start(bf16[2,64,1280]{2,1,0:T(8,128)(2,1)S(1)} %get-tuple-element.47), channel_id=1, source_target_pairs={{0,65},{1,64},{64,1},{65,0},{2,67},{3,66},{66,3},{67,2},{4,69},{5,... | collective-permute-start | bytes 983048 | tf_op jit(solution)/shard_map/ppermute | solution.py:115
  59.8 14.0 %collective-permute-start.3 = (bf16[2,64,1280]{2,1,0:T(8,128)(2,1)}, bf16[2,64,1280]{2,1,0:T(8,128)(2,1)}, u32[]{:S(2)}, u32[]{:S(2)}) collective-permute-start(bf16[2,64,1280]{2,1,0:T(8,128)(2,1)} %get-tuple-element.50.refs_0_), channel_id=1, source_target_pairs={{0,64},{64,0},{1,65},{65,1},{2,66},{66,2},{3,67},{67,3},{4,68},{68... | collective-permute-start | bytes 983048 | tf_op jit(solution)/shard_map/ppermute | solution.py:116
  66.8 7.0 %collective-permute-start.5 = (bf16[2,64,1280]{2,1,0:T(8,128)(2,1)}, bf16[2,64,1280]{2,1,0:T(8,128)(2,1)}, u32[]{:S(2)}, u32[]{:S(2)}) collective-permute-start(bf16[2,64,1280]{2,1,0:T(8,128)(2,1)} %collective-permute-done.4.refs_2_), channel_id=1, source_target_pairs={{0,64},{64,0},{1,65},{65,1},{2,66},{66,2},{3,67},{67,3},{4,68},{68... | collective-permute-start | bytes 983048 | tf_op jit(solution)/shard_map/ppermute | solution.py:117
  66.8 18.5 %collective-permute-start.6 = (bf16[2,64,1280]{2,1,0:T(8,128)(2,1)S(1)}, bf16[2,64,1280]{2,1,0:T(8,128)(2,1)}, u32[]{:S(2)}, u32[]{:S(2)}) collective-permute-start(bf16[2,64,1280]{2,1,0:T(8,128)(2,1)S(1)} %get-tuple-element.55.refs_0_), channel_id=1, source_target_pairs={{0,64},{64,0},{1,65},{65,1},{2,66},{66,2},{3,67},{67,3},{4,68},{68... | collective-permute-start | bytes 983048 | tf_op jit(solution)/shard_map/ppermute | solution.py:116
  73.8 13.5 %collective-permute-start.7 = (bf16[2,64,1280]{2,1,0:T(8,128)(2,1)}, bf16[2,64,1280]{2,1,0:T(8,128)(2,1)}, u32[]{:S(2)}, u32[]{:S(2)}) collective-permute-start(bf16[2,64,1280]{2,1,0:T(8,128)(2,1)} %collective-permute-done.2.refs_2_), channel_id=1, source_target_pairs={{0,64},{64,0},{1,65},{65,1},{2,66},{66,2},{3,67},{67,3},{4,68},{68... | collective-permute-start | bytes 983048 | tf_op jit(solution)/shard_map/ppermute | solution.py:117
  83.5 15.1 %collective-permute-start.8 = (bf16[2,64,1280]{2,1,0:T(8,128)(2,1)}, bf16[2,64,1280]{2,1,0:T(8,128)(2,1)S(1)}, u32[]{:S(2)}, u32[]{:S(2)}) collective-permute-start(bf16[2,64,1280]{2,1,0:T(8,128)(2,1)} %get-tuple-element.60), channel_id=1, source_target_pairs={{0,64},{64,0},{1,65},{65,1},{2,66},{66,2},{3,67},{67,3},{4,68},{68... | collective-permute-start | bytes 983048 | tf_op jit(solution)/shard_map/ppermute | solution.py:264
  85.0 16.2 %collective-permute-start.9 = (bf16[2,64,1280]{2,1,0:T(8,128)(2,1)}, bf16[2,64,1280]{2,1,0:T(8,128)(2,1)S(1)}, u32[]{:S(2)}, u32[]{:S(2)}) collective-permute-start(bf16[2,64,1280]{2,1,0:T(8,128)(2,1)} %get-tuple-element.61), channel_id=1, source_target_pairs={{0,64},{64,0},{1,65},{65,1},{2,66},{66,2},{3,67},{67,3},{4,68},{68... | collective-permute-start | bytes 983048 | tf_op jit(solution)/shard_map/ppermute | solution.py:265
  87.3 13.9 %copy-start.15 = (bf16[2,64,1280]{2,1,0:T(8,128)(2,1)S(1)}, bf16[2,64,1280]{2,1,0:T(8,128)(2,1)}, u32[]{:S(2)}) copy-start(bf16[2,64,1280]{2,1,0:T(8,128)(2,1)} %get-tuple-element.63.left) | copy-start | bytes 983044
  97.0 15.0 %copy-start.8 = (bf16[2,256,640]{2,1,0:T(8,128)(2,1)S(1)}, bf16[2,256,640]{2,1,0:T(8,128)(2,1)}, u32[]{:S(2)}) copy-start(bf16[2,256,640]{2,1,0:T(8,128)(2,1)} %get-tuple-element.76.active) | copy-start | bytes 1966084
  97.0 15.0 %copy-start.9 = (bf16[256,1280]{1,0:T(8,128)(2,1)S(1)}, bf16[256,1280]{1,0:T(8,128)(2,1)}, u32[]{:S(2)}) copy-start(bf16[256,1280]{1,0:T(8,128)(2,1)} %get-tuple-element.77.grads) | copy-start | bytes 1966084
  97.0 11.2 %collective-permute-start.12 = (bf16[2,64,1280]{2,1,0:T(8,128)(2,1)}, bf16[2,64,1280]{2,1,0:T(8,128)(2,1)S(1)}, u32[]{:S(2)}, u32[]{:S(2)}) collective-permute-start(bf16[2,64,1280]{2,1,0:T(8,128)(2,1)} %get-tuple-element.67), channel_id=1, source_target_pairs={{0,64},{64,0},{1,65},{65,1},{2,66},{66,2},{3,67},{67,3},{4,68},{68... | collective-permute-start | bytes 983048 | tf_op jit(solution)/shard_map/ppermute | solution.py:266
  97.4 29.6 %collective-permute-start.11 = (bf16[2,64,1280]{2,1,0:T(8,128)(2,1)}, bf16[2,64,1280]{2,1,0:T(8,128)(2,1)S(1)}, u32[]{:S(2)}, u32[]{:S(2)}) collective-permute-start(bf16[2,64,1280]{2,1,0:T(8,128)(2,1)} %get-tuple-element.65), channel_id=1, source_target_pairs={{0,64},{64,0},{1,65},{65,1},{2,66},{66,2},{3,67},{67,3},{4,68},{68... | collective-permute-start | bytes 983048 | tf_op jit(solution)/shard_map/ppermute | solution.py:267
  101.2 22.3 %copy-start.6 = (bf16[2,256,640]{2,1,0:T(8,128)(2,1)S(1)}, bf16[2,256,640]{2,1,0:T(8,128)(2,1)}, u32[]{:S(2)}) copy-start(bf16[2,256,640]{2,1,0:T(8,128)(2,1)} %get-tuple-element.73.active) | copy-start | bytes 1966084
  101.2 22.3 %copy-start.7 = (bf16[256,1280]{1,0:T(8,128)(2,1)S(1)}, bf16[256,1280]{1,0:T(8,128)(2,1)}, u32[]{:S(2)}) copy-start(bf16[256,1280]{1,0:T(8,128)(2,1)} %get-tuple-element.74.grads) | copy-start | bytes 1966084
  108.3 1.0 copy-start.16
  109.2 17.8 %copy-start.13 = (bf16[2,64,1280]{2,1,0:T(8,128)(2,1)S(1)}, bf16[2,64,1280]{2,1,0:T(8,128)(2,1)}, u32[]{:S(2)}) copy-start(bf16[2,64,1280]{2,1,0:T(8,128)(2,1)} %get-tuple-element.54.refs_0_) | copy-start | bytes 983044
  109.2 17.9 %copy-start.14 = (bf16[2,64,1280]{2,1,0:T(8,128)(2,1)S(1)}, bf16[2,64,1280]{2,1,0:T(8,128)(2,1)}, u32[]{:S(2)}) copy-start(bf16[2,64,1280]{2,1,0:T(8,128)(2,1)} %get-tuple-element.59.refs_3_) | copy-start | bytes 983044
  109.3 17.7 %collective-permute-start.13 = (bf16[2,64,1280]{2,1,0:T(8,128)(2,1)S(1)}, bf16[2,64,1280]{2,1,0:T(8,128)(2,1)S(1)}, u32[]{:S(2)}, u32[]{:S(2)}) collective-permute-start(bf16[2,64,1280]{2,1,0:T(8,128)(2,1)S(1)} %shard_map.81), channel_id=1, source_target_pairs={{0,65},{1,64},{64,1},{65,0},{2,67},{3,66},{66,3},{67,2},{4,69},{5,... | collective-permute-start | bytes 983048 | tf_op jit(solution)/shard_map/ppermute | solution.py:273
  110.3 16.8 %collective-permute-start.10 = (bf16[2,64,1280]{2,1,0:T(8,128)(2,1)S(1)}, bf16[2,64,1280]{2,1,0:T(8,128)(2,1)S(1)}, u32[]{:S(2)}, u32[]{:S(2)}) collective-permute-start(bf16[2,64,1280]{2,1,0:T(8,128)(2,1)S(1)} %shard_map.80), channel_id=1, source_target_pairs={{0,65},{1,64},{64,1},{65,0},{2,67},{3,66},{66,3},{67,2},{4,69},{5,... | collective-permute-start | bytes 983048 | tf_op jit(solution)/shard_map/ppermute | solution.py:270
  114.3 1.2 copy-start.2
  115.5 51.6 %collective-permute-start.15 = (bf16[640,1280]{1,0:T(8,128)(2,1)}, bf16[640,1280]{1,0:T(8,128)(2,1)}, u32[]{:S(2)}, u32[]{:S(2)}) collective-permute-start(bf16[640,1280]{1,0:T(8,128)(2,1)} %get-tuple-element.80), channel_id=1, source_target_pairs={{0,32},{32,0},{1,33},{33,1},{2,34},{34,2},{3,35},{35,3},{4,36},{36... | collective-permute-start | bytes 4915208 | tf_op jit(solution)/shard_map/ppermute | solution.py:284
  125.8 1.3 copy-start.4
  127.0 40.0 %collective-permute-start.14 = (bf16[640,1280]{1,0:T(8,128)(2,1)}, bf16[640,1280]{1,0:T(8,128)(2,1)}, u32[]{:S(2)}, u32[]{:S(2)}) collective-permute-start(bf16[640,1280]{1,0:T(8,128)(2,1)} %get-tuple-element.79), channel_id=1, source_target_pairs={{0,32},{32,0},{1,33},{33,1},{2,34},{34,2},{3,35},{35,3},{4,36},{36... | collective-permute-start | bytes 4915208 | tf_op jit(solution)/shard_map/ppermute | solution.py:283
  128.1 25.7 %copy-start.19 = (f32[2,256,128]{2,1,0:T(8,128)S(1)}, f32[2,256,128]{2,1,0:T(8,128)}, u32[]{:S(2)}) copy-start(f32[2,256,128]{2,1,0:T(8,128)} %copy-done.18) | copy-start | bytes 786436
  156.9 0.8 copy-start.10
  157.7 0.8 copy-start.12
  158.5 8.6 %copy-start.3 = (bf16[640,1280]{1,0:T(8,128)(2,1)S(1)}, bf16[640,1280]{1,0:T(8,128)(2,1)}, u32[]{:S(2)}) copy-start(bf16[640,1280]{1,0:T(8,128)(2,1)} %copy-done.2) | copy-start | bytes 4915204
  158.5 19.1 %all-to-all-start.3 = ((bf16[128,10,128]{2,1,0:T(8,128)(2,1)}), bf16[128,10,128]{2,1,0:T(8,128)(2,1)}, u32[]{:S(2)}, u32[]{:S(2)}) async-start(bf16[128,10,128]{2,1,0:T(8,128)(2,1)} %copy-done.12), calls=%async_computation.3 | async-start | bytes 1048576 | tf_op jit(solution)/shard_map/all_to_all | solution.py:26
  164.0 3.1 %copy-start.5 = (bf16[640,1280]{1,0:T(8,128)(2,1)S(1)}, bf16[640,1280]{1,0:T(8,128)(2,1)}, u32[]{:S(2)}) copy-start(bf16[640,1280]{1,0:T(8,128)(2,1)} %copy-done.4) | copy-start | bytes 4915204
  164.0 1.2 copy-start.11

commit v4 on v3

--- a/solution.py
+++ b/solution.py
@@ -22,11 +22,6 @@
     return lax.all_to_all(spread, ALL, split_axis=0, concat_axis=0, tiled=True).reshape(rows, -1)
 
 
-def reduce_router(router_term):
-    received = lax.all_to_all(router_term, ALL, split_axis=0, concat_axis=0, tiled=True)
-    return jnp.sum(received.astype(jnp.float32), axis=0).reshape(1, -1)
-
-
 def exchange(blocks):
     return lax.all_to_all(blocks, PLANE, split_axis=0, concat_axis=0, tiled=True)
 
@@ -45,7 +40,7 @@
     source = source_of(lax.broadcasted_iota(jnp.int32, (count, count), 0))
     column = lax.broadcasted_iota(jnp.int32, (count, count), 1)
     pick = jnp.where(source == column, 1.0, 0.0).astype(rows.dtype)
-    return product(pick, rows).astype(rows.dtype)
+    return product(pick, rows)
 
 
 def bits(number, *widths):
@@ -57,18 +52,18 @@
 
 
 def wire_from_slots(high, row):
-    core, place, tensor, half, image, expert = bits(row, 1, 4, 1, 1, 1, 1)
-    return (tensor << 8) | (image << 7) | (place << 3) | ((half ^ high) << 2) | (core << 1) | expert
+    core, place, half, image, expert = bits(row, 1, 4, 1, 1, 1)
+    return (image << 7) | (place << 3) | ((half ^ high) << 2) | (core << 1) | expert
 
 
 def sorted_from_wire(row):
-    expert, half, tensor, core, place, image = bits(row, 1, 1, 1, 1, 4, 1)
-    return (core << 8) | (place << 4) | (tensor << 3) | (half << 2) | (image << 1) | expert
+    expert, half, tensor, place, image = bits(row, 1, 1, 1, 4, 1)
+    return (place << 4) | (tensor << 3) | (half << 2) | (image << 1) | expert
 
 
 def wire_from_sorted(row):
-    core, place, tensor, half, image, expert = bits(row, 1, 4, 1, 1, 1, 1)
-    return (expert << 8) | (half << 7) | (tensor << 6) | (core << 5) | (place << 1) | image
+    place, tensor, half, image, expert = bits(row, 4, 1, 1, 1, 1)
+    return (expert << 7) | (half << 6) | (tensor << 5) | (place << 1) | image
 
 
 def slots_from_wire(high, row):
@@ -76,45 +71,56 @@
     return (core << 8) | (place << 4) | (tensor << 3) | ((here ^ high) << 2) | (image << 1) | expert
 
 
-def call(kernel, outs, arrays, scalars=(), limit=20, specs=None, out_specs=None, **more):
+def call(
+    kernel, outs, arrays, scalars=(), limit=20, specs=None, out_specs=None, cost=FREE, **more
+):
     whole = [pl.BlockSpec(memory_space=pltpu.VMEM)] * len(arrays)
     return pl.pallas_call(
         kernel,
         in_specs=[pl.BlockSpec(memory_space=pltpu.SMEM)] * len(scalars) + (specs or whole),
         out_specs=out_specs or [pl.BlockSpec(memory_space=pltpu.VMEM)] * len(outs),
-        out_shape=[jax.ShapeDtypeStruct(*out) for out in outs],
+        out_shape=[(out[2] if len(out) > 2 else jax.ShapeDtypeStruct)(*out[:2]) for out in outs],
         compiler_params=pltpu.CompilerParams(vmem_limit_bytes=limit * MIB),
-        cost_estimate=FREE,
+        cost_estimate=cost,
         **more,
     )(*scalars, *arrays)
 
 
-def front_kernel(score_scale, high, tokens, router, d_out, wire, dispatch, combine):
+def front_kernel(
+    score_scale, high, tokens, router, d_out, wire, dispatch, combine, held_0, held_1, sems
+):
     slots, grads = [], []
     for image in range(2):
         logits = product(tokens[image], router[...], 1, 1) * score_scale
         raised = jnp.exp(logits - jnp.max(logits, axis=0, keepdims=True))
-        spread = raised / jnp.sum(raised, axis=0, keepdims=True)
-        dispatch[image] = spread
-        slots.append(product(spread.astype(wire.dtype), tokens[image], 0, 0).astype(wire.dtype))
+        share = raised / jnp.sum(raised, axis=0, keepdims=True)
+        held_0[image] = share
+        slots.append(product(share.astype(wire.dtype), tokens[image], 0, 0).astype(wire.dtype))
         raised = jnp.exp(logits - jnp.max(logits, axis=1, keepdims=True))
-        spread = raised / jnp.sum(raised, axis=1, keepdims=True)
-        combine[image] = spread
-        grads.append(product(spread.astype(wire.dtype), d_out[image], 0, 0).astype(wire.dtype))
-    rows = jnp.concatenate(slots + grads, axis=0)
-    wire[...] = moved(functools.partial(wire_from_slots, high[0]), rows).reshape(wire.shape)
+        share = raised / jnp.sum(raised, axis=1, keepdims=True)
+        held_1[image] = share
+        grads.append(product(share.astype(wire.dtype), d_out[image], 0, 0).astype(wire.dtype))
+    copies = [
+        pltpu.make_async_copy(held_0, dispatch, sems.at[0]),
+        pltpu.make_async_copy(held_1, combine, sems.at[1]),
+    ]
+    for copy in copies:
+        copy.start()
+    order = functools.partial(wire_from_slots, high[0])
+    rows = [moved(order, jnp.concatenate(part, axis=0)) for part in (slots, grads)]
+    rows = jnp.concatenate([part.reshape(32, 8, -1) for part in rows], axis=1)
+    wire[...] = rows.astype(wire.dtype)
+    for copy in copies:
+        copy.wait()
 
 
 def sort_kernel(wire, *parts):
-    rows = moved(sorted_from_wire, wire[...].reshape(512, -1))
-    for index, part in enumerate(parts):
-        part[...] = rows[128 * index : 128 * index + 128].reshape(part.shape)
-
-
-def spread(own, other):
-    cross = lax.ppermute(other, ("zl", "zh"), CROSS)
-    pair = lax.ppermute(own, "zl", SWAP)
-    return [own, pair, cross, lax.ppermute(cross, "zl", SWAP)]
+    for core in range(2):
+        rows = wire[16 * core : 16 * core + 16].reshape(256, -1)
+        rows = moved(sorted_from_wire, rows).astype(wire.dtype)
+        for index in range(8):
+            part = parts[index // 2]
+            part[index % 2, 32 * core : 32 * core + 32] = rows[32 * index : 32 * index + 32]
 
 
 def expert_kernel(chunk, core, *refs):
@@ -161,8 +167,9 @@
         outs,
         list(blocks) + list(weights),
         [core],
-        limit=56,
+        limit=28,
         specs=[vmem] * 4 + [pl.BlockSpec(memory_space=pltpu.HBM)] * 4,
+        cost=pl.CostEstimate(flops=8 * 10**9, bytes_accessed=24 * MIB, transcendentals=0),
         scratch_shapes=[
             pltpu.VMEM((2, width, hidden), half),
             pltpu.VMEM((2, hidden, width), half),
@@ -181,18 +188,31 @@
 
 def unsort_kernel(*refs):
     wire = refs[6]
-    rows = []
+    totals = []
     for index in range(2):
         own, pair, other = refs[3 * index : 3 * index + 3]
         total = own[...].astype(jnp.float32) + pair[...].astype(jnp.float32)
-        rows += [total.astype(wire.dtype).reshape(128, -1), other[...].reshape(128, -1)]
-    wire[...] = moved(wire_from_sorted, jnp.concatenate(rows, axis=0)).reshape(wire.shape)
-
-
-def score_kernel(score_scale, high, wire, tokens, d_out, dispatch, combine, logit_grad, slot_back, term):
+        totals += [total.astype(wire.dtype), other[...]]
+    for core in range(2):
+        mine = slice(32 * core, 32 * core + 32)
+        rows = [total[tensor, mine] for total in totals for tensor in range(2)]
+        rows = moved(wire_from_sorted, jnp.concatenate(rows, axis=0)).astype(wire.dtype)
+        wire[16 * core : 16 * core + 16] = rows.reshape(16, 16, -1)
+
+
+def score_kernel(
+    score_scale, high, wire, tokens, d_out, dispatch, combine,
+    logit_grad, slot_back, term, held_back, held_term, sems,
+):
     rows = moved(functools.partial(slots_from_wire, high[0]), wire[...].reshape(512, -1))
+    rows = rows.astype(wire.dtype)
     expert_out, back = rows[:256], rows[256:]
-    slot_back[...] = back
+    held_back[...] = back
+    copies = [
+        pltpu.make_async_copy(held_back, slot_back, sems.at[0]),
+        pltpu.make_async_copy(held_term, term, sems.at[1]),
+    ]
+    copies[0].start()
     total = None
     for image in range(2):
         mine = slice(128 * image, 128 * image + 128)
@@ -207,7 +227,10 @@
         part = product(score, tokens[image], 0, 0)
         total = part if total is None else total + part
     for index in range(term.shape[1]):
-        term[:, index] = total[:, 128 * index : 128 * index + 128].astype(term.dtype)
+        held_term[:, index] = total[:, 128 * index : 128 * index + 128].astype(term.dtype)
+    copies[1].start()
+    for copy in copies:
+        copy.wait()
 
 
 def token_kernel(dispatch, logit_grad, slot_back, router, d_tokens):
@@ -217,20 +240,67 @@
         d_tokens[image] = (total + product(logit_grad[image], router[...])).astype(d_tokens.dtype)
 
 
-def weight_kernel(active, grads, mine, away):
-    mine[...] = product(active[0], grads[...], 0, 0).astype(mine.dtype)
-    away[...] = product(active[1], grads[...], 0, 0).astype(away.dtype)
-
-
-def gather_kernel(core, *refs):
-    blocks, whole = refs[:4], refs[4]
-    step = pl.program_id(0)
-    source = step ^ (2 * core[0])
-    for index, block in enumerate(blocks):
-
-        @pl.when(source == index)
-        def _():
-            whole[0] = block[...]
+def weight_kernel(chunk, core, active, grads, *refs):
+    whole, away, held, sems = refs[-4:]
+    copies = []
+    for index, ref in enumerate((whole.at[2 * core[0] + chunk], away)):
+        held[index] = product(active[index], grads[...], 0, 0).astype(held.dtype)
+        copies.append(pltpu.make_async_copy(held.at[index], ref, sems.at[index]))
+        copies[index].start()
+    for copy in copies:
+        copy.wait()
+
+
+def weight_call(chunk, core, active, grads, *whole):
+    shape = (active.shape[2], grads.shape[1])
+    hbm = pl.BlockSpec(memory_space=pltpu.HBM)
+    return call(
+        functools.partial(weight_kernel, chunk),
+        [((4,) + shape, grads.dtype, pltpu.HBM), (shape, grads.dtype, pltpu.HBM)],
+        [active, grads, *whole],
+        [core],
+        specs=[pl.BlockSpec(memory_space=pltpu.VMEM)] * 2 + [hbm] * len(whole),
+        out_specs=[hbm] * 2,
+        scratch_shapes=[pltpu.VMEM((2,) + shape, grads.dtype), pltpu.SemaphoreType.DMA((2,))],
+        input_output_aliases={3: 0} if whole else {},
+    )
+
+
+def gather_kernel(core, came_0, came_1, _, whole, held, sems):
+    first = 2 - 2 * core[0]
+    arrive = [
+        pltpu.make_async_copy(came, held.at[index], sems.at[index])
+        for index, came in enumerate((came_0, came_1))
+    ]
+    leave = [
+        pltpu.make_async_copy(held.at[index], whole.at[first + index], sems.at[2 + index])
+        for index in range(2)
+    ]
+    for copy in arrive:
+        copy.start()
+    for coming, going in zip(arrive, leave):
+        coming.wait()
+        going.start()
+    for copy in leave:
+        copy.wait()
+
+
+def gather_call(core, came_0, came_1, whole):
+    hbm = pl.BlockSpec(memory_space=pltpu.HBM)
+    came = [pltpu.with_memory_space_constraint(part, pltpu.HBM) for part in (came_0, came_1)]
+    return call(
+        gather_kernel,
+        [(whole.shape, whole.dtype, pltpu.HBM)],
+        [*came, whole],
+        [core],
+        specs=[hbm] * 3,
+        out_specs=[hbm],
+        scratch_shapes=[
+            pltpu.VMEM((2,) + whole.shape[1:], whole.dtype),
+            pltpu.SemaphoreType.DMA((4,)),
+        ],
+        input_output_aliases={3: 0},
+    )[0]
 
 
 def body(tokens, router, w_in, w_out, d_out):
@@ -245,64 +315,90 @@
     far_out = lax.ppermute(w_out, "core", SWAP)
     router_full = gather_router(router)
     weights = ((images, count, slots), jnp.float32)
+    vmem = pl.BlockSpec(memory_space=pltpu.VMEM)
+    hbm = pl.BlockSpec(memory_space=pltpu.HBM)
     wire, dispatch, combine = call(
         functools.partial(front_kernel, score_scale),
-        [((32, 16, width), half), weights, weights],
+        [((32, 16, width), half), weights + (pltpu.HBM,), weights + (pltpu.HBM,)],
         [tokens, router_full, d_out],
         [high],
+        out_specs=[vmem, hbm, hbm],
+        scratch_shapes=[pltpu.VMEM(*weights)] * 2 + [pltpu.SemaphoreType.DMA((2,))],
     )
     (wire,) = after(far_out, *after(far_in, exchange(wire)))
-    own_0, other_0, own_1, other_1 = call(sort_kernel, [((2, 64, width), half)] * 4, [wire])
-    rows_0 = spread(own_0, other_0)
-    rows_1 = spread(own_1, other_1)
-    shards = [w_in, w_out, far_in, far_out]
-
-    rows_0 = after(rows_1[2], *rows_0)
+    own_0, other_0, own_1, other_1 = call(
+        sort_kernel,
+        [((2, 64, width), half)] * 4,
+        [wire],
+        cost=pl.CostEstimate(flops=10**6, bytes_accessed=40 * MIB, transcendentals=0),
+    )
+    pair_0 = lax.ppermute(own_0, "zl", SWAP)
+    cross_0 = lax.ppermute(other_0, ("zl", "zh"), CROSS)
+    (cross_0,) = after(pair_0, cross_0)
+    far_0 = lax.ppermute(cross_0, "zl", SWAP)
+    (other_1,) = after(cross_0, other_1)
+    cross_1 = lax.ppermute(other_1, ("zl", "zh"), CROSS)
+    (own_1,) = after(far_0, own_1)
+    pair_1 = lax.ppermute(own_1, "zl", SWAP)
+    far_1 = lax.ppermute(cross_1, "zl", SWAP)
+    rows_0 = [own_0, pair_0, cross_0, far_0]
+    rows_1 = [own_1, pair_1, cross_1, far_1]
+    shards = [
+        pltpu.with_memory_space_constraint(shard, pltpu.HBM)
+        for shard in (w_in, w_out, far_in, far_out)
+    ]
+
     *parts_0, active_0, grads_0 = expert_call(0, core, rows_0, shards)
-    rows_1[1:] = after(parts_0[0], *rows_1[1:])
+    rows_1[1::2] = after(parts_0[0], *rows_1[1::2])
     *parts_1, active_1, grads_1 = expert_call(1, core, rows_1, shards)
     far_0 = lax.ppermute(parts_0[3], "zl", SWAP)
     pair_0 = lax.ppermute(parts_0[1], "zl", SWAP)
     far_1 = lax.ppermute(parts_1[3], "zl", SWAP)
     pair_1 = lax.ppermute(parts_1[1], "zl", SWAP)
-    far_0, pair_0 = after(parts_1[0], far_0, pair_0)
+    (far_0,) = after(parts_1[0], far_0)
     cross_0 = sum_of(parts_0[2], far_0)
     other_0 = lax.ppermute(cross_0, ("zl", "zh"), CROSS)
-    (far_1,) = after(cross_0, far_1)
+    (active_0,) = after(cross_0, active_0)
+    whole, away_0 = weight_call(0, core, active_0, grads_0)
+    (far_1,) = after(away_0, far_1)
     cross_1 = sum_of(parts_1[2], far_1)
     other_1 = lax.ppermute(cross_1, ("zl", "zh"), CROSS)
-    shape = [((hidden, width), half)] * 2
-    mine_0, away_0 = call(weight_kernel, shape, [active_0, grads_0])
-    mine_1, away_1 = call(weight_kernel, shape, [active_1, grads_1])
+    (active_1,) = after(cross_1, active_1)
+    whole, away_1 = weight_call(1, core, active_1, grads_1, whole)
+    other_0, other_1 = after(away_1, other_0, other_1)
+    came_0 = lax.ppermute(away_0, "core", SWAP)
+    came_1 = lax.ppermute(away_1, "core", SWAP)
     wire = call(
         unsort_kernel,
         [((32, 16, width), half)],
         [parts_0[0], pair_0, other_0, parts_1[0], pair_1, other_1],
     )[0]
     wire = exchange(wire)
-    came_0 = lax.ppermute(away_0, "core", SWAP)
-    came_1 = lax.ppermute(away_1, "core", SWAP)
 
     logit_grad, slot_back, term = call(
         functools.partial(score_kernel, score_scale),
-        [((images, count, slots), half), ((images * slots, width), half), ((slots, width // 128, 128), half)],
+        [
+            ((images, count, slots), half),
+            ((images * slots, width), half, pltpu.HBM),
+            ((slots, width // 128, 128), half, pltpu.HBM),
+        ],
         [wire, tokens, d_out, dispatch, combine],
         [high],
-    )
-    d_router = reduce_router(term)
+        out_specs=[vmem, hbm, hbm],
+        scratch_shapes=[
+            pltpu.VMEM((images * slots, width), half),
+            pltpu.VMEM((slots, width // 128, 128), half),
+            pltpu.SemaphoreType.DMA((2,)),
+        ],
+    )
+    received = lax.all_to_all(term, ALL, split_axis=0, concat_axis=0, tiled=True)
+    d_router = jnp.sum(received.astype(jnp.float32), axis=0).reshape(1, -1)
+    d_w_out = gather_call(core, *after(logit_grad, came_0, came_1), whole)
+    (slot_back,) = after(d_w_out, slot_back)
     d_tokens = call(
         token_kernel,
         [((images, count, width), half)],
         [dispatch, logit_grad, slot_back, router_full],
-    )[0]
-    came_0, came_1 = after(logit_grad, came_0, came_1)
-    d_w_out = call(
-        gather_kernel,
-        [(w_out.shape, half)],
-        [mine_0, mine_1, came_0, came_1],
-        [core],
-        out_specs=[pl.BlockSpec((1, hidden, width), lambda step: (step, 0, 0))],
-        grid=(4,),
     )[0]
     return (d_tokens, d_router, d_w_out)
 

time: 180 us -> 172 us (0.956)
  blocking collectives: 49.3 us -> 54.3 us
  Pallas kernels: 38.8 us -> 34 us
  local copies, waits for them, and re-layouts: 9 us -> 5.44 us
  waiting for transfers between devices: 43.6 us -> 41 us
    ppermute x1, starting transfers between devices: 0.01 us -> 9.7 us  [body(): came_0 = lax.ppermute(away_0, 'core', SWAP)]
    ppermute x1, starting transfers between devices: 8.08 us -> 0.09 us  [body(): came_1 = lax.ppermute(away_1, 'core', SWAP)]
    all_to_all x2, blocking collectives: 49.3 us -> 54.3 us  [exchange(): lax.all_to_all(blocks, PLANE, split_axis=0, concat_axis=0, tiled=True)]
    pallas_call x12, Pallas kernels: 38.8 us -> 34 us  [call(): pl.pallas_call(kernel, in_specs=[pl.BlockSpec(memory_space=pltpu.SMEM)] *...]
    ppermute x1, waiting for transfers between devices: 6.93 us -> 2.41 us  [body(): far_1 = lax.ppermute(parts_1[3], 'zl', SWAP)]
    unnamed x41 -> x19, local copies, waits for them, and re-layouts: 7.59 us -> 4.03 us
    all_to_all x1, waiting for transfers between devices: 5.5 us -> 8.72 us  [body(): lax.all_to_all(term, ALL, split_axis=0, concat_axis=0, tiled=True)]
    ppermute x1, waiting for transfers between devices: 2.63 us -> 0.01 us  [body(): pair_0 = lax.ppermute(parts_0[1], 'zl', SWAP)]
  transfers between devices with their start and end apart: 18 -> 18, of which waited for: 7 -> 7; matrix products, arithmetic and copies ran while one was open for 1% -> 1% of each run, Pallas kernels for 21% -> 19%
where the time goes in v4:
time: 172 us; the launch traced here: 171 us
  blocking collectives  54.3 us (32%)
  waiting for transfers between devices  41 us (24%)
  starting transfers between devices  34.8 us (20%)
  Pallas kernels  34 us (20%)
  local copies, waits for them, and re-layouts  5.44 us (3%)
    all_to_all x2, blocking collectives, exchange(): lax.all_to_all(blocks, PLANE, split_axis=0, concat_axis=0, tiled=True)  54.3 us
    pallas_call x12, Pallas kernels, call(): pl.pallas_call(kernel, in_specs=[pl.BlockSpec(memory_space=pltpu.SMEM)] *...  34 us
    all_to_all x1, waiting for transfers between devices, gather_router(): lax.all_to_all(spread, ALL, split_axis=0, concat_axis=0, tiled=True)  13.9 us
    all_to_all x1, starting transfers between devices, gather_router(): lax.all_to_all(spread, ALL, split_axis=0, concat_axis=0, tiled=True)  10.7 us
    ppermute x1, starting transfers between devices, body(): came_0 = lax.ppermute(away_0, 'core', SWAP)  9.7 us
    all_to_all x1, waiting for transfers between devices, body(): lax.all_to_all(term, ALL, split_axis=0, concat_axis=0, tiled=True)  8.72 us
    ppermute x1, waiting for transfers between devices, body(): cross_0 = lax.ppermute(other_0, ('zl', 'zh'), CROSS)  8 us
    ppermute x1, waiting for transfers between devices, body(): far_0 = lax.ppermute(cross_0, 'zl', SWAP)  6.56 us
  transfers between devices with their start and end apart: 18, of which 7 were waited for; matrix products, arithmetic and copies ran while one was open for 1% of the time, Pallas kernels for 19%

profile of v4, /device:TPU:1, one launch (start us, length us, event | category | flops | bytes accessed | tf_op | source)
XLA Modules:
  0.0 171.3 jit_solution(14240759618385980265)
XLA Ops:
  0.7 1.5 collective-permute-start.1
  2.2 0.1 collective-permute-start
  2.2 0.7 reduce
  3.0 0.9 broadcast_in_dim.8
  3.8 10.7 %all-to-all-start = ((bf16[128,10,128]{2,1,0:T(8,128)(2,1)}), bf16[128,10,128]{2,1,0:T(8,128)(2,1)S(1)}, u32[]{:S(2)}, u32[]{:S(2)}) async-start(bf16[128,10,128]{2,1,0:T(8,128)(2,1)} %broadcast_in_dim.8), calls=%async_computation | async-start | bytes 1048576 | tf_op jit(solution)/shard_map/all_to_all | solution.py:22
  14.5 13.9 %all-to-all-done = bf16[128,10,128]{2,1,0:T(8,128)(2,1)S(1)} async-done(((bf16[128,10,128]{2,1,0:T(8,128)(2,1)}), bf16[128,10,128]{2,1,0:T(8,128)(2,1)S(1)}, u32[]{:S(2)}, u32[]{:S(2)}) %all-to-all-start) | async-done | bytes 327712 | tf_op jit(solution)/shard_map/all_to_all | solution.py:22
  28.4 0.4 copy.12
  28.8 0.2 copy.13.router
  29.0 1.9 %shard_map.76 = (bf16[32,16,1280]{2,1,0:T(8,128)(2,1)S(1)}, f32[2,256,128]{2,1,0:T(8,128)}, f32[2,256,128]{2,1,0:T(8,128)}) custom-call(s32[1]{0:T(128)} %bitcast.high, bf16[2,256,1280]{2,1,0:T(8,128)(2,1)S(1)} %copy-done, bf16[128,1280]{1,0:T(8,128)(2,1)S(1)} %copy.13.router, bf16[2,256,1280]{2,1,0:T(8,128)(2,1)S(1)} %copy-done.1), custom_call_target="tpu_custom_call" | custom-call | tf_op jit(solution)/shard_map/pallas_call | solution.py:78
  30.8 23.6 %all_to_all.20.wire = bf16[32,16,1280]{2,1,0:T(8,128)(2,1)S(1)} all-to-all(bf16[32,16,1280]{2,1,0:T(8,128)(2,1)S(1)} %get-tuple-element.46), channel_id=1, replica_groups=mesh['zl'=2,'core'=2,'xy'=16,'zh'=2] {'core','xy'}, dimensions={0} | all-to-all | bytes 2621440 | tf_op jit(solution)/shard_map/all_to_all | solution.py:26
  54.5 1.3 shard_map.77
  55.7 0.9 collective-permute-start.3
  56.6 0.1 collective-permute-start.2
  56.7 0.7 copy-done.5
  57.4 8.0 %collective-permute-done.3.refs_2_ = bf16[2,64,1280]{2,1,0:T(8,128)(2,1)} collective-permute-done((bf16[2,64,1280]{2,1,0:T(8,128)(2,1)S(1)}, bf16[2,64,1280]{2,1,0:T(8,128)(2,1)}, u32[]{:S(2)}, u32[]{:S(2)}) %collective-permute-start.3) | collective-permute-done | bytes 327712 | tf_op jit(solution)/shard_map/ppermute | solution.py:336
  65.4 0.7 copy-done.7
  66.1 1.2 collective-permute-start.7
  67.4 6.6 %collective-permute-done.4.refs_3_ = bf16[2,64,1280]{2,1,0:T(8,128)(2,1)} collective-permute-done((bf16[2,64,1280]{2,1,0:T(8,128)(2,1)}, bf16[2,64,1280]{2,1,0:T(8,128)(2,1)}, u32[]{:S(2)}, u32[]{:S(2)}) %collective-permute-start.4) | collective-permute-done | bytes 327712 | tf_op jit(solution)/shard_map/ppermute | solution.py:338
  73.9 0.3 collective-permute-start.6
  74.2 0.9 collective-permute-done.7.refs_2_
  75.1 0.3 collective-permute-start.8
  75.4 1.0 copy-done.6
  76.4 1.0 copy-done.8
  77.3 8.2 %shard_map.78 = (bf16[2,64,1280]{2,1,0:T(8,128)(2,1)S(1)}, bf16[2,64,1280]{2,1,0:T(8,128)(2,1)S(1)}, bf16[2,64,1280]{2,1,0:T(8,128)(2,1)S(1)}, bf16[2,64,1280]{2...) custom-call(s32[1]{0:T(128)} %bitcast.2.core, ...), custom_call_target="tpu_custom_call" | custom-call | flops 8000000000 | bytes 25165824 | tf_op jit(solution)/shard_map/pallas_call | solution.py:78
  85.5 1.5 collective-permute-start.9
  87.0 0.5 collective-permute-done.8.refs_3_
  87.5 8.1 %shard_map.79 = (bf16[2,64,1280]{2,1,0:T(8,128)(2,1)S(1)}, bf16[2,64,1280]{2,1,0:T(8,128)(2,1)S(1)}, bf16[2,64,1280]{2,1,0:T(8,128)(2,1)S(1)}, bf16[2,64,1280]{2...) custom-call(s32[1]{0:T(128)} %bitcast.2.core, ...), custom_call_target="tpu_custom_call" | custom-call | flops 8000000000 | bytes 25165824 | tf_op jit(solution)/shard_map/pallas_call | solution.py:78
  95.6 0.6 collective-permute-start.10
  96.2 0.1 shard_map.80
  96.3 0.4 collective-permute-start.11
  96.7 2.4 %shard_map.81 = (bf16[4,640,1280]{2,1,0:T(8,128)(2,1)}, bf16[640,1280]{1,0:T(8,128)(2,1)}) custom-call(s32[1]{0:T(128)} %bitcast.2.core, bf16[2,256,640]{2,1,0:T(8,128)(2,1)S(1)} %get-tuple-element.66.active, bf16[256,1280]{1,0:T(8,128)(2,1)S(1)} %get-tuple-element.67.grads), custom_call_target="tpu_custom_call" | custom-call | tf_op jit(solution)/shard_map/pallas_call | solution.py:78
  99.2 2.4 %collective-permute-done.10.right = bf16[2,64,1280]{2,1,0:T(8,128)(2,1)S(1)} collective-permute-done((bf16[2,64,1280]{2,1,0:T(8,128)(2,1)S(1)}, bf16[2,64,1280]{2,1,0:T(8,128)(2,1)S(1)}, u32[]{:S(2)}, u32[]{:S(2)}) %collective-permute-start.10) | collective-permute-done | bytes 327712 | tf_op jit(solution)/shard_map/ppermute | solution.py:356
  101.6 0.1 shard_map.82
  101.6 0.8 collective-permute-start.12
  102.5 1.5 collective-permute-start.13
  103.9 9.7 %collective-permute-start.14 = (bf16[640,1280]{1,0:T(8,128)(2,1)}, bf16[640,1280]{1,0:T(8,128)(2,1)}, u32[]{:S(2)}, u32[]{:S(2)}) collective-permute-start(bf16[640,1280]{1,0:T(8,128)(2,1)} %get-tuple-element.68), channel_id=1, source_target_pairs={{0,32},{32,0},{1,33},{33,1},{2,34},{34,2},{3,35},{35,3},{4,36},{36... | collective-permute-start | bytes 4915208 | tf_op jit(solution)/shard_map/ppermute | solution.py:369
  113.7 2.5 %shard_map.83 = (bf16[4,640,1280]{2,1,0:T(8,128)(2,1)}, bf16[640,1280]{1,0:T(8,128)(2,1)}) custom-call(s32[1]{0:T(128)} %bitcast.2.core, bf16[2,256,640]{2,1,0:T(8,128)(2,1)S(1)} %get-tuple-element.72.active, bf16[256,1280]{1,0:T(8,128)(2,1)S(1)} %get-tuple-element.73.grads, ...), custom_call_target="tpu_custom_call", output_to_operand_aliasing={{0}: (3, {})} | custom-call | tf_op jit(solution)/shard_map/pallas_call | solution.py:78
  116.1 0.1 collective-permute-start.15
  116.3 0.6 shard_map.84
  116.9 30.7 %all_to_all.21.wire = bf16[32,16,1280]{2,1,0:T(8,128)(2,1)S(1)} all-to-all(bf16[32,16,1280]{2,1,0:T(8,128)(2,1)S(1)} %shard_map.84), channel_id=1, replica_groups=mesh['zl'=2,'core'=2,'xy'=16,'zh'=2] {'core','xy'}, dimensions={0} | all-to-all | bytes 2621440 | tf_op jit(solution)/shard_map/all_to_all | solution.py:26
  147.6 3.9 %shard_map.85 = (bf16[2,256,128]{2,1,0:T(8,128)(2,1)S(1)}, bf16[256,1280]{1,0:T(8,128)(2,1)}, bf16[128,10,128]{2,1,0:T(8,128)(2,1)}) custom-call(s32[1]{0:T(128)} %bitcast.high, bf16[32,16,1280]{2,1,0:T(8,128)(2,1)S(1)} %all_to_all.21.wire, bf16[2,256,1280]{2,1,0:T(8,128)(2,1)S(1)} %copy-done, bf16[2,256,1280]{2,1,0:T(8,128)(2,1)S(1)} %copy-done.1, ...), custom_call_target="tpu_custom_call" | custom-call | tf_op jit(solution)/shard_map/pallas_call | solution.py:78
  151.4 5.2 %all-to-all-start.3 = ((bf16[128,10,128]{2,1,0:T(8,128)(2,1)}), bf16[128,10,128]{2,1,0:T(8,128)(2,1)S(1)}, u32[]{:S(2)}, u32[]{:S(2)}) async-start(bf16[128,10,128]{2,1,0:T(8,128)(2,1)} %get-tuple-element.86), calls=%async_computation.3 | async-start | bytes 1048576 | tf_op jit(solution)/shard_map/all_to_all | solution.py:394
  156.6 0.0 copy-start.3
  156.7 3.2 %shard_map.86 = bf16[4,640,1280]{2,1,0:T(8,128)(2,1)} custom-call(s32[1]{0:T(128)} %bitcast.2.core, bf16[640,1280]{1,0:T(8,128)(2,1)} %collective-permute-done.14.came_0, bf16[640,1280]{1,0:T(8,128)(2,1)} %collective-permute-done.15.came_1, bf16[4,640,1280]{2,1,0:T(8,128)(2,1)} %get-tuple-element.83._), custom_call_target="tpu_custom_call", output_to_operand_aliasing={{}: (3, {})} | custom-call | tf_op jit(solution)/shard_map/pallas_call | solution.py:78
  159.9 1.9 %shard_map.87 = bf16[2,256,1280]{2,1,0:T(8,128)(2,1)} custom-call(f32[2,256,128]{2,1,0:T(8,128)S(1)} %copy-done.2, bf16[2,256,128]{2,1,0:T(8,128)(2,1)S(1)} %get-tuple-element.80.logit_grad, bf16[256,1280]{1,0:T(8,128)(2,1)S(1)} %copy-done.3, bf16[128,1280]{1,0:T(8,128)(2,1)S(1)} %copy.13.router), custom_call_target="tpu_custom_call" | custom-call | tf_op jit(solution)/shard_map/pallas_call | solution.py:78
  161.8 8.7 %all-to-all-done.3 = bf16[128,10,128]{2,1,0:T(8,128)(2,1)S(1)} async-done(((bf16[128,10,128]{2,1,0:T(8,128)(2,1)}), bf16[128,10,128]{2,1,0:T(8,128)(2,1)S(1)}, u32[]{:S(2)}, u32[]{:S(2)}) %all-to-all-start.3) | async-done | bytes 327712 | tf_op jit(solution)/shard_map/all_to_all | solution.py:394
  170.5 0.1 convert_reduce_fusion
  170.7 0.6 copy.17
  (26 shorter events, 0.1 us)
Async XLA Ops:
  0.6 28.3 %copy-start.1 = (bf16[2,256,1280]{2,1,0:T(8,128)(2,1)S(1)}, bf16[2,256,1280]{2,1,0:T(8,128)(2,1)}, u32[]{:S(2)}) copy-start(bf16[2,256,1280]{2,1,0:T(8,128)(2,1)} %d_out.3) | copy-start | bytes 3932164
  0.6 28.3 %copy-start = (bf16[2,256,1280]{2,1,0:T(8,128)(2,1)S(1)}, bf16[2,256,1280]{2,1,0:T(8,128)(2,1)}, u32[]{:S(2)}) copy-start(bf16[2,256,1280]{2,1,0:T(8,128)(2,1)} %tokens.3) | copy-start | bytes 3932164
  0.7 53.8 %collective-permute-start.1 = (bf16[4,1280,640]{2,1,0:T(8,128)(2,1)}, bf16[4,1280,640]{2,1,0:T(8,128)(2,1)}, u32[]{:S(2)}, u32[]{:S(2)}) collective-permute-start(bf16[4,1280,640]{2,1,0:T(8,128)(2,1)} %refs_4_.3), channel_id=1, source_target_pairs={{0,32},{32,0},{1,33},{33,1},{2,34},{34,2},{3,35},{35,3},{4,36},{36... | collective-permute-start | bytes 19660808 | tf_op jit(solution)/shard_map/ppermute | solution.py:314
  2.2 52.3 %collective-permute-start = (bf16[4,640,1280]{2,1,0:T(8,128)(2,1)}, bf16[4,640,1280]{2,1,0:T(8,128)(2,1)}, u32[]{:S(2)}, u32[]{:S(2)}) collective-permute-start(bf16[4,640,1280]{2,1,0:T(8,128)(2,1)} %refs_5_.3), channel_id=1, source_target_pairs={{0,32},{32,0},{1,33},{33,1},{2,34},{34,2},{3,35},{35,3},{4,36},{36... | collective-permute-start | bytes 19660808 | tf_op jit(solution)/shard_map/ppermute | solution.py:315
  3.8 24.6 %all-to-all-start = ((bf16[128,10,128]{2,1,0:T(8,128)(2,1)}), bf16[128,10,128]{2,1,0:T(8,128)(2,1)S(1)}, u32[]{:S(2)}, u32[]{:S(2)}) async-start(bf16[128,10,128]{2,1,0:T(8,128)(2,1)} %broadcast_in_dim.8), calls=%async_computation | async-start | bytes 1048576 | tf_op jit(solution)/shard_map/all_to_all | solution.py:22
  55.7 9.7 %collective-permute-start.3 = (bf16[2,64,1280]{2,1,0:T(8,128)(2,1)S(1)}, bf16[2,64,1280]{2,1,0:T(8,128)(2,1)}, u32[]{:S(2)}, u32[]{:S(2)}) collective-permute-start(bf16[2,64,1280]{2,1,0:T(8,128)(2,1)S(1)} %get-tuple-element.50), channel_id=1, source_target_pairs={{0,65},{1,64},{64,1},{65,0},{2,67},{3,66},{66,3},{67,2},{4,69},{5,... | collective-permute-start | bytes 983048 | tf_op jit(solution)/shard_map/ppermute | solution.py:336
  56.6 8.8 %collective-permute-start.2 = (bf16[2,64,1280]{2,1,0:T(8,128)(2,1)S(1)}, bf16[2,64,1280]{2,1,0:T(8,128)(2,1)S(1)}, u32[]{:S(2)}, u32[]{:S(2)}) collective-permute-start(bf16[2,64,1280]{2,1,0:T(8,128)(2,1)S(1)} %get-tuple-element.49.refs_0_), channel_id=1, source_target_pairs={{0,64},{64,0},{1,65},{65,1},{2,66},{66,2},{3,67},{67,3},{4,68},{68... | collective-permute-start | bytes 983048 | tf_op jit(solution)/shard_map/ppermute | solution.py:335
  56.7 0.7 copy-start.5
  65.4 0.7 copy-start.7
  66.1 7.8 %collective-permute-start.4 = (bf16[2,64,1280]{2,1,0:T(8,128)(2,1)}, bf16[2,64,1280]{2,1,0:T(8,128)(2,1)}, u32[]{:S(2)}, u32[]{:S(2)}) collective-permute-start(bf16[2,64,1280]{2,1,0:T(8,128)(2,1)} %collective-permute-done.3.refs_2_), channel_id=1, source_target_pairs={{0,64},{64,0},{1,65},{65,1},{2,66},{66,2},{3,67},{67,3},{4,68},{68... | collective-permute-start | bytes 983048 | tf_op jit(solution)/shard_map/ppermute | solution.py:338
  66.1 9.0 %collective-permute-start.7 = (bf16[2,64,1280]{2,1,0:T(8,128)(2,1)}, bf16[2,64,1280]{2,1,0:T(8,128)(2,1)}, u32[]{:S(2)}, u32[]{:S(2)}) collective-permute-start(bf16[2,64,1280]{2,1,0:T(8,128)(2,1)} %get-tuple-element.57), channel_id=1, source_target_pairs={{0,65},{1,64},{64,1},{65,0},{2,67},{3,66},{66,3},{67,2},{4,69},{5,... | collective-permute-start | bytes 983048 | tf_op jit(solution)/shard_map/ppermute | solution.py:340
  73.9 13.6 %collective-permute-start.6 = (bf16[2,64,1280]{2,1,0:T(8,128)(2,1)S(1)}, bf16[2,64,1280]{2,1,0:T(8,128)(2,1)S(1)}, u32[]{:S(2)}, u32[]{:S(2)}) collective-permute-start(bf16[2,64,1280]{2,1,0:T(8,128)(2,1)S(1)} %get-tuple-element.55.refs_0_), channel_id=1, source_target_pairs={{0,64},{64,0},{1,65},{65,1},{2,66},{66,2},{3,67},{67,3},{4,68},{68... | collective-permute-start | bytes 983048 | tf_op jit(solution)/shard_map/ppermute | solution.py:342
  75.1 12.3 %collective-permute-start.8 = (bf16[2,64,1280]{2,1,0:T(8,128)(2,1)}, bf16[2,64,1280]{2,1,0:T(8,128)(2,1)S(1)}, u32[]{:S(2)}, u32[]{:S(2)}) collective-permute-start(bf16[2,64,1280]{2,1,0:T(8,128)(2,1)} %collective-permute-done.7.refs_2_), channel_id=1, source_target_pairs={{0,64},{64,0},{1,65},{65,1},{2,66},{66,2},{3,67},{67,3},{4,68},{68... | collective-permute-start | bytes 983048 | tf_op jit(solution)/shard_map/ppermute | solution.py:343
  75.4 1.0 copy-start.6
  76.4 1.0 copy-start.8
  85.5 10.7 %collective-permute-start.9 = (bf16[2,64,1280]{2,1,0:T(8,128)(2,1)S(1)}, bf16[2,64,1280]{2,1,0:T(8,128)(2,1)S(1)}, u32[]{:S(2)}, u32[]{:S(2)}) collective-permute-start(bf16[2,64,1280]{2,1,0:T(8,128)(2,1)S(1)} %get-tuple-element.63), channel_id=1, source_target_pairs={{0,64},{64,0},{1,65},{65,1},{2,66},{66,2},{3,67},{67,3},{4,68},{68... | collective-permute-start | bytes 983048 | tf_op jit(solution)/shard_map/ppermute | solution.py:354
  95.6 6.0 %collective-permute-start.10 = (bf16[2,64,1280]{2,1,0:T(8,128)(2,1)S(1)}, bf16[2,64,1280]{2,1,0:T(8,128)(2,1)S(1)}, u32[]{:S(2)}, u32[]{:S(2)}) collective-permute-start(bf16[2,64,1280]{2,1,0:T(8,128)(2,1)S(1)} %get-tuple-element.69), channel_id=1, source_target_pairs={{0,64},{64,0},{1,65},{65,1},{2,66},{66,2},{3,67},{67,3},{4,68},{68... | collective-permute-start | bytes 983048 | tf_op jit(solution)/shard_map/ppermute | solution.py:356
  96.3 19.8 %collective-permute-start.11 = (bf16[2,64,1280]{2,1,0:T(8,128)(2,1)S(1)}, bf16[2,64,1280]{2,1,0:T(8,128)(2,1)S(1)}, u32[]{:S(2)}, u32[]{:S(2)}) collective-permute-start(bf16[2,64,1280]{2,1,0:T(8,128)(2,1)S(1)} %shard_map.80), channel_id=1, source_target_pairs={{0,65},{1,64},{64,1},{65,0},{2,67},{3,66},{66,3},{67,2},{4,69},{5,... | collective-permute-start | bytes 983048 | tf_op jit(solution)/shard_map/ppermute | solution.py:360
  101.6 14.6 %collective-permute-start.12 = (bf16[2,64,1280]{2,1,0:T(8,128)(2,1)S(1)}, bf16[2,64,1280]{2,1,0:T(8,128)(2,1)S(1)}, u32[]{:S(2)}, u32[]{:S(2)}) collective-permute-start(bf16[2,64,1280]{2,1,0:T(8,128)(2,1)S(1)} %shard_map.82), channel_id=1, source_target_pairs={{0,65},{1,64},{64,1},{65,0},{2,67},{3,66},{66,3},{67,2},{4,69},{5,... | collective-permute-start | bytes 983048 | tf_op jit(solution)/shard_map/ppermute | solution.py:365
  102.5 13.8 %collective-permute-start.5 = (bf16[2,64,1280]{2,1,0:T(8,128)(2,1)S(1)}, bf16[2,64,1280]{2,1,0:T(8,128)(2,1)S(1)}, u32[]{:S(2)}, u32[]{:S(2)}) collective-permute-start(bf16[2,64,1280]{2,1,0:T(8,128)(2,1)S(1)} %get-tuple-element.53), channel_id=1, source_target_pairs={{0,64},{64,0},{1,65},{65,1},{2,66},{66,2},{3,67},{67,3},{4,68},{68... | collective-permute-start | bytes 983048 | tf_op jit(solution)/shard_map/ppermute | solution.py:355
  102.5 13.8 %collective-permute-start.13 = (bf16[2,64,1280]{2,1,0:T(8,128)(2,1)S(1)}, bf16[2,64,1280]{2,1,0:T(8,128)(2,1)S(1)}, u32[]{:S(2)}, u32[]{:S(2)}) collective-permute-start(bf16[2,64,1280]{2,1,0:T(8,128)(2,1)S(1)} %get-tuple-element.77), channel_id=1, source_target_pairs={{0,64},{64,0},{1,65},{65,1},{2,66},{66,2},{3,67},{67,3},{4,68},{68... | collective-permute-start | bytes 983048 | tf_op jit(solution)/shard_map/ppermute | solution.py:357
  103.9 52.7 %collective-permute-start.14 = (bf16[640,1280]{1,0:T(8,128)(2,1)}, bf16[640,1280]{1,0:T(8,128)(2,1)}, u32[]{:S(2)}, u32[]{:S(2)}) collective-permute-start(bf16[640,1280]{1,0:T(8,128)(2,1)} %get-tuple-element.68), channel_id=1, source_target_pairs={{0,32},{32,0},{1,33},{33,1},{2,34},{34,2},{3,35},{35,3},{4,36},{36... | collective-permute-start | bytes 4915208 | tf_op jit(solution)/shard_map/ppermute | solution.py:369
  116.1 40.5 %collective-permute-start.15 = (bf16[640,1280]{1,0:T(8,128)(2,1)}, bf16[640,1280]{1,0:T(8,128)(2,1)}, u32[]{:S(2)}, u32[]{:S(2)}) collective-permute-start(bf16[640,1280]{1,0:T(8,128)(2,1)} %get-tuple-element.75), channel_id=1, source_target_pairs={{0,32},{32,0},{1,33},{33,1},{2,34},{34,2},{3,35},{35,3},{4,36},{36... | collective-permute-start | bytes 4915208 | tf_op jit(solution)/shard_map/ppermute | solution.py:370
  116.8 30.7 %copy-start.2 = (f32[2,256,128]{2,1,0:T(8,128)S(1)}, f32[2,256,128]{2,1,0:T(8,128)}, u32[]{:S(2)}) copy-start(f32[2,256,128]{2,1,0:T(8,128)} %get-tuple-element.45.dispatch) | copy-start | bytes 786436
  116.8 30.7 %copy-start.4 = (f32[2,256,128]{2,1,0:T(8,128)S(1)}, f32[2,256,128]{2,1,0:T(8,128)}, u32[]{:S(2)}) copy-start(f32[2,256,128]{2,1,0:T(8,128)} %get-tuple-element.79.combine) | copy-start | bytes 786436
  151.4 19.1 %all-to-all-start.3 = ((bf16[128,10,128]{2,1,0:T(8,128)(2,1)}), bf16[128,10,128]{2,1,0:T(8,128)(2,1)S(1)}, u32[]{:S(2)}, u32[]{:S(2)}) async-start(bf16[128,10,128]{2,1,0:T(8,128)(2,1)} %get-tuple-element.86), calls=%async_computation.3 | async-start | bytes 1048576 | tf_op jit(solution)/shard_map/all_to_all | solution.py:394
  156.6 3.3 %copy-start.3 = (bf16[256,1280]{1,0:T(8,128)(2,1)S(1)}, bf16[256,1280]{1,0:T(8,128)(2,1)}, u32[]{:S(2)}) copy-start(bf16[256,1280]{1,0:T(8,128)(2,1)} %get-tuple-element.85.slot_back) | copy-start | bytes 1966084

commit v5 on v4

--- a/solution.py
+++ b/solution.py
@@ -123,33 +123,54 @@
             part[index % 2, 32 * core : 32 * core + 32] = rows[32 * index : 32 * index + 32]
 
 
-def expert_kernel(chunk, core, *refs):
-    blocks, weights, refs = refs[:4], refs[4:8], refs[8:]
-    parts, (active, grads), (held_in, held_out, sems) = refs[:4], refs[4:6], refs[6:]
-    expert = 2 * core[0] + chunk
+def stage_kernel(core, near_in, near_out, far_in, far_out, held_in, held_out, sems):
     copies = []
-    for index, weight in enumerate(weights):
-        held = (held_in if index % 2 == 0 else held_out).at[index // 2]
-        copies.append(pltpu.make_async_copy(weight.at[expert], held, sems.at[index]))
+    for index, (weight, held) in enumerate(
+        [(near_in, held_in), (near_out, held_out), (far_in, held_in), (far_out, held_out)]
+    ):
+        source = weight.at[pl.ds(2 * core[0], 2)]
+        copies.append(pltpu.make_async_copy(source, held.at[index // 2], sems.at[index]))
     for copy in copies:
         copy.start()
+    for copy in copies:
+        copy.wait()
+
+
+def stage(core, near_in, near_out, far_in, far_out):
+    shards = [
+        pltpu.with_memory_space_constraint(shard, pltpu.HBM)
+        for shard in (near_in, near_out, far_in, far_out)
+    ]
+    shape = lambda shard: ((2, 2) + shard.shape[1:], shard.dtype, pltpu.VMEM)
+    return call(
+        stage_kernel,
+        [shape(near_in), shape(near_out)],
+        shards,
+        [core],
+        specs=[pl.BlockSpec(memory_space=pltpu.HBM)] * 4,
+        scratch_shapes=[pltpu.SemaphoreType.DMA((4,))],
+    )
+
+
+def expert_kernel(chunk, *refs):
+    blocks, (held_in, held_out), refs = refs[:4], refs[4:6], refs[6:]
+    parts, (active, grads) = refs[:4], refs[4:]
     rows = jnp.concatenate([block[0] for block in blocks], axis=0)
     grad = jnp.concatenate([block[1] for block in blocks], axis=0)
     grads[...] = grad
     out = back = None
     for quarter in range(2):
-        copies[2 * quarter].wait()
-        before = product(rows, held_in[quarter])
+        first, second = held_in[quarter, chunk], held_out[quarter, chunk]
+        before = product(rows, first)
         below = 0.5 + 0.5 * lax.erf(before * math.sqrt(0.5))
         bell = jnp.exp(-0.5 * before * before) * (1.0 / math.sqrt(2.0 * math.pi))
         slope = below + before * bell
         rounded = (before * below).astype(active.dtype)
         active[quarter] = rounded
-        copies[2 * quarter + 1].wait()
-        part = product(rounded, held_out[quarter])
+        part = product(rounded, second)
         out = part if out is None else out + part
-        rounded = (product(grad, held_out[quarter], 1, 1) * slope).astype(grad.dtype)
-        part = product(rounded, held_in[quarter], 1, 1)
+        rounded = (product(grad, second, 1, 1) * slope).astype(grad.dtype)
+        part = product(rounded, first, 1, 1)
         back = part if back is None else back + part
     for index, part in enumerate(parts):
         mine = slice(64 * index, 64 * index + 64)
@@ -157,24 +178,17 @@
         part[1] = back[mine].astype(part.dtype)
 
 
-def expert_call(chunk, core, blocks, weights):
+def expert_call(chunk, blocks, held):
     half = jnp.bfloat16
-    _, width, hidden = weights[0].shape
-    vmem = pl.BlockSpec(memory_space=pltpu.VMEM)
-    outs = [((2, 64, width), half)] * 4 + [((2, 256, hidden), half), ((256, width), half)]
+    width, hidden = held[0].shape[2:]
+    outs = [((2, 64, width), half, pltpu.VMEM)] * 4
+    outs += [((2, 256, hidden), half), ((256, width), half)]
+    held = [pltpu.with_memory_space_constraint(weight, pltpu.VMEM) for weight in held]
     return call(
         functools.partial(expert_kernel, chunk),
         outs,
-        list(blocks) + list(weights),
-        [core],
-        limit=28,
-        specs=[vmem] * 4 + [pl.BlockSpec(memory_space=pltpu.HBM)] * 4,
+        list(blocks) + held,
         cost=pl.CostEstimate(flops=8 * 10**9, bytes_accessed=24 * MIB, transcendentals=0),
-        scratch_shapes=[
-            pltpu.VMEM((2, width, hidden), half),
-            pltpu.VMEM((2, hidden, width), half),
-            pltpu.SemaphoreType.DMA((4,)),
-        ],
     )
 
 
@@ -320,7 +334,7 @@
     wire, dispatch, combine = call(
         functools.partial(front_kernel, score_scale),
         [((32, 16, width), half), weights + (pltpu.HBM,), weights + (pltpu.HBM,)],
-        [tokens, router_full, d_out],
+        [tokens, pltpu.with_memory_space_constraint(router_full, pltpu.VMEM), d_out],
         [high],
         out_specs=[vmem, hbm, hbm],
         scratch_shapes=[pltpu.VMEM(*weights)] * 2 + [pltpu.SemaphoreType.DMA((2,))],
@@ -328,29 +342,23 @@
     (wire,) = after(far_out, *after(far_in, exchange(wire)))
     own_0, other_0, own_1, other_1 = call(
         sort_kernel,
-        [((2, 64, width), half)] * 4,
+        [((2, 64, width), half, kind) for kind in (pltpu.HBM, pltpu.VMEM) * 2],
         [wire],
         cost=pl.CostEstimate(flops=10**6, bytes_accessed=40 * MIB, transcendentals=0),
     )
-    pair_0 = lax.ppermute(own_0, "zl", SWAP)
+    pair_0, pair_1 = (lax.ppermute(own, "zl", SWAP) for own in (own_0, own_1))
     cross_0 = lax.ppermute(other_0, ("zl", "zh"), CROSS)
-    (cross_0,) = after(pair_0, cross_0)
-    far_0 = lax.ppermute(cross_0, "zl", SWAP)
-    (other_1,) = after(cross_0, other_1)
     cross_1 = lax.ppermute(other_1, ("zl", "zh"), CROSS)
-    (own_1,) = after(far_0, own_1)
-    pair_1 = lax.ppermute(own_1, "zl", SWAP)
-    far_1 = lax.ppermute(cross_1, "zl", SWAP)
+    held = stage(core, *after(own_0, w_in, w_out, far_in, far_out))
+    (cross_0,) = after(held[0], *after(pair_0, cross_0))
+    (cross_1,) = after(pair_1, cross_1)
+    far_0, far_1 = (lax.ppermute(cross, "zl", SWAP) for cross in (cross_0, cross_1))
+    (far_0,) = after(cross_1, far_0)
     rows_0 = [own_0, pair_0, cross_0, far_0]
     rows_1 = [own_1, pair_1, cross_1, far_1]
-    shards = [
-        pltpu.with_memory_space_constraint(shard, pltpu.HBM)
-        for shard in (w_in, w_out, far_in, far_out)
-    ]
-
-    *parts_0, active_0, grads_0 = expert_call(0, core, rows_0, shards)
-    rows_1[1::2] = after(parts_0[0], *rows_1[1::2])
-    *parts_1, active_1, grads_1 = expert_call(1, core, rows_1, shards)
+    *parts_0, active_0, grads_0 = expert_call(0, rows_0, held)
+    rows_1[3:] = after(parts_0[0], *rows_1[3:])
+    *parts_1, active_1, grads_1 = expert_call(1, rows_1, held)
     far_0 = lax.ppermute(parts_0[3], "zl", SWAP)
     pair_0 = lax.ppermute(parts_0[1], "zl", SWAP)
     far_1 = lax.ppermute(parts_1[3], "zl", SWAP)
@@ -363,9 +371,10 @@
     (far_1,) = after(away_0, far_1)
     cross_1 = sum_of(parts_1[2], far_1)
     other_1 = lax.ppermute(cross_1, ("zl", "zh"), CROSS)
-    (active_1,) = after(cross_1, active_1)
+    (active_1,) = after(pair_0, *after(cross_1, active_1))
     whole, away_1 = weight_call(1, core, active_1, grads_1, whole)
     other_0, other_1 = after(away_1, other_0, other_1)
+    (away_0,) = after(away_1, away_0)
     came_0 = lax.ppermute(away_0, "core", SWAP)
     came_1 = lax.ppermute(away_1, "core", SWAP)
     wire = call(

time: 172 us -> 168 us (0.977)
  waiting for transfers between devices: 41 us -> 47.9 us
  blocking collectives: 54.3 us -> 49.7 us
  starting transfers between devices: 34.8 us -> 31 us
    ppermute x1, waiting for transfers between devices: 8 us -> 1.39 us  [body(): cross_0 = lax.ppermute(other_0, ('zl', 'zh'), CROSS)]
    ppermute x1, waiting for transfers between devices: 0.93 us -> 7.02 us  [body(): cross_1 = lax.ppermute(other_1, ('zl', 'zh'), CROSS)]
    ppermute x1, waiting for transfers between devices: 0.01 us -> 5.1 us  [body(): pair_0 = lax.ppermute(parts_0[1], 'zl', SWAP)]
    ppermute x1, starting transfers between devices: 9.7 us -> 4.88 us  [body(): came_0 = lax.ppermute(away_0, 'core', SWAP)]
    all_to_all x2, blocking collectives: 54.3 us -> 49.7 us  [exchange(): lax.all_to_all(blocks, PLANE, split_axis=0, concat_axis=0, tiled=True)]
    unnamed x19 -> x17, local copies, waits for them, and re-layouts: 4.03 us -> 1.35 us
    pallas_call x12 -> x13, Pallas kernels: 34 us -> 33 us  [call(): pl.pallas_call(kernel, in_specs=[pl.BlockSpec(memory_space=pltpu.SMEM)] *...]
  transfers between devices with their start and end apart: 18 -> 18, of which waited for: 7 -> 9; matrix products, arithmetic and copies ran while one was open for 1% -> 2% of each run, Pallas kernels for 19% -> 19%
where the time goes in v5:
time: 168 us
  blocking collectives  49.7 us (30%)
  waiting for transfers between devices  47.9 us (29%)
  Pallas kernels  33 us (20%)
  starting transfers between devices  31 us (18%)
  local copies, waits for them, and re-layouts  4.42 us (3%)
    all_to_all x2, blocking collectives, exchange(): lax.all_to_all(blocks, PLANE, split_axis=0, concat_axis=0, tiled=True)  49.7 us
    pallas_call x13, Pallas kernels, call(): pl.pallas_call(kernel, in_specs=[pl.BlockSpec(memory_space=pltpu.SMEM)] *...  33 us
    all_to_all x1, waiting for transfers between devices, gather_router(): lax.all_to_all(spread, ALL, split_axis=0, concat_axis=0, tiled=True)  13.9 us
    all_to_all x1, starting transfers between devices, gather_router(): lax.all_to_all(spread, ALL, split_axis=0, concat_axis=0, tiled=True)  10.7 us
    all_to_all x1, waiting for transfers between devices, body(): lax.all_to_all(term, ALL, split_axis=0, concat_axis=0, tiled=True)  8.72 us
    ppermute x2, waiting for transfers between devices, body(): lax.ppermute(cross, 'zl', SWAP)  7.79 us
    ppermute x1, waiting for transfers between devices, body(): cross_1 = lax.ppermute(other_1, ('zl', 'zh'), CROSS)  7.02 us
    ppermute x1, waiting for transfers between devices, body(): pair_0 = lax.ppermute(parts_0[1], 'zl', SWAP)  5.1 us
  transfers between devices with their start and end apart: 18, of which 9 were waited for; matrix products, arithmetic and copies ran while one was open for 2% of the time, Pallas kernels for 19%

profile of v5, /device:TPU:1, one launch (start us, length us, event | category | flops | bytes accessed | tf_op | source)
XLA Modules:
  0.0 167.7 jit_solution(24155263259084015)
XLA Ops:
  0.7 1.5 collective-permute-start.1
  2.2 0.1 collective-permute-start
  2.2 0.7 reduce
  3.0 0.9 broadcast_in_dim.8
  3.8 10.7 %all-to-all-start = ((bf16[128,10,128]{2,1,0:T(8,128)(2,1)}), bf16[128,10,128]{2,1,0:T(8,128)(2,1)S(1)}, u32[]{:S(2)}, u32[]{:S(2)}) async-start(bf16[128,10,128]{2,1,0:T(8,128)(2,1)} %broadcast_in_dim.8), calls=%async_computation | async-start | bytes 1048576 | tf_op jit(solution)/shard_map/all_to_all | solution.py:22
  14.5 13.9 %all-to-all-done = bf16[128,10,128]{2,1,0:T(8,128)(2,1)S(1)} async-done(((bf16[128,10,128]{2,1,0:T(8,128)(2,1)}), bf16[128,10,128]{2,1,0:T(8,128)(2,1)S(1)}, u32[]{:S(2)}, u32[]{:S(2)}) %all-to-all-start) | async-done | bytes 327712 | tf_op jit(solution)/shard_map/all_to_all | solution.py:22
  28.4 1.1 copy.12
  29.5 1.1 copy.13.router
  30.6 1.9 %shard_map.76 = (bf16[32,16,1280]{2,1,0:T(8,128)(2,1)S(1)}, f32[2,256,128]{2,1,0:T(8,128)}, f32[2,256,128]{2,1,0:T(8,128)}) custom-call(s32[1]{0:T(128)} %bitcast.high, bf16[2,256,1280]{2,1,0:T(8,128)(2,1)S(1)} %copy-done, bf16[128,1280]{1,0:T(8,128)(2,1)S(1)} %copy.13.router, bf16[2,256,1280]{2,1,0:T(8,128)(2,1)S(1)} %copy-done.1), custom_call_target="tpu_custom_call" | custom-call | tf_op jit(solution)/shard_map/pallas_call | solution.py:78
  32.5 23.6 %all_to_all.20.wire = bf16[32,16,1280]{2,1,0:T(8,128)(2,1)S(1)} all-to-all(bf16[32,16,1280]{2,1,0:T(8,128)(2,1)S(1)} %get-tuple-element.54), channel_id=1, replica_groups=mesh['zl'=2,'core'=2,'xy'=16,'zh'=2] {'core','xy'}, dimensions={0} | all-to-all | bytes 2621440 | tf_op jit(solution)/shard_map/all_to_all | solution.py:26
  56.1 0.0 collective-permute-done.far_out
  56.1 1.4 shard_map.77
  57.5 0.7 copy-done.7
  58.2 0.9 collective-permute-start.3
  59.2 0.1 collective-permute-start.2
  59.2 1.7 %collective-permute-start.5 = (bf16[2,64,1280]{2,1,0:T(8,128)(2,1)}, bf16[2,64,1280]{2,1,0:T(8,128)(2,1)S(1)}, u32[]{:S(2)}, u32[]{:S(2)}) collective-permute-start(bf16[2,64,1280]{2,1,0:T(8,128)(2,1)} %copy-done.7), channel_id=1, source_target_pairs={{0,65},{1,64},{64,1},{65,0},{2,67},{3,66},{66,3},{67,2},{4,69},{5,... | collective-permute-start | bytes 983048 | tf_op jit(solution)/shard_map/ppermute | solution.py:351
  60.9 0.9 collective-permute-start.4
  61.8 4.9 %shard_map.78 = (bf16[2,2,1280,640]{3,2,1,0:T(8,128)(2,1)S(1)}, bf16[2,2,640,1280]{3,2,1,0:T(8,128)(2,1)S(1)}) custom-call(s32[1]{0:T(128)} %bitcast.2.core, bf16[4,1280,640]{2,1,0:T(8,128)(2,1)} %near_in, bf16[4,640,1280]{2,1,0:T(8,128)(2,1)} %near_out, bf16[4,1280,640]{2,1,0:T(8,128)(2,1)} %collective-permute-done.1.far_in, ...), custom_call_target="tpu_custom_call" | custom-call | tf_op jit(solution)/shard_map/pallas_call | solution.py:78
  66.7 1.4 collective-permute-done.3.refs_2_
  68.1 7.0 %collective-permute-done.5.refs_2_ = bf16[2,64,1280]{2,1,0:T(8,128)(2,1)S(1)} collective-permute-done((bf16[2,64,1280]{2,1,0:T(8,128)(2,1)}, bf16[2,64,1280]{2,1,0:T(8,128)(2,1)S(1)}, u32[]{:S(2)}, u32[]{:S(2)}) %collective-permute-start.5) | collective-permute-done | bytes 327712 | tf_op jit(solution)/shard_map/ppermute | solution.py:351
  75.1 6.4 %collective-permute-done.6.refs_3_ = bf16[2,64,1280]{2,1,0:T(8,128)(2,1)S(1)} collective-permute-done((bf16[2,64,1280]{2,1,0:T(8,128)(2,1)S(1)}, bf16[2,64,1280]{2,1,0:T(8,128)(2,1)S(1)}, u32[]{:S(2)}, u32[]{:S(2)}) %collective-permute-start.6) | collective-permute-done | bytes 327712 | tf_op jit(solution)/shard_map/ppermute | solution.py:355
  81.5 5.6 %shard_map.79 = (bf16[2,64,1280]{2,1,0:T(8,128)(2,1)S(1)}, bf16[2,64,1280]{2,1,0:T(8,128)(2,1)S(1)}, bf16[2,64,1280]{2,1,0:T(8,128)(2,1)S(1)}, bf16[2,64,1280]{2...) custom-call(bf16[2,64,1280]{2,1,0:T(8,128)(2,1)S(1)} %copy-done.6, ...), custom_call_target="tpu_custom_call" | custom-call | flops 8000000000 | bytes 25165824 | tf_op jit(solution)/shard_map/pallas_call | solution.py:78
  87.1 1.4 collective-permute-done.8.refs_3_
  88.5 0.1 collective-permute-start.9
  88.6 4.6 %shard_map.80 = (bf16[2,64,1280]{2,1,0:T(8,128)(2,1)S(1)}, bf16[2,64,1280]{2,1,0:T(8,128)(2,1)S(1)}, bf16[2,64,1280]{2,1,0:T(8,128)(2,1)S(1)}, bf16[2,64,1280]{2...) custom-call(bf16[2,64,1280]{2,1,0:T(8,128)(2,1)S(1)} %copy-done.5, ...), custom_call_target="tpu_custom_call" | custom-call | flops 8000000000 | bytes 25165824 | tf_op jit(solution)/shard_map/pallas_call | solution.py:78
  93.2 1.5 collective-permute-start.10
  94.7 0.1 collective-permute-start.7
  94.8 0.4 collective-permute-done.9.right
  95.1 0.1 shard_map.81
  95.2 1.8 %collective-permute-start.11 = (bf16[2,64,1280]{2,1,0:T(8,128)(2,1)S(1)}, bf16[2,64,1280]{2,1,0:T(8,128)(2,1)S(1)}, u32[]{:S(2)}, u32[]{:S(2)}) collective-permute-start(bf16[2,64,1280]{2,1,0:T(8,128)(2,1)S(1)} %shard_map.81), channel_id=1, source_target_pairs={{0,65},{1,64},{64,1},{65,0},{2,67},{3,66},{66,3},{67,2},{4,69},{5,... | collective-permute-start | bytes 983048 | tf_op jit(solution)/shard_map/ppermute | solution.py:368
  97.0 2.4 %shard_map.82 = (bf16[4,640,1280]{2,1,0:T(8,128)(2,1)}, bf16[640,1280]{1,0:T(8,128)(2,1)}) custom-call(s32[1]{0:T(128)} %bitcast.2.core, bf16[2,256,640]{2,1,0:T(8,128)(2,1)S(1)} %get-tuple-element.80.active, bf16[256,1280]{1,0:T(8,128)(2,1)S(1)} %get-tuple-element.81.grads), custom_call_target="tpu_custom_call" | custom-call | tf_op jit(solution)/shard_map/pallas_call | solution.py:78
  99.5 3.6 %collective-permute-done.10.right = bf16[2,64,1280]{2,1,0:T(8,128)(2,1)S(1)} collective-permute-done((bf16[2,64,1280]{2,1,0:T(8,128)(2,1)S(1)}, bf16[2,64,1280]{2,1,0:T(8,128)(2,1)S(1)}, u32[]{:S(2)}, u32[]{:S(2)}) %collective-permute-start.10) | collective-permute-done | bytes 327712 | tf_op jit(solution)/shard_map/ppermute | solution.py:364
  103.1 0.1 shard_map.83
  103.1 1.8 %collective-permute-start.12 = (bf16[2,64,1280]{2,1,0:T(8,128)(2,1)S(1)}, bf16[2,64,1280]{2,1,0:T(8,128)(2,1)S(1)}, u32[]{:S(2)}, u32[]{:S(2)}) collective-permute-start(bf16[2,64,1280]{2,1,0:T(8,128)(2,1)S(1)} %shard_map.83), channel_id=1, source_target_pairs={{0,65},{1,64},{64,1},{65,0},{2,67},{3,66},{66,3},{67,2},{4,69},{5,... | collective-permute-start | bytes 983048 | tf_op jit(solution)/shard_map/ppermute | solution.py:373
  105.0 5.1 %collective-permute-done.7.refs_1_ = bf16[2,64,1280]{2,1,0:T(8,128)(2,1)S(1)} collective-permute-done((bf16[2,64,1280]{2,1,0:T(8,128)(2,1)S(1)}, bf16[2,64,1280]{2,1,0:T(8,128)(2,1)S(1)}, u32[]{:S(2)}, u32[]{:S(2)}) %collective-permute-start.7) | collective-permute-done | bytes 327712 | tf_op jit(solution)/shard_map/ppermute | solution.py:363
  110.1 2.5 %shard_map.84 = (bf16[4,640,1280]{2,1,0:T(8,128)(2,1)}, bf16[640,1280]{1,0:T(8,128)(2,1)}) custom-call(s32[1]{0:T(128)} %bitcast.2.core, bf16[2,256,640]{2,1,0:T(8,128)(2,1)S(1)} %get-tuple-element.87.active, bf16[256,1280]{1,0:T(8,128)(2,1)S(1)} %get-tuple-element.88.grads, ...), custom_call_target="tpu_custom_call", output_to_operand_aliasing={{0}: (3, {})} | custom-call | tf_op jit(solution)/shard_map/pallas_call | solution.py:78
  112.6 4.9 %collective-permute-start.14 = (bf16[640,1280]{1,0:T(8,128)(2,1)}, bf16[640,1280]{1,0:T(8,128)(2,1)}, u32[]{:S(2)}, u32[]{:S(2)}) collective-permute-start(bf16[640,1280]{1,0:T(8,128)(2,1)} %get-tuple-element.96), channel_id=1, source_target_pairs={{0,32},{32,0},{1,33},{33,1},{2,34},{34,2},{3,35},{35,3},{4,36},{36... | collective-permute-start | bytes 4915208 | tf_op jit(solution)/shard_map/ppermute | solution.py:378
  117.4 0.1 collective-permute-start.15
  117.5 0.6 shard_map.85
  118.1 26.1 %all_to_all.21.wire = bf16[32,16,1280]{2,1,0:T(8,128)(2,1)S(1)} all-to-all(bf16[32,16,1280]{2,1,0:T(8,128)(2,1)S(1)} %shard_map.85), channel_id=1, replica_groups=mesh['zl'=2,'core'=2,'xy'=16,'zh'=2] {'core','xy'}, dimensions={0} | all-to-all | bytes 2621440 | tf_op jit(solution)/shard_map/all_to_all | solution.py:26
  144.3 3.9 %shard_map.86 = (bf16[2,256,128]{2,1,0:T(8,128)(2,1)S(1)}, bf16[256,1280]{1,0:T(8,128)(2,1)}, bf16[128,10,128]{2,1,0:T(8,128)(2,1)}) custom-call(s32[1]{0:T(128)} %bitcast.high, bf16[32,16,1280]{2,1,0:T(8,128)(2,1)S(1)} %all_to_all.21.wire, bf16[2,256,1280]{2,1,0:T(8,128)(2,1)S(1)} %copy-done, bf16[2,256,1280]{2,1,0:T(8,128)(2,1)S(1)} %copy-done.1, ...), custom_call_target="tpu_custom_call" | custom-call | tf_op jit(solution)/shard_map/pallas_call | solution.py:78
  148.2 4.9 %all-to-all-start.3 = ((bf16[128,10,128]{2,1,0:T(8,128)(2,1)}), bf16[128,10,128]{2,1,0:T(8,128)(2,1)S(1)}, u32[]{:S(2)}, u32[]{:S(2)}) async-start(bf16[128,10,128]{2,1,0:T(8,128)(2,1)} %get-tuple-element.102), calls=%async_computation.3 | async-start | bytes 1048576 | tf_op jit(solution)/shard_map/all_to_all | solution.py:403
  153.1 0.0 copy-start.3
  153.1 3.2 %shard_map.87 = bf16[4,640,1280]{2,1,0:T(8,128)(2,1)} custom-call(s32[1]{0:T(128)} %bitcast.2.core, bf16[640,1280]{1,0:T(8,128)(2,1)} %collective-permute-done.14.came_0, bf16[640,1280]{1,0:T(8,128)(2,1)} %collective-permute-done.15.came_1, bf16[4,640,1280]{2,1,0:T(8,128)(2,1)} %get-tuple-element.99._), custom_call_target="tpu_custom_call", output_to_operand_aliasing={{}: (3, {})} | custom-call | tf_op jit(solution)/shard_map/pallas_call | solution.py:78
  156.4 1.9 %shard_map.88 = bf16[2,256,1280]{2,1,0:T(8,128)(2,1)} custom-call(f32[2,256,128]{2,1,0:T(8,128)S(1)} %copy-done.2, bf16[2,256,128]{2,1,0:T(8,128)(2,1)S(1)} %get-tuple-element.95.logit_grad, bf16[256,1280]{1,0:T(8,128)(2,1)S(1)} %copy-done.3, bf16[128,1280]{1,0:T(8,128)(2,1)S(1)} %copy.13.router), custom_call_target="tpu_custom_call" | custom-call | tf_op jit(solution)/shard_map/pallas_call | solution.py:78
  158.3 8.7 %all-to-all-done.3 = bf16[128,10,128]{2,1,0:T(8,128)(2,1)S(1)} async-done(((bf16[128,10,128]{2,1,0:T(8,128)(2,1)}), bf16[128,10,128]{2,1,0:T(8,128)(2,1)S(1)}, u32[]{:S(2)}, u32[]{:S(2)}) %all-to-all-start.3) | async-done | bytes 327712 | tf_op jit(solution)/shard_map/all_to_all | solution.py:403
  167.0 0.1 convert_reduce_fusion
  167.1 0.6 copy.17
  (25 shorter events, 0.1 us)
Async XLA Ops:
  0.6 30.0 %copy-start.1 = (bf16[2,256,1280]{2,1,0:T(8,128)(2,1)S(1)}, bf16[2,256,1280]{2,1,0:T(8,128)(2,1)}, u32[]{:S(2)}) copy-start(bf16[2,256,1280]{2,1,0:T(8,128)(2,1)} %d_out.3) | copy-start | bytes 3932164
  0.6 30.0 %copy-start = (bf16[2,256,1280]{2,1,0:T(8,128)(2,1)S(1)}, bf16[2,256,1280]{2,1,0:T(8,128)(2,1)}, u32[]{:S(2)}) copy-start(bf16[2,256,1280]{2,1,0:T(8,128)(2,1)} %tokens.3) | copy-start | bytes 3932164
  0.7 55.5 %collective-permute-start.1 = (bf16[4,1280,640]{2,1,0:T(8,128)(2,1)}, bf16[4,1280,640]{2,1,0:T(8,128)(2,1)}, u32[]{:S(2)}, u32[]{:S(2)}) collective-permute-start(bf16[4,1280,640]{2,1,0:T(8,128)(2,1)} %near_in), channel_id=1, source_target_pairs={{0,32},{32,0},{1,33},{33,1},{2,34},{34,2},{3,35},{35,3},{4,36},{36... | collective-permute-start | bytes 19660808 | tf_op jit(solution)/shard_map/ppermute | solution.py:328
  2.2 54.0 %collective-permute-start = (bf16[4,640,1280]{2,1,0:T(8,128)(2,1)}, bf16[4,640,1280]{2,1,0:T(8,128)(2,1)}, u32[]{:S(2)}, u32[]{:S(2)}) collective-permute-start(bf16[4,640,1280]{2,1,0:T(8,128)(2,1)} %near_out), channel_id=1, source_target_pairs={{0,32},{32,0},{1,33},{33,1},{2,34},{34,2},{3,35},{35,3},{4,36},{36... | collective-permute-start | bytes 19660808 | tf_op jit(solution)/shard_map/ppermute | solution.py:329
  3.8 24.6 %all-to-all-start = ((bf16[128,10,128]{2,1,0:T(8,128)(2,1)}), bf16[128,10,128]{2,1,0:T(8,128)(2,1)S(1)}, u32[]{:S(2)}, u32[]{:S(2)}) async-start(bf16[128,10,128]{2,1,0:T(8,128)(2,1)} %broadcast_in_dim.8), calls=%async_computation | async-start | bytes 1048576 | tf_op jit(solution)/shard_map/all_to_all | solution.py:22
  57.5 0.7 copy-start.7
  58.2 9.8 %collective-permute-start.3 = (bf16[2,64,1280]{2,1,0:T(8,128)(2,1)}, bf16[2,64,1280]{2,1,0:T(8,128)(2,1)S(1)}, u32[]{:S(2)}, u32[]{:S(2)}) collective-permute-start(bf16[2,64,1280]{2,1,0:T(8,128)(2,1)} %get-tuple-element.63), channel_id=1, source_target_pairs={{0,65},{1,64},{64,1},{65,0},{2,67},{3,66},{66,3},{67,2},{4,69},{5,... | collective-permute-start | bytes 983048 | tf_op jit(solution)/shard_map/ppermute | solution.py:350
  59.2 8.9 %collective-permute-start.2 = (bf16[2,64,1280]{2,1,0:T(8,128)(2,1)}, bf16[2,64,1280]{2,1,0:T(8,128)(2,1)}, u32[]{:S(2)}, u32[]{:S(2)}) collective-permute-start(bf16[2,64,1280]{2,1,0:T(8,128)(2,1)} %get-tuple-element.57.refs_0_), channel_id=1, source_target_pairs={{0,64},{64,0},{1,65},{65,1},{2,66},{66,2},{3,67},{67,3},{4,68},{68... | collective-permute-start | bytes 983048 | tf_op jit(solution)/shard_map/ppermute | solution.py:349
  59.2 15.9 %collective-permute-start.5 = (bf16[2,64,1280]{2,1,0:T(8,128)(2,1)}, bf16[2,64,1280]{2,1,0:T(8,128)(2,1)S(1)}, u32[]{:S(2)}, u32[]{:S(2)}) collective-permute-start(bf16[2,64,1280]{2,1,0:T(8,128)(2,1)} %copy-done.7), channel_id=1, source_target_pairs={{0,65},{1,64},{64,1},{65,0},{2,67},{3,66},{66,3},{67,2},{4,69},{5,... | collective-permute-start | bytes 983048 | tf_op jit(solution)/shard_map/ppermute | solution.py:351
  60.9 14.1 %collective-permute-start.4 = (bf16[2,64,1280]{2,1,0:T(8,128)(2,1)}, bf16[2,64,1280]{2,1,0:T(8,128)(2,1)S(1)}, u32[]{:S(2)}, u32[]{:S(2)}) collective-permute-start(bf16[2,64,1280]{2,1,0:T(8,128)(2,1)} %get-tuple-element.66.refs_0_), channel_id=1, source_target_pairs={{0,64},{64,0},{1,65},{65,1},{2,66},{66,2},{3,67},{67,3},{4,68},{68... | collective-permute-start | bytes 983048 | tf_op jit(solution)/shard_map/ppermute | solution.py:349
  61.8 19.7 %copy-start.6 = (bf16[2,64,1280]{2,1,0:T(8,128)(2,1)S(1)}, bf16[2,64,1280]{2,1,0:T(8,128)(2,1)}, u32[]{:S(2)}) copy-start(bf16[2,64,1280]{2,1,0:T(8,128)(2,1)} %get-tuple-element.57.refs_0_) | copy-start | bytes 983044
  68.1 13.4 %collective-permute-start.6 = (bf16[2,64,1280]{2,1,0:T(8,128)(2,1)S(1)}, bf16[2,64,1280]{2,1,0:T(8,128)(2,1)S(1)}, u32[]{:S(2)}, u32[]{:S(2)}) collective-permute-start(bf16[2,64,1280]{2,1,0:T(8,128)(2,1)S(1)} %collective-permute-done.3.refs_2_), channel_id=1, source_target_pairs={{0,64},{64,0},{1,65},{65,1},{2,66},{66,2},{3,67},{67,3},{4,68},{68... | collective-permute-start | bytes 983048 | tf_op jit(solution)/shard_map/ppermute | solution.py:355
  75.1 13.4 %collective-permute-start.8 = (bf16[2,64,1280]{2,1,0:T(8,128)(2,1)S(1)}, bf16[2,64,1280]{2,1,0:T(8,128)(2,1)S(1)}, u32[]{:S(2)}, u32[]{:S(2)}) collective-permute-start(bf16[2,64,1280]{2,1,0:T(8,128)(2,1)S(1)} %collective-permute-done.5.refs_2_), channel_id=1, source_target_pairs={{0,64},{64,0},{1,65},{65,1},{2,66},{66,2},{3,67},{67,3},{4,68},{68... | collective-permute-start | bytes 983048 | tf_op jit(solution)/shard_map/ppermute | solution.py:355
  81.5 7.1 %copy-start.5 = (bf16[2,64,1280]{2,1,0:T(8,128)(2,1)S(1)}, bf16[2,64,1280]{2,1,0:T(8,128)(2,1)}, u32[]{:S(2)}) copy-start(bf16[2,64,1280]{2,1,0:T(8,128)(2,1)} %get-tuple-element.66.refs_0_) | copy-start | bytes 983044
  88.5 6.6 %collective-permute-start.9 = (bf16[2,64,1280]{2,1,0:T(8,128)(2,1)S(1)}, bf16[2,64,1280]{2,1,0:T(8,128)(2,1)S(1)}, u32[]{:S(2)}, u32[]{:S(2)}) collective-permute-start(bf16[2,64,1280]{2,1,0:T(8,128)(2,1)S(1)} %get-tuple-element.77), channel_id=1, source_target_pairs={{0,64},{64,0},{1,65},{65,1},{2,66},{66,2},{3,67},{67,3},{4,68},{68... | collective-permute-start | bytes 983048 | tf_op jit(solution)/shard_map/ppermute | solution.py:362
  93.2 9.9 %collective-permute-start.10 = (bf16[2,64,1280]{2,1,0:T(8,128)(2,1)S(1)}, bf16[2,64,1280]{2,1,0:T(8,128)(2,1)S(1)}, u32[]{:S(2)}, u32[]{:S(2)}) collective-permute-start(bf16[2,64,1280]{2,1,0:T(8,128)(2,1)S(1)} %get-tuple-element.83), channel_id=1, source_target_pairs={{0,64},{64,0},{1,65},{65,1},{2,66},{66,2},{3,67},{67,3},{4,68},{68... | collective-permute-start | bytes 983048 | tf_op jit(solution)/shard_map/ppermute | solution.py:364
  94.7 15.4 %collective-permute-start.7 = (bf16[2,64,1280]{2,1,0:T(8,128)(2,1)S(1)}, bf16[2,64,1280]{2,1,0:T(8,128)(2,1)S(1)}, u32[]{:S(2)}, u32[]{:S(2)}) collective-permute-start(bf16[2,64,1280]{2,1,0:T(8,128)(2,1)S(1)} %get-tuple-element.72), channel_id=1, source_target_pairs={{0,64},{64,0},{1,65},{65,1},{2,66},{66,2},{3,67},{67,3},{4,68},{68... | collective-permute-start | bytes 983048 | tf_op jit(solution)/shard_map/ppermute | solution.py:363
  95.2 22.3 %collective-permute-start.11 = (bf16[2,64,1280]{2,1,0:T(8,128)(2,1)S(1)}, bf16[2,64,1280]{2,1,0:T(8,128)(2,1)S(1)}, u32[]{:S(2)}, u32[]{:S(2)}) collective-permute-start(bf16[2,64,1280]{2,1,0:T(8,128)(2,1)S(1)} %shard_map.81), channel_id=1, source_target_pairs={{0,65},{1,64},{64,1},{65,0},{2,67},{3,66},{66,3},{67,2},{4,69},{5,... | collective-permute-start | bytes 983048 | tf_op jit(solution)/shard_map/ppermute | solution.py:368
  103.1 14.4 %collective-permute-start.12 = (bf16[2,64,1280]{2,1,0:T(8,128)(2,1)S(1)}, bf16[2,64,1280]{2,1,0:T(8,128)(2,1)S(1)}, u32[]{:S(2)}, u32[]{:S(2)}) collective-permute-start(bf16[2,64,1280]{2,1,0:T(8,128)(2,1)S(1)} %shard_map.83), channel_id=1, source_target_pairs={{0,65},{1,64},{64,1},{65,0},{2,67},{3,66},{66,3},{67,2},{4,69},{5,... | collective-permute-start | bytes 983048 | tf_op jit(solution)/shard_map/ppermute | solution.py:373
  105.0 12.6 %collective-permute-start.13 = (bf16[2,64,1280]{2,1,0:T(8,128)(2,1)S(1)}, bf16[2,64,1280]{2,1,0:T(8,128)(2,1)S(1)}, u32[]{:S(2)}, u32[]{:S(2)}) collective-permute-start(bf16[2,64,1280]{2,1,0:T(8,128)(2,1)S(1)} %get-tuple-element.92), channel_id=1, source_target_pairs={{0,64},{64,0},{1,65},{65,1},{2,66},{66,2},{3,67},{67,3},{4,68},{68... | collective-permute-start | bytes 983048 | tf_op jit(solution)/shard_map/ppermute | solution.py:365
  112.6 40.5 %collective-permute-start.14 = (bf16[640,1280]{1,0:T(8,128)(2,1)}, bf16[640,1280]{1,0:T(8,128)(2,1)}, u32[]{:S(2)}, u32[]{:S(2)}) collective-permute-start(bf16[640,1280]{1,0:T(8,128)(2,1)} %get-tuple-element.96), channel_id=1, source_target_pairs={{0,32},{32,0},{1,33},{33,1},{2,34},{34,2},{3,35},{35,3},{4,36},{36... | collective-permute-start | bytes 4915208 | tf_op jit(solution)/shard_map/ppermute | solution.py:378
  117.4 35.7 %collective-permute-start.15 = (bf16[640,1280]{1,0:T(8,128)(2,1)}, bf16[640,1280]{1,0:T(8,128)(2,1)}, u32[]{:S(2)}, u32[]{:S(2)}) collective-permute-start(bf16[640,1280]{1,0:T(8,128)(2,1)} %get-tuple-element.90), channel_id=1, source_target_pairs={{0,32},{32,0},{1,33},{33,1},{2,34},{34,2},{3,35},{35,3},{4,36},{36... | collective-permute-start | bytes 4915208 | tf_op jit(solution)/shard_map/ppermute | solution.py:379
  118.1 26.1 %copy-start.2 = (f32[2,256,128]{2,1,0:T(8,128)S(1)}, f32[2,256,128]{2,1,0:T(8,128)}, u32[]{:S(2)}) copy-start(f32[2,256,128]{2,1,0:T(8,128)} %get-tuple-element.53.dispatch) | copy-start | bytes 786436
  118.1 26.1 %copy-start.4 = (f32[2,256,128]{2,1,0:T(8,128)S(1)}, f32[2,256,128]{2,1,0:T(8,128)}, u32[]{:S(2)}) copy-start(f32[2,256,128]{2,1,0:T(8,128)} %get-tuple-element.94.combine) | copy-start | bytes 786436
  148.2 18.8 %all-to-all-start.3 = ((bf16[128,10,128]{2,1,0:T(8,128)(2,1)}), bf16[128,10,128]{2,1,0:T(8,128)(2,1)S(1)}, u32[]{:S(2)}, u32[]{:S(2)}) async-start(bf16[128,10,128]{2,1,0:T(8,128)(2,1)} %get-tuple-element.102), calls=%async_computation.3 | async-start | bytes 1048576 | tf_op jit(solution)/shard_map/all_to_all | solution.py:403
  153.1 3.3 %copy-start.3 = (bf16[256,1280]{1,0:T(8,128)(2,1)S(1)}, bf16[256,1280]{1,0:T(8,128)(2,1)}, u32[]{:S(2)}) copy-start(bf16[256,1280]{1,0:T(8,128)(2,1)} %get-tuple-element.101.slot_back) | copy-start | bytes 1966084

commit v6 on v5

--- a/solution.py
+++ b/solution.py
@@ -14,12 +14,6 @@
 CROSS = [(index, index ^ 3) for index in range(4)]
 MIB = 2**20
 FREE = pl.CostEstimate(flops=0, bytes_accessed=0, transcendentals=0)
-
-
-def gather_router(router):
-    rows = lax.axis_size(ALL) * router.shape[0]
-    spread = jnp.broadcast_to(router.reshape(1, 10, 128), (rows, 10, 128))
-    return lax.all_to_all(spread, ALL, split_axis=0, concat_axis=0, tiled=True).reshape(rows, -1)
 
 
 def exchange(blocks):
@@ -86,9 +80,43 @@
     )(*scalars, *arrays)
 
 
+def widen_kernel(router, wide):
+    count, pieces, lanes = wide.shape
+    row = router[...].astype(jnp.float32)
+    row = [row[:, lanes * index : lanes * index + lanes] for index in range(pieces)]
+    row = jnp.concatenate(row, axis=0)[None]
+    wide[...] = jnp.broadcast_to(row, wide.shape).astype(wide.dtype)
+
+
+def gather_router(router):
+    wide = ((lax.axis_size(ALL), router.shape[1] // 128, 128), router.dtype, pltpu.HBM)
+    wide = call(widen_kernel, [wide], [router])[0]
+    return lax.all_to_all(wide, ALL, split_axis=0, concat_axis=0, tiled=True)
+
+
+def hold_kernel(source, held, sem):
+    copy = pltpu.make_async_copy(source, held, sem)
+    copy.start()
+    copy.wait()
+
+
+def hold(array):
+    return call(
+        hold_kernel,
+        [(array.shape, array.dtype, pltpu.VMEM)],
+        [pltpu.with_memory_space_constraint(array, pltpu.HBM)],
+        specs=[pl.BlockSpec(memory_space=pltpu.HBM)],
+        scratch_shapes=[pltpu.SemaphoreType.DMA(())],
+        cost=pl.CostEstimate(flops=10**6, bytes_accessed=8 * MIB, transcendentals=0),
+    )[0]
+
+
 def front_kernel(
-    score_scale, high, tokens, router, d_out, wire, dispatch, combine, held_0, held_1, sems
+    score_scale, high, tokens, received, d_out,
+    wire, dispatch, combine, router_full, held_0, held_1, router, sems,
 ):
+    for index in range(received.shape[1]):
+        router[:, 128 * index : 128 * index + 128] = received[:, index]
     slots, grads = [], []
     for image in range(2):
         logits = product(tokens[image], router[...], 1, 1) * score_scale
@@ -103,6 +131,7 @@
     copies = [
         pltpu.make_async_copy(held_0, dispatch, sems.at[0]),
         pltpu.make_async_copy(held_1, combine, sems.at[1]),
+        pltpu.make_async_copy(router, router_full, sems.at[2]),
     ]
     for copy in copies:
         copy.start()
@@ -327,22 +356,27 @@
     core = lax.axis_index("core").reshape(1).astype(jnp.int32)
     far_in = lax.ppermute(w_in, "core", SWAP)
     far_out = lax.ppermute(w_out, "core", SWAP)
-    router_full = gather_router(router)
+    received = gather_router(router)
+    held_tokens, held_out = hold(tokens), hold(d_out)
+    (received,) = after(held_out, *after(held_tokens, received))
+    rows = ((slots, width), half)
     weights = ((images, count, slots), jnp.float32)
     vmem = pl.BlockSpec(memory_space=pltpu.VMEM)
     hbm = pl.BlockSpec(memory_space=pltpu.HBM)
-    wire, dispatch, combine = call(
+    wire, dispatch, combine, router_full = call(
         functools.partial(front_kernel, score_scale),
-        [((32, 16, width), half), weights + (pltpu.HBM,), weights + (pltpu.HBM,)],
-        [tokens, pltpu.with_memory_space_constraint(router_full, pltpu.VMEM), d_out],
+        [((32, 16, width), half)] + [kind + (pltpu.HBM,) for kind in (weights, weights, rows)],
+        [pltpu.with_memory_space_constraint(part, pltpu.VMEM) for part in (held_tokens,)]
+        + [received, pltpu.with_memory_space_constraint(held_out, pltpu.VMEM)],
         [high],
-        out_specs=[vmem, hbm, hbm],
-        scratch_shapes=[pltpu.VMEM(*weights)] * 2 + [pltpu.SemaphoreType.DMA((2,))],
+        out_specs=[vmem, hbm, hbm, hbm],
+        scratch_shapes=[pltpu.VMEM(*kind) for kind in (weights, weights, rows)]
+        + [pltpu.SemaphoreType.DMA((3,))],
     )
     (wire,) = after(far_out, *after(far_in, exchange(wire)))
     own_0, other_0, own_1, other_1 = call(
         sort_kernel,
-        [((2, 64, width), half, kind) for kind in (pltpu.HBM, pltpu.VMEM) * 2],
+        [((2, 64, width), half, kind) for kind in (pltpu.HBM, jax.ShapeDtypeStruct) * 2],
         [wire],
         cost=pl.CostEstimate(flops=10**6, bytes_accessed=40 * MIB, transcendentals=0),
     )

time: 168 us -> 165 us (0.982)
  Pallas kernels: 33 us -> 35.7 us
  waiting for transfers between devices: 47.9 us -> 45.7 us
  local copies, waits for them, and re-layouts: 4.42 us -> 2.48 us
    pallas_call x13 -> x16, Pallas kernels: 33 us -> 35.7 us  [call(): pl.pallas_call(kernel, in_specs=[pl.BlockSpec(memory_space=pltpu.SMEM)] *...]
    all_to_all x1, waiting for transfers between devices: 13.9 us -> 11.2 us  [gather_router(): return lax.all_to_all(wide, ALL, split_axis=0, concat_axis=0, tiled=True)]
  transfers between devices with their start and end apart: 18 -> 18, of which waited for: 9 -> 9; matrix products, arithmetic and copies ran while one was open for 2% -> 0% of each run, Pallas kernels for 19% -> 21%
where the time goes in v6:
time: 165 us
  blocking collectives  49.8 us (30%)
  waiting for transfers between devices  45.7 us (28%)
  Pallas kernels  35.7 us (22%)
  starting transfers between devices  30 us (18%)
  local copies, waits for them, and re-layouts  2.48 us (2%)
    all_to_all x2, blocking collectives, exchange(): lax.all_to_all(blocks, PLANE, split_axis=0, concat_axis=0, tiled=True)  49.8 us
    pallas_call x16, Pallas kernels, call(): pl.pallas_call(kernel, in_specs=[pl.BlockSpec(memory_space=pltpu.SMEM)] *...  35.7 us
    all_to_all x1, waiting for transfers between devices, gather_router(): return lax.all_to_all(wide, ALL, split_axis=0, concat_axis=0, tiled=True)  11.2 us
    all_to_all x1, starting transfers between devices, gather_router(): return lax.all_to_all(wide, ALL, split_axis=0, concat_axis=0, tiled=True)  10.5 us
    ppermute x2, waiting for transfers between devices, body(): lax.ppermute(cross, 'zl', SWAP)  9.22 us
    all_to_all x1, waiting for transfers between devices, body(): lax.all_to_all(term, ALL, split_axis=0, concat_axis=0, tiled=True)  7.53 us
    ppermute x1, waiting for transfers between devices, body(): cross_1 = lax.ppermute(other_1, ('zl', 'zh'), CROSS)  7.02 us
    ppermute x1, waiting for transfers between devices, body(): pair_0 = lax.ppermute(parts_0[1], 'zl', SWAP)  5.39 us
  transfers between devices with their start and end apart: 18, of which 9 were waited for; matrix products, arithmetic and copies ran while one was open for 0% of the time, Pallas kernels for 21%

profile of v6, /device:TPU:1, one launch (start us, length us, event | category | flops | bytes accessed | tf_op | source)
XLA Modules:
  0.0 164.8 jit_solution(13764603441586425815)
XLA Ops:
  0.6 1.5 collective-permute-start.1
  2.1 0.1 collective-permute-start
  2.2 0.7 copy-done.6
  2.9 0.9 shard_map.78
  3.8 10.5 %all-to-all-start = ((bf16[128,10,128]{2,1,0:T(8,128)(2,1)}), bf16[128,10,128]{2,1,0:T(8,128)(2,1)S(1)}, u32[]{:S(2)}, u32[]{:S(2)}) async-start(bf16[128,10,128]{2,1,0:T(8,128)(2,1)} %shard_map.78), calls=%async_computation | async-start | bytes 1048576 | tf_op jit(solution)/shard_map/all_to_all | solution.py:94
  14.3 1.3 shard_map.76.tokens
  15.6 1.3 shard_map.77.d_out
  17.0 11.2 %all-to-all-done.received = bf16[128,10,128]{2,1,0:T(8,128)(2,1)S(1)} async-done(((bf16[128,10,128]{2,1,0:T(8,128)(2,1)}), bf16[128,10,128]{2,1,0:T(8,128)(2,1)S(1)}, u32[]{:S(2)}, u32[]{:S(2)}) %all-to-all-start) | async-done | bytes 327712 | tf_op jit(solution)/shard_map/all_to_all | solution.py:94
  28.2 2.2 %shard_map.79 = (bf16[32,16,1280]{2,1,0:T(8,128)(2,1)S(1)}, f32[2,256,128]{2,1,0:T(8,128)}, f32[2,256,128]{2,1,0:T(8,128)}, bf16[128,1280]{1,0:T(8,128)(2,1)}) custom-call(s32[1]{0:T(128)} %bitcast.high, bf16[2,256,1280]{2,1,0:T(8,128)(2,1)S(1)} %shard_map.76.tokens, bf16[128,10,128]{2,1,0:T(8,128)(2,1)S(1)} %all-to-all-done.received, ...), custom_call_target="tpu_custom_call" | custom-call | tf_op jit(solution)/shard_map/pallas_call | solution.py:72
  30.4 23.6 %all_to_all.20.wire = bf16[32,16,1280]{2,1,0:T(8,128)(2,1)S(1)} all-to-all(bf16[32,16,1280]{2,1,0:T(8,128)(2,1)S(1)} %get-tuple-element.59), channel_id=1, replica_groups=mesh['zl'=2,'core'=2,'xy'=16,'zh'=2] {'core','xy'}, dimensions={0} | all-to-all | bytes 2621440 | tf_op jit(solution)/shard_map/all_to_all | solution.py:20
  54.0 0.0 collective-permute-done.1.far_in
  54.0 1.3 shard_map.80
  55.3 1.1 collective-permute-start.3
  56.4 1.6 collective-permute-start.5
  58.0 0.9 collective-permute-start.4
  58.8 4.9 %shard_map.81 = (bf16[2,2,1280,640]{3,2,1,0:T(8,128)(2,1)S(1)}, bf16[2,2,640,1280]{3,2,1,0:T(8,128)(2,1)S(1)}) custom-call(s32[1]{0:T(128)} %bitcast.1.core, bf16[4,1280,640]{2,1,0:T(8,128)(2,1)} %near_in, bf16[4,640,1280]{2,1,0:T(8,128)(2,1)} %near_out, bf16[4,1280,640]{2,1,0:T(8,128)(2,1)} %collective-permute-done.1.far_in, ...), custom_call_target="tpu_custom_call" | custom-call | tf_op jit(solution)/shard_map/pallas_call | solution.py:72
  63.7 1.2 collective-permute-done.3.refs_2_
  64.9 7.0 %collective-permute-done.5.refs_2_ = bf16[2,64,1280]{2,1,0:T(8,128)(2,1)S(1)} collective-permute-done((bf16[2,64,1280]{2,1,0:T(8,128)(2,1)S(1)}, bf16[2,64,1280]{2,1,0:T(8,128)(2,1)S(1)}, u32[]{:S(2)}, u32[]{:S(2)}) %collective-permute-start.5) | collective-permute-done | bytes 327712 | tf_op jit(solution)/shard_map/ppermute | solution.py:385
  71.9 6.8 %collective-permute-done.6.refs_3_ = bf16[2,64,1280]{2,1,0:T(8,128)(2,1)S(1)} collective-permute-done((bf16[2,64,1280]{2,1,0:T(8,128)(2,1)S(1)}, bf16[2,64,1280]{2,1,0:T(8,128)(2,1)S(1)}, u32[]{:S(2)}, u32[]{:S(2)}) %collective-permute-start.6) | collective-permute-done | bytes 327712 | tf_op jit(solution)/shard_map/ppermute | solution.py:389
  78.7 4.6 %shard_map.82 = (bf16[2,64,1280]{2,1,0:T(8,128)(2,1)S(1)}, bf16[2,64,1280]{2,1,0:T(8,128)(2,1)S(1)}, bf16[2,64,1280]{2,1,0:T(8,128)(2,1)S(1)}, bf16[2,64,1280]{2...) custom-call(bf16[2,64,1280]{2,1,0:T(8,128)(2,1)S(1)} %copy-done.8, ...), custom_call_target="tpu_custom_call" | custom-call | flops 8000000000 | bytes 25165824 | tf_op jit(solution)/shard_map/pallas_call | solution.py:72
  83.3 2.4 %collective-permute-done.8.refs_3_ = bf16[2,64,1280]{2,1,0:T(8,128)(2,1)S(1)} collective-permute-done((bf16[2,64,1280]{2,1,0:T(8,128)(2,1)S(1)}, bf16[2,64,1280]{2,1,0:T(8,128)(2,1)S(1)}, u32[]{:S(2)}, u32[]{:S(2)}) %collective-permute-start.8) | collective-permute-done | bytes 327712 | tf_op jit(solution)/shard_map/ppermute | solution.py:389
  85.7 0.2 collective-permute-start.9
  85.9 4.6 %shard_map.83 = (bf16[2,64,1280]{2,1,0:T(8,128)(2,1)S(1)}, bf16[2,64,1280]{2,1,0:T(8,128)(2,1)S(1)}, bf16[2,64,1280]{2,1,0:T(8,128)(2,1)S(1)}, bf16[2,64,1280]{2...) custom-call(bf16[2,64,1280]{2,1,0:T(8,128)(2,1)S(1)} %copy-done.7, ...), custom_call_target="tpu_custom_call" | custom-call | flops 8000000000 | bytes 25165824 | tf_op jit(solution)/shard_map/pallas_call | solution.py:72
  90.5 1.4 collective-permute-start.10
  91.9 0.2 collective-permute-start.7
  92.1 0.8 collective-permute-done.9.right
  92.9 0.1 shard_map.84
  93.0 1.6 collective-permute-start.11
  94.6 2.4 %shard_map.85 = (bf16[4,640,1280]{2,1,0:T(8,128)(2,1)}, bf16[640,1280]{1,0:T(8,128)(2,1)}) custom-call(s32[1]{0:T(128)} %bitcast.1.core, bf16[2,256,640]{2,1,0:T(8,128)(2,1)S(1)} %get-tuple-element.85.active, bf16[256,1280]{1,0:T(8,128)(2,1)S(1)} %get-tuple-element.86.grads), custom_call_target="tpu_custom_call" | custom-call | tf_op jit(solution)/shard_map/pallas_call | solution.py:72
  97.1 3.3 %collective-permute-done.10.right = bf16[2,64,1280]{2,1,0:T(8,128)(2,1)S(1)} collective-permute-done((bf16[2,64,1280]{2,1,0:T(8,128)(2,1)S(1)}, bf16[2,64,1280]{2,1,0:T(8,128)(2,1)S(1)}, u32[]{:S(2)}, u32[]{:S(2)}) %collective-permute-start.10) | collective-permute-done | bytes 327712 | tf_op jit(solution)/shard_map/ppermute | solution.py:398
  100.4 0.1 shard_map.86
  100.5 1.5 collective-permute-start.12
  102.0 5.4 %collective-permute-done.7.refs_1_ = bf16[2,64,1280]{2,1,0:T(8,128)(2,1)S(1)} collective-permute-done((bf16[2,64,1280]{2,1,0:T(8,128)(2,1)S(1)}, bf16[2,64,1280]{2,1,0:T(8,128)(2,1)S(1)}, u32[]{:S(2)}, u32[]{:S(2)}) %collective-permute-start.7) | collective-permute-done | bytes 327712 | tf_op jit(solution)/shard_map/ppermute | solution.py:397
  107.4 2.4 %shard_map.87 = (bf16[4,640,1280]{2,1,0:T(8,128)(2,1)}, bf16[640,1280]{1,0:T(8,128)(2,1)}) custom-call(s32[1]{0:T(128)} %bitcast.1.core, bf16[2,256,640]{2,1,0:T(8,128)(2,1)S(1)} %get-tuple-element.92.active, bf16[256,1280]{1,0:T(8,128)(2,1)S(1)} %get-tuple-element.93.grads, ...), custom_call_target="tpu_custom_call", output_to_operand_aliasing={{0}: (3, {})} | custom-call | tf_op jit(solution)/shard_map/pallas_call | solution.py:72
  109.9 4.7 %collective-permute-start.14 = (bf16[640,1280]{1,0:T(8,128)(2,1)}, bf16[640,1280]{1,0:T(8,128)(2,1)S(1)}, u32[]{:S(2)}, u32[]{:S(2)}) collective-permute-start(bf16[640,1280]{1,0:T(8,128)(2,1)} %get-tuple-element.101), channel_id=1, source_target_pairs={{0,32},{32,0},{1,33},{33,1},{2,34},{34,2},{3,35},{35,3},{4,36},{36... | collective-permute-start | bytes 4915208 | tf_op jit(solution)/shard_map/ppermute | solution.py:412
  114.5 0.1 collective-permute-start.15
  114.7 0.6 shard_map.88
  115.3 0.0 copy-start
  115.3 0.0 copy-start.1
  115.3 26.2 %all_to_all.21.wire = bf16[32,16,1280]{2,1,0:T(8,128)(2,1)S(1)} all-to-all(bf16[32,16,1280]{2,1,0:T(8,128)(2,1)S(1)} %shard_map.88), channel_id=1, replica_groups=mesh['zl'=2,'core'=2,'xy'=16,'zh'=2] {'core','xy'}, dimensions={0} | all-to-all | bytes 2621440 | tf_op jit(solution)/shard_map/all_to_all | solution.py:20
  141.5 3.9 %shard_map.89 = (bf16[2,256,128]{2,1,0:T(8,128)(2,1)S(1)}, bf16[256,1280]{1,0:T(8,128)(2,1)}, bf16[128,10,128]{2,1,0:T(8,128)(2,1)}) custom-call(s32[1]{0:T(128)} %bitcast.high, bf16[32,16,1280]{2,1,0:T(8,128)(2,1)S(1)} %all_to_all.21.wire, bf16[2,256,1280]{2,1,0:T(8,128)(2,1)S(1)} %copy-done, bf16[2,256,1280]{2,1,0:T(8,128)(2,1)S(1)} %copy-done.1, ...), custom_call_target="tpu_custom_call" | custom-call | tf_op jit(solution)/shard_map/pallas_call | solution.py:72
  145.5 4.7 %all-to-all-start.3 = ((bf16[128,10,128]{2,1,0:T(8,128)(2,1)}), bf16[128,10,128]{2,1,0:T(8,128)(2,1)S(1)}, u32[]{:S(2)}, u32[]{:S(2)}) async-start(bf16[128,10,128]{2,1,0:T(8,128)(2,1)} %get-tuple-element.108), calls=%async_computation.3 | async-start | bytes 1048576 | tf_op jit(solution)/shard_map/all_to_all | solution.py:437
  150.2 1.2 copy-done.9
  151.4 3.3 %shard_map.90 = bf16[4,640,1280]{2,1,0:T(8,128)(2,1)} custom-call(s32[1]{0:T(128)} %bitcast.1.core, bf16[640,1280]{1,0:T(8,128)(2,1)} %copy-done.9, bf16[640,1280]{1,0:T(8,128)(2,1)} %collective-permute-done.15.came_1, bf16[4,640,1280]{2,1,0:T(8,128)(2,1)} %get-tuple-element.104._), custom_call_target="tpu_custom_call", output_to_operand_aliasing={{}: (3, {})} | custom-call | tf_op jit(solution)/shard_map/pallas_call | solution.py:72
  154.7 1.9 %shard_map.91 = bf16[2,256,1280]{2,1,0:T(8,128)(2,1)} custom-call(f32[2,256,128]{2,1,0:T(8,128)S(1)} %copy-done.2, bf16[2,256,128]{2,1,0:T(8,128)(2,1)S(1)} %get-tuple-element.100.logit_grad, bf16[256,1280]{1,0:T(8,128)(2,1)S(1)} %copy-done.3, bf16[128,1280]{1,0:T(8,128)(2,1)S(1)} %copy-done.4), custom_call_target="tpu_custom_call" | custom-call | tf_op jit(solution)/shard_map/pallas_call | solution.py:72
  156.6 7.5 %all-to-all-done.3 = bf16[128,10,128]{2,1,0:T(8,128)(2,1)S(1)} async-done(((bf16[128,10,128]{2,1,0:T(8,128)(2,1)}), bf16[128,10,128]{2,1,0:T(8,128)(2,1)S(1)}, u32[]{:S(2)}, u32[]{:S(2)}) %all-to-all-start.3) | async-done | bytes 327712 | tf_op jit(solution)/shard_map/all_to_all | solution.py:437
  164.1 0.1 convert_reduce_fusion
  164.2 0.6 copy.12
  (28 shorter events, 0.1 us)
Async XLA Ops:
  0.6 53.3 %collective-permute-start.1 = (bf16[4,1280,640]{2,1,0:T(8,128)(2,1)}, bf16[4,1280,640]{2,1,0:T(8,128)(2,1)}, u32[]{:S(2)}, u32[]{:S(2)}) collective-permute-start(bf16[4,1280,640]{2,1,0:T(8,128)(2,1)} %near_in), channel_id=1, source_target_pairs={{0,32},{32,0},{1,33},{33,1},{2,34},{34,2},{3,35},{35,3},{4,36},{36... | collective-permute-start | bytes 19660808 | tf_op jit(solution)/shard_map/ppermute | solution.py:357
  2.1 51.8 %collective-permute-start = (bf16[4,640,1280]{2,1,0:T(8,128)(2,1)}, bf16[4,640,1280]{2,1,0:T(8,128)(2,1)}, u32[]{:S(2)}, u32[]{:S(2)}) collective-permute-start(bf16[4,640,1280]{2,1,0:T(8,128)(2,1)} %near_out), channel_id=1, source_target_pairs={{0,32},{32,0},{1,33},{33,1},{2,34},{34,2},{3,35},{35,3},{4,36},{36... | collective-permute-start | bytes 19660808 | tf_op jit(solution)/shard_map/ppermute | solution.py:358
  2.2 0.7 copy-start.6
  3.8 24.4 %all-to-all-start = ((bf16[128,10,128]{2,1,0:T(8,128)(2,1)}), bf16[128,10,128]{2,1,0:T(8,128)(2,1)S(1)}, u32[]{:S(2)}, u32[]{:S(2)}) async-start(bf16[128,10,128]{2,1,0:T(8,128)(2,1)} %shard_map.78), calls=%async_computation | async-start | bytes 1048576 | tf_op jit(solution)/shard_map/all_to_all | solution.py:94
  55.3 9.6 %collective-permute-start.3 = (bf16[2,64,1280]{2,1,0:T(8,128)(2,1)S(1)}, bf16[2,64,1280]{2,1,0:T(8,128)(2,1)S(1)}, u32[]{:S(2)}, u32[]{:S(2)}) collective-permute-start(bf16[2,64,1280]{2,1,0:T(8,128)(2,1)S(1)} %get-tuple-element.68), channel_id=1, source_target_pairs={{0,65},{1,64},{64,1},{65,0},{2,67},{3,66},{66,3},{67,2},{4,69},{5,... | collective-permute-start | bytes 983048 | tf_op jit(solution)/shard_map/ppermute | solution.py:384
  56.4 8.5 %collective-permute-start.2 = (bf16[2,64,1280]{2,1,0:T(8,128)(2,1)}, bf16[2,64,1280]{2,1,0:T(8,128)(2,1)S(1)}, u32[]{:S(2)}, u32[]{:S(2)}) collective-permute-start(bf16[2,64,1280]{2,1,0:T(8,128)(2,1)} %get-tuple-element.62.refs_0_), channel_id=1, source_target_pairs={{0,64},{64,0},{1,65},{65,1},{2,66},{66,2},{3,67},{67,3},{4,68},{68... | collective-permute-start | bytes 983048 | tf_op jit(solution)/shard_map/ppermute | solution.py:383
  56.4 15.5 %collective-permute-start.5 = (bf16[2,64,1280]{2,1,0:T(8,128)(2,1)S(1)}, bf16[2,64,1280]{2,1,0:T(8,128)(2,1)S(1)}, u32[]{:S(2)}, u32[]{:S(2)}) collective-permute-start(bf16[2,64,1280]{2,1,0:T(8,128)(2,1)S(1)} %get-tuple-element.72), channel_id=1, source_target_pairs={{0,65},{1,64},{64,1},{65,0},{2,67},{3,66},{66,3},{67,2},{4,69},{5,... | collective-permute-start | bytes 983048 | tf_op jit(solution)/shard_map/ppermute | solution.py:385
  58.0 13.9 %collective-permute-start.4 = (bf16[2,64,1280]{2,1,0:T(8,128)(2,1)}, bf16[2,64,1280]{2,1,0:T(8,128)(2,1)S(1)}, u32[]{:S(2)}, u32[]{:S(2)}) collective-permute-start(bf16[2,64,1280]{2,1,0:T(8,128)(2,1)} %get-tuple-element.71.refs_0_), channel_id=1, source_target_pairs={{0,64},{64,0},{1,65},{65,1},{2,66},{66,2},{3,67},{67,3},{4,68},{68... | collective-permute-start | bytes 983048 | tf_op jit(solution)/shard_map/ppermute | solution.py:383
  58.8 19.9 %copy-start.8 = (bf16[2,64,1280]{2,1,0:T(8,128)(2,1)S(1)}, bf16[2,64,1280]{2,1,0:T(8,128)(2,1)}, u32[]{:S(2)}) copy-start(bf16[2,64,1280]{2,1,0:T(8,128)(2,1)} %get-tuple-element.62.refs_0_) | copy-start | bytes 983044
  64.9 13.8 %collective-permute-start.6 = (bf16[2,64,1280]{2,1,0:T(8,128)(2,1)S(1)}, bf16[2,64,1280]{2,1,0:T(8,128)(2,1)S(1)}, u32[]{:S(2)}, u32[]{:S(2)}) collective-permute-start(bf16[2,64,1280]{2,1,0:T(8,128)(2,1)S(1)} %collective-permute-done.3.refs_2_), channel_id=1, source_target_pairs={{0,64},{64,0},{1,65},{65,1},{2,66},{66,2},{3,67},{67,3},{4,68},{68... | collective-permute-start | bytes 983048 | tf_op jit(solution)/shard_map/ppermute | solution.py:389
  71.9 13.8 %collective-permute-start.8 = (bf16[2,64,1280]{2,1,0:T(8,128)(2,1)S(1)}, bf16[2,64,1280]{2,1,0:T(8,128)(2,1)S(1)}, u32[]{:S(2)}, u32[]{:S(2)}) collective-permute-start(bf16[2,64,1280]{2,1,0:T(8,128)(2,1)S(1)} %collective-permute-done.5.refs_2_), channel_id=1, source_target_pairs={{0,64},{64,0},{1,65},{65,1},{2,66},{66,2},{3,67},{67,3},{4,68},{68... | collective-permute-start | bytes 983048 | tf_op jit(solution)/shard_map/ppermute | solution.py:389
  78.7 7.2 %copy-start.7 = (bf16[2,64,1280]{2,1,0:T(8,128)(2,1)S(1)}, bf16[2,64,1280]{2,1,0:T(8,128)(2,1)}, u32[]{:S(2)}) copy-start(bf16[2,64,1280]{2,1,0:T(8,128)(2,1)} %get-tuple-element.71.refs_0_) | copy-start | bytes 983044
  85.7 7.2 %collective-permute-start.9 = (bf16[2,64,1280]{2,1,0:T(8,128)(2,1)S(1)}, bf16[2,64,1280]{2,1,0:T(8,128)(2,1)S(1)}, u32[]{:S(2)}, u32[]{:S(2)}) collective-permute-start(bf16[2,64,1280]{2,1,0:T(8,128)(2,1)S(1)} %get-tuple-element.82), channel_id=1, source_target_pairs={{0,64},{64,0},{1,65},{65,1},{2,66},{66,2},{3,67},{67,3},{4,68},{68... | collective-permute-start | bytes 983048 | tf_op jit(solution)/shard_map/ppermute | solution.py:396
  90.5 9.9 %collective-permute-start.10 = (bf16[2,64,1280]{2,1,0:T(8,128)(2,1)S(1)}, bf16[2,64,1280]{2,1,0:T(8,128)(2,1)S(1)}, u32[]{:S(2)}, u32[]{:S(2)}) collective-permute-start(bf16[2,64,1280]{2,1,0:T(8,128)(2,1)S(1)} %get-tuple-element.88), channel_id=1, source_target_pairs={{0,64},{64,0},{1,65},{65,1},{2,66},{66,2},{3,67},{67,3},{4,68},{68... | collective-permute-start | bytes 983048 | tf_op jit(solution)/shard_map/ppermute | solution.py:398
  91.9 15.5 %collective-permute-start.7 = (bf16[2,64,1280]{2,1,0:T(8,128)(2,1)S(1)}, bf16[2,64,1280]{2,1,0:T(8,128)(2,1)S(1)}, u32[]{:S(2)}, u32[]{:S(2)}) collective-permute-start(bf16[2,64,1280]{2,1,0:T(8,128)(2,1)S(1)} %get-tuple-element.77), channel_id=1, source_target_pairs={{0,64},{64,0},{1,65},{65,1},{2,66},{66,2},{3,67},{67,3},{4,68},{68... | collective-permute-start | bytes 983048 | tf_op jit(solution)/shard_map/ppermute | solution.py:397
  93.0 21.7 %collective-permute-start.11 = (bf16[2,64,1280]{2,1,0:T(8,128)(2,1)S(1)}, bf16[2,64,1280]{2,1,0:T(8,128)(2,1)S(1)}, u32[]{:S(2)}, u32[]{:S(2)}) collective-permute-start(bf16[2,64,1280]{2,1,0:T(8,128)(2,1)S(1)} %shard_map.84), channel_id=1, source_target_pairs={{0,65},{1,64},{64,1},{65,0},{2,67},{3,66},{66,3},{67,2},{4,69},{5,... | collective-permute-start | bytes 983048 | tf_op jit(solution)/shard_map/ppermute | solution.py:402
  100.5 14.2 %collective-permute-start.12 = (bf16[2,64,1280]{2,1,0:T(8,128)(2,1)S(1)}, bf16[2,64,1280]{2,1,0:T(8,128)(2,1)S(1)}, u32[]{:S(2)}, u32[]{:S(2)}) collective-permute-start(bf16[2,64,1280]{2,1,0:T(8,128)(2,1)S(1)} %shard_map.86), channel_id=1, source_target_pairs={{0,65},{1,64},{64,1},{65,0},{2,67},{3,66},{66,3},{67,2},{4,69},{5,... | collective-permute-start | bytes 983048 | tf_op jit(solution)/shard_map/ppermute | solution.py:407
  102.0 12.6 %collective-permute-start.13 = (bf16[2,64,1280]{2,1,0:T(8,128)(2,1)S(1)}, bf16[2,64,1280]{2,1,0:T(8,128)(2,1)S(1)}, u32[]{:S(2)}, u32[]{:S(2)}) collective-permute-start(bf16[2,64,1280]{2,1,0:T(8,128)(2,1)S(1)} %get-tuple-element.97), channel_id=1, source_target_pairs={{0,64},{64,0},{1,65},{65,1},{2,66},{66,2},{3,67},{67,3},{4,68},{68... | collective-permute-start | bytes 983048 | tf_op jit(solution)/shard_map/ppermute | solution.py:399
  109.9 40.3 %collective-permute-start.14 = (bf16[640,1280]{1,0:T(8,128)(2,1)}, bf16[640,1280]{1,0:T(8,128)(2,1)S(1)}, u32[]{:S(2)}, u32[]{:S(2)}) collective-permute-start(bf16[640,1280]{1,0:T(8,128)(2,1)} %get-tuple-element.101), channel_id=1, source_target_pairs={{0,32},{32,0},{1,33},{33,1},{2,34},{34,2},{3,35},{35,3},{4,36},{36... | collective-permute-start | bytes 4915208 | tf_op jit(solution)/shard_map/ppermute | solution.py:412
  114.5 35.7 %collective-permute-start.15 = (bf16[640,1280]{1,0:T(8,128)(2,1)}, bf16[640,1280]{1,0:T(8,128)(2,1)}, u32[]{:S(2)}, u32[]{:S(2)}) collective-permute-start(bf16[640,1280]{1,0:T(8,128)(2,1)} %get-tuple-element.95), channel_id=1, source_target_pairs={{0,32},{32,0},{1,33},{33,1},{2,34},{34,2},{3,35},{35,3},{4,36},{36... | collective-permute-start | bytes 4915208 | tf_op jit(solution)/shard_map/ppermute | solution.py:413
  114.6 26.9 %copy-start.2 = (f32[2,256,128]{2,1,0:T(8,128)S(1)}, f32[2,256,128]{2,1,0:T(8,128)}, u32[]{:S(2)}) copy-start(f32[2,256,128]{2,1,0:T(8,128)} %get-tuple-element.58.dispatch) | copy-start | bytes 786436
  114.7 26.9 %copy-start.5 = (f32[2,256,128]{2,1,0:T(8,128)S(1)}, f32[2,256,128]{2,1,0:T(8,128)}, u32[]{:S(2)}) copy-start(f32[2,256,128]{2,1,0:T(8,128)} %get-tuple-element.99.combine) | copy-start | bytes 786436
  115.3 26.3 %copy-start = (bf16[2,256,1280]{2,1,0:T(8,128)(2,1)S(1)}, bf16[2,256,1280]{2,1,0:T(8,128)(2,1)}, u32[]{:S(2)}) copy-start(bf16[2,256,1280]{2,1,0:T(8,128)(2,1)} %tokens.1) | copy-start | bytes 3932164
  115.3 26.3 %copy-start.1 = (bf16[2,256,1280]{2,1,0:T(8,128)(2,1)S(1)}, bf16[2,256,1280]{2,1,0:T(8,128)(2,1)}, u32[]{:S(2)}) copy-start(bf16[2,256,1280]{2,1,0:T(8,128)(2,1)} %d_out.1) | copy-start | bytes 3932164
  145.5 18.6 %all-to-all-start.3 = ((bf16[128,10,128]{2,1,0:T(8,128)(2,1)}), bf16[128,10,128]{2,1,0:T(8,128)(2,1)S(1)}, u32[]{:S(2)}, u32[]{:S(2)}) async-start(bf16[128,10,128]{2,1,0:T(8,128)(2,1)} %get-tuple-element.108), calls=%async_computation.3 | async-start | bytes 1048576 | tf_op jit(solution)/shard_map/all_to_all | solution.py:437
  150.2 1.2 copy-start.9
  151.4 3.3 %copy-start.3 = (bf16[256,1280]{1,0:T(8,128)(2,1)S(1)}, bf16[256,1280]{1,0:T(8,128)(2,1)}, u32[]{:S(2)}) copy-start(bf16[256,1280]{1,0:T(8,128)(2,1)} %get-tuple-element.106.slot_back) | copy-start | bytes 1966084
  151.4 3.3 %copy-start.4 = (bf16[128,1280]{1,0:T(8,128)(2,1)S(1)}, bf16[128,1280]{1,0:T(8,128)(2,1)}, u32[]{:S(2)}) copy-start(bf16[128,1280]{1,0:T(8,128)(2,1)} %get-tuple-element.107.router) | copy-start | bytes 983044

commit v7 on v6

--- a/solution.py
+++ b/solution.py
@@ -89,7 +89,7 @@
 
 
 def gather_router(router):
-    wide = ((lax.axis_size(ALL), router.shape[1] // 128, 128), router.dtype, pltpu.HBM)
+    wide = ((lax.axis_size(ALL), 2, router.shape[1] // 2), router.dtype, pltpu.HBM)
     wide = call(widen_kernel, [wide], [router])[0]
     return lax.all_to_all(wide, ALL, split_axis=0, concat_axis=0, tiled=True)
 
@@ -115,8 +115,9 @@
     score_scale, high, tokens, received, d_out,
     wire, dispatch, combine, router_full, held_0, held_1, router, sems,
 ):
+    lanes = received.shape[2]
     for index in range(received.shape[1]):
-        router[:, 128 * index : 128 * index + 128] = received[:, index]
+        router[:, lanes * index : lanes * index + lanes] = received[:, index]
     slots, grads = [], []
     for image in range(2):
         logits = product(tokens[image], router[...], 1, 1) * score_scale
@@ -269,8 +270,9 @@
         logit_grad[image] = score
         part = product(score, tokens[image], 0, 0)
         total = part if total is None else total + part
+    lanes = term.shape[2]
     for index in range(term.shape[1]):
-        held_term[:, index] = total[:, 128 * index : 128 * index + 128].astype(term.dtype)
+        held_term[:, index] = total[:, lanes * index : lanes * index + lanes].astype(term.dtype)
     copies[1].start()
     for copy in copies:
         copy.wait()
@@ -423,14 +425,14 @@
         [
             ((images, count, slots), half),
             ((images * slots, width), half, pltpu.HBM),
-            ((slots, width // 128, 128), half, pltpu.HBM),
+            ((slots, 2, width // 2), half, pltpu.HBM),
         ],
         [wire, tokens, d_out, dispatch, combine],
         [high],
         out_specs=[vmem, hbm, hbm],
         scratch_shapes=[
             pltpu.VMEM((images * slots, width), half),
-            pltpu.VMEM((slots, width // 128, 128), half),
+            pltpu.VMEM((slots, 2, width // 2), half),
             pltpu.SemaphoreType.DMA((2,)),
         ],
     )

time: 165 us -> 163 us (0.988)
  waiting for transfers between devices: 45.7 us -> 43.9 us
    all_to_all x1, waiting for transfers between devices: 11.2 us -> 9.11 us  [gather_router(): return lax.all_to_all(wide, ALL, split_axis=0, concat_axis=0, tiled=True)]
    ppermute x2, waiting for transfers between devices: 0.01 us -> 2.1 us  [body(): pair_0, pair_1 = (lax.ppermute(own, 'zl', SWAP) for own in (own_0, own_1))]
    ppermute x1, starting transfers between devices: 1.11 us -> 3.18 us  [body(): cross_0 = lax.ppermute(other_0, ('zl', 'zh'), CROSS)]
    all_to_all x1, waiting for transfers between devices: 7.53 us -> 5.56 us  [body(): lax.all_to_all(term, ALL, split_axis=0, concat_axis=0, tiled=True)]
  transfers between devices with their start and end apart: 18 -> 18, of which waited for: 9 -> 12; matrix products, arithmetic and copies ran while one was open for 0% -> 0% of each run, Pallas kernels for 21% -> 21%
where the time goes in v7:
time: 163 us; the launch traced here: 162 us
  blocking collectives  50.1 us (31%)
  waiting for transfers between devices  43.9 us (27%)
  Pallas kernels  35.2 us (22%)
  starting transfers between devices  29.4 us (18%)
  local copies, waits for them, and re-layouts  2.48 us (2%)
    all_to_all x2, blocking collectives, exchange(): lax.all_to_all(blocks, PLANE, split_axis=0, concat_axis=0, tiled=True)  50.1 us
    pallas_call x16, Pallas kernels, call(): pl.pallas_call(kernel, in_specs=[pl.BlockSpec(memory_space=pltpu.SMEM)] *...  35.2 us
    all_to_all x1, starting transfers between devices, gather_router(): return lax.all_to_all(wide, ALL, split_axis=0, concat_axis=0, tiled=True)  10.5 us
    ppermute x2, waiting for transfers between devices, body(): lax.ppermute(cross, 'zl', SWAP)  9.12 us
    all_to_all x1, waiting for transfers between devices, gather_router(): return lax.all_to_all(wide, ALL, split_axis=0, concat_axis=0, tiled=True)  9.11 us
    ppermute x1, waiting for transfers between devices, body(): pair_0 = lax.ppermute(parts_0[1], 'zl', SWAP)  6.2 us
    ppermute x1, waiting for transfers between devices, body(): cross_1 = lax.ppermute(other_1, ('zl', 'zh'), CROSS)  5.66 us
    all_to_all x1, waiting for transfers between devices, body(): lax.all_to_all(term, ALL, split_axis=0, concat_axis=0, tiled=True)  5.56 us
  transfers between devices with their start and end apart: 18, of which 12 were waited for; matrix products, arithmetic and copies ran while one was open for 0% of the time, Pallas kernels for 21%

profile of v7, /device:TPU:1, one launch (start us, length us, event | category | flops | bytes accessed | tf_op | source)
XLA Modules:
  0.0 162.2 jit_solution(9279598654079777024)
XLA Ops:
  0.6 1.5 collective-permute-start.1
  2.1 0.1 collective-permute-start
  2.2 0.7 copy-done.6
  2.9 0.8 shard_map.78
  3.7 10.5 %all-to-all-start = ((bf16[128,2,640]{2,1,0:T(2,128)(2,1)}), bf16[128,2,640]{2,1,0:T(2,128)(2,1)S(1)}, u32[]{:S(2)}, u32[]{:S(2)}) async-start(bf16[128,2,640]{2,1,0:T(2,128)(2,1)} %shard_map.78), calls=%async_computation | async-start | bytes 655360 | tf_op jit(solution)/shard_map/all_to_all | solution.py:94
  14.2 1.3 shard_map.76.tokens
  15.5 1.3 shard_map.77.d_out
  16.9 9.1 %all-to-all-done.received = bf16[128,2,640]{2,1,0:T(2,128)(2,1)S(1)} async-done(((bf16[128,2,640]{2,1,0:T(2,128)(2,1)}), bf16[128,2,640]{2,1,0:T(2,128)(2,1)S(1)}, u32[]{:S(2)}, u32[]{:S(2)}) %all-to-all-start) | async-done | bytes 327712 | tf_op jit(solution)/shard_map/all_to_all | solution.py:94
  26.0 2.5 %shard_map.79 = (bf16[32,16,1280]{2,1,0:T(8,128)(2,1)S(1)}, f32[2,256,128]{2,1,0:T(8,128)}, f32[2,256,128]{2,1,0:T(8,128)}, bf16[128,1280]{1,0:T(8,128)(2,1)}) custom-call(s32[1]{0:T(128)} %bitcast.high, bf16[2,256,1280]{2,1,0:T(8,128)(2,1)S(1)} %shard_map.76.tokens, bf16[128,2,640]{2,1,0:T(2,128)(2,1)S(1)} %all-to-all-done.received, ...), custom_call_target="tpu_custom_call" | custom-call | tf_op jit(solution)/shard_map/pallas_call | solution.py:72
  28.5 23.7 %all_to_all.20.wire = bf16[32,16,1280]{2,1,0:T(8,128)(2,1)S(1)} all-to-all(bf16[32,16,1280]{2,1,0:T(8,128)(2,1)S(1)} %get-tuple-element.59), channel_id=1, replica_groups=mesh['zl'=2,'core'=2,'xy'=16,'zh'=2] {'core','xy'}, dimensions={0} | all-to-all | bytes 2621440 | tf_op jit(solution)/shard_map/all_to_all | solution.py:20
  52.2 1.3 shard_map.80
  53.5 3.2 %collective-permute-start.3 = (bf16[2,64,1280]{2,1,0:T(8,128)(2,1)S(1)}, bf16[2,64,1280]{2,1,0:T(8,128)(2,1)S(1)}, u32[]{:S(2)}, u32[]{:S(2)}) collective-permute-start(bf16[2,64,1280]{2,1,0:T(8,128)(2,1)S(1)} %get-tuple-element.68), channel_id=1, source_target_pairs={{0,65},{1,64},{64,1},{65,0},{2,67},{3,66},{66,3},{67,2},{4,69},{5,... | collective-permute-start | bytes 983048 | tf_op jit(solution)/shard_map/ppermute | solution.py:386
  56.7 0.1 collective-permute-start.5
  56.8 1.3 collective-permute-start.4
  58.2 4.9 %shard_map.81 = (bf16[2,2,1280,640]{3,2,1,0:T(8,128)(2,1)S(1)}, bf16[2,2,640,1280]{3,2,1,0:T(8,128)(2,1)S(1)}) custom-call(s32[1]{0:T(128)} %bitcast.1.core, bf16[4,1280,640]{2,1,0:T(8,128)(2,1)} %near_in, bf16[4,640,1280]{2,1,0:T(8,128)(2,1)} %near_out, bf16[4,1280,640]{2,1,0:T(8,128)(2,1)} %collective-permute-done.1.far_in, ...), custom_call_target="tpu_custom_call" | custom-call | tf_op jit(solution)/shard_map/pallas_call | solution.py:72
  63.1 0.9 collective-permute-done.3.refs_2_
  63.9 1.0 collective-permute-done.2.refs_1_
  65.0 0.3 collective-permute-start.6
  65.3 5.7 %collective-permute-done.5.refs_2_ = bf16[2,64,1280]{2,1,0:T(8,128)(2,1)S(1)} collective-permute-done((bf16[2,64,1280]{2,1,0:T(8,128)(2,1)S(1)}, bf16[2,64,1280]{2,1,0:T(8,128)(2,1)S(1)}, u32[]{:S(2)}, u32[]{:S(2)}) %collective-permute-start.5) | collective-permute-done | bytes 327712 | tf_op jit(solution)/shard_map/ppermute | solution.py:387
  71.0 1.0 collective-permute-done.4.refs_1_
  72.0 0.3 collective-permute-start.8
  72.3 6.7 %collective-permute-done.6.refs_3_ = bf16[2,64,1280]{2,1,0:T(8,128)(2,1)S(1)} collective-permute-done((bf16[2,64,1280]{2,1,0:T(8,128)(2,1)S(1)}, bf16[2,64,1280]{2,1,0:T(8,128)(2,1)S(1)}, u32[]{:S(2)}, u32[]{:S(2)}) %collective-permute-start.6) | collective-permute-done | bytes 327712 | tf_op jit(solution)/shard_map/ppermute | solution.py:391
  79.0 4.6 %shard_map.82 = (bf16[2,64,1280]{2,1,0:T(8,128)(2,1)S(1)}, bf16[2,64,1280]{2,1,0:T(8,128)(2,1)S(1)}, bf16[2,64,1280]{2,1,0:T(8,128)(2,1)S(1)}, bf16[2,64,1280]{2...) custom-call(bf16[2,64,1280]{2,1,0:T(8,128)(2,1)S(1)} %copy-done.8, ...), custom_call_target="tpu_custom_call" | custom-call | flops 8000000000 | bytes 25165824 | tf_op jit(solution)/shard_map/pallas_call | solution.py:72
  83.7 2.4 %collective-permute-done.8.refs_3_ = bf16[2,64,1280]{2,1,0:T(8,128)(2,1)S(1)} collective-permute-done((bf16[2,64,1280]{2,1,0:T(8,128)(2,1)S(1)}, bf16[2,64,1280]{2,1,0:T(8,128)(2,1)S(1)}, u32[]{:S(2)}, u32[]{:S(2)}) %collective-permute-start.8) | collective-permute-done | bytes 327712 | tf_op jit(solution)/shard_map/ppermute | solution.py:391
  86.1 0.3 collective-permute-start.9
  86.4 4.6 %shard_map.83 = (bf16[2,64,1280]{2,1,0:T(8,128)(2,1)S(1)}, bf16[2,64,1280]{2,1,0:T(8,128)(2,1)S(1)}, bf16[2,64,1280]{2,1,0:T(8,128)(2,1)S(1)}, bf16[2,64,1280]{2...) custom-call(bf16[2,64,1280]{2,1,0:T(8,128)(2,1)S(1)} %copy-done.7, ...), custom_call_target="tpu_custom_call" | custom-call | flops 8000000000 | bytes 25165824 | tf_op jit(solution)/shard_map/pallas_call | solution.py:72
  91.0 1.2 collective-permute-start.10
  92.2 0.3 collective-permute-start.7
  92.5 0.7 collective-permute-done.9.right
  93.3 0.7 collective-permute-start.11
  94.0 2.4 %shard_map.85 = (bf16[4,640,1280]{2,1,0:T(8,128)(2,1)}, bf16[640,1280]{1,0:T(8,128)(2,1)}) custom-call(s32[1]{0:T(128)} %bitcast.1.core, bf16[2,256,640]{2,1,0:T(8,128)(2,1)S(1)} %get-tuple-element.85.active, bf16[256,1280]{1,0:T(8,128)(2,1)S(1)} %get-tuple-element.86.grads), custom_call_target="tpu_custom_call" | custom-call | tf_op jit(solution)/shard_map/pallas_call | solution.py:72
  96.4 4.4 %collective-permute-done.10.right = bf16[2,64,1280]{2,1,0:T(8,128)(2,1)S(1)} collective-permute-done((bf16[2,64,1280]{2,1,0:T(8,128)(2,1)S(1)}, bf16[2,64,1280]{2,1,0:T(8,128)(2,1)S(1)}, u32[]{:S(2)}, u32[]{:S(2)}) %collective-permute-start.10) | collective-permute-done | bytes 327712 | tf_op jit(solution)/shard_map/ppermute | solution.py:400
  101.0 0.7 collective-permute-start.13
  101.7 6.2 %collective-permute-done.7.refs_1_ = bf16[2,64,1280]{2,1,0:T(8,128)(2,1)S(1)} collective-permute-done((bf16[2,64,1280]{2,1,0:T(8,128)(2,1)S(1)}, bf16[2,64,1280]{2,1,0:T(8,128)(2,1)S(1)}, u32[]{:S(2)}, u32[]{:S(2)}) %collective-permute-start.7) | collective-permute-done | bytes 327712 | tf_op jit(solution)/shard_map/ppermute | solution.py:399
  107.9 2.4 %shard_map.87 = (bf16[4,640,1280]{2,1,0:T(8,128)(2,1)}, bf16[640,1280]{1,0:T(8,128)(2,1)}) custom-call(s32[1]{0:T(128)} %bitcast.1.core, bf16[2,256,640]{2,1,0:T(8,128)(2,1)S(1)} %get-tuple-element.92.active, bf16[256,1280]{1,0:T(8,128)(2,1)S(1)} %get-tuple-element.93.grads, ...), custom_call_target="tpu_custom_call", output_to_operand_aliasing={{0}: (3, {})} | custom-call | tf_op jit(solution)/shard_map/pallas_call | solution.py:72
  110.3 4.4 %collective-permute-start.14 = (bf16[640,1280]{1,0:T(8,128)(2,1)}, bf16[640,1280]{1,0:T(8,128)(2,1)S(1)}, u32[]{:S(2)}, u32[]{:S(2)}) collective-permute-start(bf16[640,1280]{1,0:T(8,128)(2,1)} %get-tuple-element.101), channel_id=1, source_target_pairs={{0,32},{32,0},{1,33},{33,1},{2,34},{34,2},{3,35},{35,3},{4,36},{36... | collective-permute-start | bytes 4915208 | tf_op jit(solution)/shard_map/ppermute | solution.py:414
  114.7 0.1 collective-permute-start.15
  114.8 0.1 collective-permute-done.13.refs_4_
  114.9 0.6 shard_map.88
  115.5 26.3 %all_to_all.21.wire = bf16[32,16,1280]{2,1,0:T(8,128)(2,1)S(1)} all-to-all(bf16[32,16,1280]{2,1,0:T(8,128)(2,1)S(1)} %shard_map.88), channel_id=1, replica_groups=mesh['zl'=2,'core'=2,'xy'=16,'zh'=2] {'core','xy'}, dimensions={0} | all-to-all | bytes 2621440 | tf_op jit(solution)/shard_map/all_to_all | solution.py:20
  141.8 3.2 %shard_map.89 = (bf16[2,256,128]{2,1,0:T(8,128)(2,1)S(1)}, bf16[256,1280]{1,0:T(8,128)(2,1)}, bf16[128,2,640]{2,1,0:T(2,128)(2,1)}) custom-call(s32[1]{0:T(128)} %bitcast.high, bf16[32,16,1280]{2,1,0:T(8,128)(2,1)S(1)} %all_to_all.21.wire, bf16[2,256,1280]{2,1,0:T(8,128)(2,1)S(1)} %copy-done, bf16[2,256,1280]{2,1,0:T(8,128)(2,1)S(1)} %copy-done.1, ...), custom_call_target="tpu_custom_call" | custom-call | tf_op jit(solution)/shard_map/pallas_call | solution.py:72
  145.0 4.3 %all-to-all-start.3 = ((bf16[128,2,640]{2,1,0:T(2,128)(2,1)}), bf16[128,2,640]{2,1,0:T(2,128)(2,1)S(1)}, u32[]{:S(2)}, u32[]{:S(2)}) async-start(bf16[128,2,640]{2,1,0:T(2,128)(2,1)} %get-tuple-element.108), calls=%async_computation.3 | async-start | bytes 655360 | tf_op jit(solution)/shard_map/all_to_all | solution.py:439
  149.3 1.2 copy-done.9
  150.5 3.3 %shard_map.90 = bf16[4,640,1280]{2,1,0:T(8,128)(2,1)} custom-call(s32[1]{0:T(128)} %bitcast.1.core, bf16[640,1280]{1,0:T(8,128)(2,1)} %copy-done.9, bf16[640,1280]{1,0:T(8,128)(2,1)} %collective-permute-done.15.came_1, bf16[4,640,1280]{2,1,0:T(8,128)(2,1)} %get-tuple-element.104._), custom_call_target="tpu_custom_call", output_to_operand_aliasing={{}: (3, {})} | custom-call | tf_op jit(solution)/shard_map/pallas_call | solution.py:72
  153.8 1.9 %shard_map.91 = bf16[2,256,1280]{2,1,0:T(8,128)(2,1)} custom-call(f32[2,256,128]{2,1,0:T(8,128)S(1)} %copy-done.2, bf16[2,256,128]{2,1,0:T(8,128)(2,1)S(1)} %get-tuple-element.100.logit_grad, bf16[256,1280]{1,0:T(8,128)(2,1)S(1)} %copy-done.3, bf16[128,1280]{1,0:T(8,128)(2,1)S(1)} %copy-done.4), custom_call_target="tpu_custom_call" | custom-call | tf_op jit(solution)/shard_map/pallas_call | solution.py:72
  155.7 5.6 %all-to-all-done.3 = bf16[128,2,640]{2,1,0:T(2,128)(2,1)S(1)} async-done(((bf16[128,2,640]{2,1,0:T(2,128)(2,1)}), bf16[128,2,640]{2,1,0:T(2,128)(2,1)S(1)}, u32[]{:S(2)}, u32[]{:S(2)}) %all-to-all-start.3) | async-done | bytes 327712 | tf_op jit(solution)/shard_map/all_to_all | solution.py:439
  161.2 0.3 convert_reduce_fusion
  161.6 0.6 copy.10
  (28 shorter events, 0.3 us)
Async XLA Ops:
  0.6 51.6 %collective-permute-start.1 = (bf16[4,1280,640]{2,1,0:T(8,128)(2,1)}, bf16[4,1280,640]{2,1,0:T(8,128)(2,1)}, u32[]{:S(2)}, u32[]{:S(2)}) collective-permute-start(bf16[4,1280,640]{2,1,0:T(8,128)(2,1)} %near_in), channel_id=1, source_target_pairs={{0,32},{32,0},{1,33},{33,1},{2,34},{34,2},{3,35},{35,3},{4,36},{36... | collective-permute-start | bytes 19660808 | tf_op jit(solution)/shard_map/ppermute | solution.py:359
  2.1 50.1 %collective-permute-start = (bf16[4,640,1280]{2,1,0:T(8,128)(2,1)}, bf16[4,640,1280]{2,1,0:T(8,128)(2,1)}, u32[]{:S(2)}, u32[]{:S(2)}) collective-permute-start(bf16[4,640,1280]{2,1,0:T(8,128)(2,1)} %near_out), channel_id=1, source_target_pairs={{0,32},{32,0},{1,33},{33,1},{2,34},{34,2},{3,35},{35,3},{4,36},{36... | collective-permute-start | bytes 19660808 | tf_op jit(solution)/shard_map/ppermute | solution.py:360
  2.2 0.7 copy-start.6
  3.7 22.3 %all-to-all-start = ((bf16[128,2,640]{2,1,0:T(2,128)(2,1)}), bf16[128,2,640]{2,1,0:T(2,128)(2,1)S(1)}, u32[]{:S(2)}, u32[]{:S(2)}) async-start(bf16[128,2,640]{2,1,0:T(2,128)(2,1)} %shard_map.78), calls=%async_computation | async-start | bytes 655360 | tf_op jit(solution)/shard_map/all_to_all | solution.py:94
  53.5 10.4 %collective-permute-start.3 = (bf16[2,64,1280]{2,1,0:T(8,128)(2,1)S(1)}, bf16[2,64,1280]{2,1,0:T(8,128)(2,1)S(1)}, u32[]{:S(2)}, u32[]{:S(2)}) collective-permute-start(bf16[2,64,1280]{2,1,0:T(8,128)(2,1)S(1)} %get-tuple-element.68), channel_id=1, source_target_pairs={{0,65},{1,64},{64,1},{65,0},{2,67},{3,66},{66,3},{67,2},{4,69},{5,... | collective-permute-start | bytes 983048 | tf_op jit(solution)/shard_map/ppermute | solution.py:386
  56.7 8.3 %collective-permute-start.2 = (bf16[2,64,1280]{2,1,0:T(8,128)(2,1)}, bf16[2,64,1280]{2,1,0:T(8,128)(2,1)S(1)}, u32[]{:S(2)}, u32[]{:S(2)}) collective-permute-start(bf16[2,64,1280]{2,1,0:T(8,128)(2,1)} %get-tuple-element.62.refs_0_), channel_id=1, source_target_pairs={{0,64},{64,0},{1,65},{65,1},{2,66},{66,2},{3,67},{67,3},{4,68},{68... | collective-permute-start | bytes 983048 | tf_op jit(solution)/shard_map/ppermute | solution.py:385
  56.7 14.3 %collective-permute-start.5 = (bf16[2,64,1280]{2,1,0:T(8,128)(2,1)S(1)}, bf16[2,64,1280]{2,1,0:T(8,128)(2,1)S(1)}, u32[]{:S(2)}, u32[]{:S(2)}) collective-permute-start(bf16[2,64,1280]{2,1,0:T(8,128)(2,1)S(1)} %get-tuple-element.72), channel_id=1, source_target_pairs={{0,65},{1,64},{64,1},{65,0},{2,67},{3,66},{66,3},{67,2},{4,69},{5,... | collective-permute-start | bytes 983048 | tf_op jit(solution)/shard_map/ppermute | solution.py:387
  56.8 15.2 %collective-permute-start.4 = (bf16[2,64,1280]{2,1,0:T(8,128)(2,1)}, bf16[2,64,1280]{2,1,0:T(8,128)(2,1)S(1)}, u32[]{:S(2)}, u32[]{:S(2)}) collective-permute-start(bf16[2,64,1280]{2,1,0:T(8,128)(2,1)} %get-tuple-element.71.refs_0_), channel_id=1, source_target_pairs={{0,64},{64,0},{1,65},{65,1},{2,66},{66,2},{3,67},{67,3},{4,68},{68... | collective-permute-start | bytes 983048 | tf_op jit(solution)/shard_map/ppermute | solution.py:385
  58.2 20.9 %copy-start.8 = (bf16[2,64,1280]{2,1,0:T(8,128)(2,1)S(1)}, bf16[2,64,1280]{2,1,0:T(8,128)(2,1)}, u32[]{:S(2)}) copy-start(bf16[2,64,1280]{2,1,0:T(8,128)(2,1)} %get-tuple-element.62.refs_0_) | copy-start | bytes 983044
  65.0 14.0 %collective-permute-start.6 = (bf16[2,64,1280]{2,1,0:T(8,128)(2,1)S(1)}, bf16[2,64,1280]{2,1,0:T(8,128)(2,1)S(1)}, u32[]{:S(2)}, u32[]{:S(2)}) collective-permute-start(bf16[2,64,1280]{2,1,0:T(8,128)(2,1)S(1)} %collective-permute-done.3.refs_2_), channel_id=1, source_target_pairs={{0,64},{64,0},{1,65},{65,1},{2,66},{66,2},{3,67},{67,3},{4,68},{68... | collective-permute-start | bytes 983048 | tf_op jit(solution)/shard_map/ppermute | solution.py:391
  72.0 14.0 %collective-permute-start.8 = (bf16[2,64,1280]{2,1,0:T(8,128)(2,1)S(1)}, bf16[2,64,1280]{2,1,0:T(8,128)(2,1)S(1)}, u32[]{:S(2)}, u32[]{:S(2)}) collective-permute-start(bf16[2,64,1280]{2,1,0:T(8,128)(2,1)S(1)} %collective-permute-done.5.refs_2_), channel_id=1, source_target_pairs={{0,64},{64,0},{1,65},{65,1},{2,66},{66,2},{3,67},{67,3},{4,68},{68... | collective-permute-start | bytes 983048 | tf_op jit(solution)/shard_map/ppermute | solution.py:391
  79.0 7.3 %copy-start.7 = (bf16[2,64,1280]{2,1,0:T(8,128)(2,1)S(1)}, bf16[2,64,1280]{2,1,0:T(8,128)(2,1)}, u32[]{:S(2)}) copy-start(bf16[2,64,1280]{2,1,0:T(8,128)(2,1)} %get-tuple-element.71.refs_0_) | copy-start | bytes 983044
  86.1 7.2 %collective-permute-start.9 = (bf16[2,64,1280]{2,1,0:T(8,128)(2,1)S(1)}, bf16[2,64,1280]{2,1,0:T(8,128)(2,1)S(1)}, u32[]{:S(2)}, u32[]{:S(2)}) collective-permute-start(bf16[2,64,1280]{2,1,0:T(8,128)(2,1)S(1)} %get-tuple-element.82), channel_id=1, source_target_pairs={{0,64},{64,0},{1,65},{65,1},{2,66},{66,2},{3,67},{67,3},{4,68},{68... | collective-permute-start | bytes 983048 | tf_op jit(solution)/shard_map/ppermute | solution.py:398
  91.0 9.9 %collective-permute-start.10 = (bf16[2,64,1280]{2,1,0:T(8,128)(2,1)S(1)}, bf16[2,64,1280]{2,1,0:T(8,128)(2,1)S(1)}, u32[]{:S(2)}, u32[]{:S(2)}) collective-permute-start(bf16[2,64,1280]{2,1,0:T(8,128)(2,1)S(1)} %get-tuple-element.88), channel_id=1, source_target_pairs={{0,64},{64,0},{1,65},{65,1},{2,66},{66,2},{3,67},{67,3},{4,68},{68... | collective-permute-start | bytes 983048 | tf_op jit(solution)/shard_map/ppermute | solution.py:400
  92.2 15.7 %collective-permute-start.7 = (bf16[2,64,1280]{2,1,0:T(8,128)(2,1)S(1)}, bf16[2,64,1280]{2,1,0:T(8,128)(2,1)S(1)}, u32[]{:S(2)}, u32[]{:S(2)}) collective-permute-start(bf16[2,64,1280]{2,1,0:T(8,128)(2,1)S(1)} %get-tuple-element.77), channel_id=1, source_target_pairs={{0,64},{64,0},{1,65},{65,1},{2,66},{66,2},{3,67},{67,3},{4,68},{68... | collective-permute-start | bytes 983048 | tf_op jit(solution)/shard_map/ppermute | solution.py:399
  93.3 21.5 %collective-permute-start.11 = (bf16[2,64,1280]{2,1,0:T(8,128)(2,1)S(1)}, bf16[2,64,1280]{2,1,0:T(8,128)(2,1)S(1)}, u32[]{:S(2)}, u32[]{:S(2)}) collective-permute-start(bf16[2,64,1280]{2,1,0:T(8,128)(2,1)S(1)} %shard_map.84), channel_id=1, source_target_pairs={{0,65},{1,64},{64,1},{65,0},{2,67},{3,66},{66,3},{67,2},{4,69},{5,... | collective-permute-start | bytes 983048 | tf_op jit(solution)/shard_map/ppermute | solution.py:404
  100.9 13.9 %collective-permute-start.12 = (bf16[2,64,1280]{2,1,0:T(8,128)(2,1)S(1)}, bf16[2,64,1280]{2,1,0:T(8,128)(2,1)S(1)}, u32[]{:S(2)}, u32[]{:S(2)}) collective-permute-start(bf16[2,64,1280]{2,1,0:T(8,128)(2,1)S(1)} %shard_map.86), channel_id=1, source_target_pairs={{0,65},{1,64},{64,1},{65,0},{2,67},{3,66},{66,3},{67,2},{4,69},{5,... | collective-permute-start | bytes 983048 | tf_op jit(solution)/shard_map/ppermute | solution.py:409
  101.0 13.9 %collective-permute-start.13 = (bf16[2,64,1280]{2,1,0:T(8,128)(2,1)S(1)}, bf16[2,64,1280]{2,1,0:T(8,128)(2,1)S(1)}, u32[]{:S(2)}, u32[]{:S(2)}) collective-permute-start(bf16[2,64,1280]{2,1,0:T(8,128)(2,1)S(1)} %get-tuple-element.97), channel_id=1, source_target_pairs={{0,64},{64,0},{1,65},{65,1},{2,66},{66,2},{3,67},{67,3},{4,68},{68... | collective-permute-start | bytes 983048 | tf_op jit(solution)/shard_map/ppermute | solution.py:401
  110.3 39.0 %collective-permute-start.14 = (bf16[640,1280]{1,0:T(8,128)(2,1)}, bf16[640,1280]{1,0:T(8,128)(2,1)S(1)}, u32[]{:S(2)}, u32[]{:S(2)}) collective-permute-start(bf16[640,1280]{1,0:T(8,128)(2,1)} %get-tuple-element.101), channel_id=1, source_target_pairs={{0,32},{32,0},{1,33},{33,1},{2,34},{34,2},{3,35},{35,3},{4,36},{36... | collective-permute-start | bytes 4915208 | tf_op jit(solution)/shard_map/ppermute | solution.py:414
  114.7 34.6 %collective-permute-start.15 = (bf16[640,1280]{1,0:T(8,128)(2,1)}, bf16[640,1280]{1,0:T(8,128)(2,1)}, u32[]{:S(2)}, u32[]{:S(2)}) collective-permute-start(bf16[640,1280]{1,0:T(8,128)(2,1)} %get-tuple-element.95), channel_id=1, source_target_pairs={{0,32},{32,0},{1,33},{33,1},{2,34},{34,2},{3,35},{35,3},{4,36},{36... | collective-permute-start | bytes 4915208 | tf_op jit(solution)/shard_map/ppermute | solution.py:415
  114.9 26.9 %copy-start.2 = (f32[2,256,128]{2,1,0:T(8,128)S(1)}, f32[2,256,128]{2,1,0:T(8,128)}, u32[]{:S(2)}) copy-start(f32[2,256,128]{2,1,0:T(8,128)} %get-tuple-element.58.dispatch) | copy-start | bytes 786436
  114.9 26.9 %copy-start.5 = (f32[2,256,128]{2,1,0:T(8,128)S(1)}, f32[2,256,128]{2,1,0:T(8,128)}, u32[]{:S(2)}) copy-start(f32[2,256,128]{2,1,0:T(8,128)} %get-tuple-element.99.combine) | copy-start | bytes 786436
  115.5 26.3 %copy-start = (bf16[2,256,1280]{2,1,0:T(8,128)(2,1)S(1)}, bf16[2,256,1280]{2,1,0:T(8,128)(2,1)}, u32[]{:S(2)}) copy-start(bf16[2,256,1280]{2,1,0:T(8,128)(2,1)} %tokens.1) | copy-start | bytes 3932164
  115.5 26.3 %copy-start.1 = (bf16[2,256,1280]{2,1,0:T(8,128)(2,1)S(1)}, bf16[2,256,1280]{2,1,0:T(8,128)(2,1)}, u32[]{:S(2)}) copy-start(bf16[2,256,1280]{2,1,0:T(8,128)(2,1)} %d_out.1) | copy-start | bytes 3932164
  145.0 16.2 %all-to-all-start.3 = ((bf16[128,2,640]{2,1,0:T(2,128)(2,1)}), bf16[128,2,640]{2,1,0:T(2,128)(2,1)S(1)}, u32[]{:S(2)}, u32[]{:S(2)}) async-start(bf16[128,2,640]{2,1,0:T(2,128)(2,1)} %get-tuple-element.108), calls=%async_computation.3 | async-start | bytes 655360 | tf_op jit(solution)/shard_map/all_to_all | solution.py:439
  149.3 1.2 copy-start.9
  150.5 3.3 %copy-start.3 = (bf16[256,1280]{1,0:T(8,128)(2,1)S(1)}, bf16[256,1280]{1,0:T(8,128)(2,1)}, u32[]{:S(2)}) copy-start(bf16[256,1280]{1,0:T(8,128)(2,1)} %get-tuple-element.106.slot_back) | copy-start | bytes 1966084
  150.5 3.3 %copy-start.4 = (bf16[128,1280]{1,0:T(8,128)(2,1)S(1)}, bf16[128,1280]{1,0:T(8,128)(2,1)}, u32[]{:S(2)}) copy-start(bf16[128,1280]{1,0:T(8,128)(2,1)} %get-tuple-element.107.router) | copy-start | bytes 983044
